TPU v7x, 512 devices: a whole 4x8x8 slice. The times are simulated.
512 devices in a mesh: rep: 16 (over z, y_lo), tp: 8 (over x, core), fsdp: 4 (over y_hi).
Axes of the slice: x: 4, y: 8 (y_hi: 4, y_lo: 2; y = y_hi * 2 + y_lo), z: 8, core: 2. Of those that a mesh axis runs over, the one named last changes fastest.
Arguments:
- hidden_in: bfloat16 [32, 2, 5120], P('rep'), may hold values from -6 to 6
- frozen_query_matrix: bfloat16 [5120, 8192], P(None, ('tp', 'fsdp')), may hold values from -0.078125 to 0.078125
- factor_down: bfloat16 [5120, 64], P('rep'), may hold values from -0.078125 to 0.078125
- factor_up: bfloat16 [64, 8192], P('rep', ('tp', 'fsdp')), may hold values from -0.75 to 0.75
- query_gain: float32 [128], replicated, may hold values from 0.1 to 1.9
- key_cache: bfloat16 [32, 4096, 1024], P('rep', 'fsdp', 'tp'), may hold values from -1600 to 1600
- value_cache: bfloat16 [32, 4096, 1024], P('rep', 'fsdp', 'tp'), may hold values from -6 to 6
- new_keys: bfloat16 [32, 2, 1024], P('rep', None, 'tp'), may hold values from -15 to 15
- new_values: bfloat16 [32, 2, 1024], P('rep', None, 'tp'), may hold values from -6 to 6
- cache_lengths: int32 [32], P('rep'), may hold values from 1024 to 4096, as said below
Outputs:
- attended: bfloat16 [32, 2, 8192], P('rep', None, ('tp', 'fsdp'))
Inputs may be any that keep to these rules, and one draw needn't show every extreme that they name: `cache_lengths`: some row has exactly 4096 valid slots.
All inputs are finite; a program needn't handle non-finite values.
Results may differ from a plain program's by a relative error of at most 0.029.
Values may be sent and summed in bfloat16 or wider, within the bound.
No kernel may reach another device: no remote copies, remote signals or barrier semaphores. Data moves between devices by JAX's collectives and lax.ppermute only.
A program may use at most 64 MiB of HBM per device.

v0:
```python
import jax
import jax.numpy as jnp
from jax import lax
from jax.sharding import PartitionSpec as P

adapter_scale = 2.0
norm_epsilon = 1e-06
masked_score = -1e30


def merged(value, axis, join):
    pieces = jax.tree.map(lambda part: lax.all_gather(part, axis), value)
    head = jax.tree.map(lambda part: part[0], pieces)
    tail = jax.tree.map(lambda part: part[1:], pieces)
    total, _ = lax.scan(lambda total, piece: (join(total, piece), None), head, tail)
    return total


def normalize_heads(query_rows, query_gain):
    spread = jnp.mean(query_rows * query_rows, axis=-1, keepdims=True)
    return query_rows * lax.rsqrt(spread + norm_epsilon) * query_gain


def combine_parts(first, second):
    top_first, total_first, acc_first = first
    top_second, total_second, acc_second = second
    highest = jnp.maximum(top_first, top_second)
    scale_first = jnp.exp(top_first - highest)
    scale_second = jnp.exp(top_second - highest)
    return (
        highest,
        total_first * scale_first + total_second * scale_second,
        acc_first * scale_first[..., None] + acc_second * scale_second[..., None],
    )


def apply_factors(tokens_flat, frozen_query_matrix, full_down, full_up):
    adapter_product = jnp.dot(full_down, full_up, preferred_element_type=jnp.float32)
    combined_matrix = frozen_query_matrix.astype(jnp.float32) + adapter_scale * adapter_product
    return jnp.dot(
        tokens_flat.astype(jnp.float32), combined_matrix, precision=lax.Precision.HIGHEST
    )


def on_device(
    hidden_in,
    frozen_query_matrix,
    factor_down,
    factor_up,
    query_gain,
    key_cache,
    value_cache,
    new_keys,
    new_values,
    cache_lengths,
):
    batch_row_count, decoded, width = hidden_in.shape
    head_dim = query_gain.shape[0]
    tokens_flat = hidden_in.reshape(batch_row_count * decoded, width)
    full_down, full_up = (
        lax.all_gather(factor_down, "rep", axis=0, tiled=True),
        lax.all_gather(factor_up, "rep", axis=0, tiled=True),
    )
    query_rows = apply_factors(tokens_flat, frozen_query_matrix, full_down, full_up)
    query_rows = query_rows.reshape(batch_row_count, decoded, -1, head_dim)
    normed = normalize_heads(query_rows, query_gain).astype(jnp.bfloat16)
    own_heads = normed.shape[2]
    gathered = lax.all_gather(
        normed.reshape(batch_row_count, decoded, own_heads * head_dim), "fsdp", axis=2, tiled=True
    )
    kv_local = key_cache.shape[2] // head_dim
    tp_heads = gathered.shape[2] // head_dim
    group = tp_heads // kv_local
    grouped = gathered.reshape(batch_row_count, decoded, kv_local, group, head_dim)
    span = key_cache.shape[1]
    keys_local = key_cache.reshape(batch_row_count, span, kv_local, head_dim)
    values_local = value_cache.reshape(batch_row_count, span, kv_local, head_dim)
    scores = jnp.einsum(
        "rnkgd,rckd->rnkgc", grouped, keys_local, preferred_element_type=jnp.float32
    ) * head_dim ** (-0.5)
    fsdp_index = lax.axis_index("fsdp")
    offset = fsdp_index * span
    valid = ((offset + jnp.arange(span, dtype=jnp.int32))[None, :] < cache_lengths[:, None])[
        :, None, None, None, :
    ]
    scores = jnp.where(valid, scores, masked_score)
    highest = jnp.max(scores, axis=-1)
    weights = jnp.where(valid, jnp.exp(scores - highest[..., None]), 0.0)
    total = jnp.sum(weights, axis=-1)
    weighted = jnp.einsum(
        "rnkgc,rckd->rnkgd",
        weights.astype(jnp.bfloat16),
        values_local,
        preferred_element_type=jnp.float32,
    )
    highest, total, weighted = merged((highest, total, weighted), "fsdp", combine_parts)
    start = fsdp_index * own_heads
    highest = lax.dynamic_slice_in_dim(
        highest.reshape(batch_row_count, decoded, tp_heads), start, own_heads, 2
    )
    total = lax.dynamic_slice_in_dim(
        total.reshape(batch_row_count, decoded, tp_heads), start, own_heads, 2
    )
    weighted = lax.dynamic_slice_in_dim(
        weighted.reshape(batch_row_count, decoded, tp_heads, head_dim), start, own_heads, 2
    )
    kv_owner = (fsdp_index * own_heads + jnp.arange(own_heads, dtype=jnp.int32)) // group
    fresh_keys = jnp.take(
        new_keys.reshape(batch_row_count, decoded, kv_local, head_dim), kv_owner, axis=2
    )
    fresh_values = jnp.take(
        new_values.reshape(batch_row_count, decoded, kv_local, head_dim), kv_owner, axis=2
    )
    fresh_scores = jnp.einsum(
        "rnhd,rmhd->rnhm", normed, fresh_keys, preferred_element_type=jnp.float32
    ) * head_dim ** (-0.5)
    steps_index = jnp.arange(decoded, dtype=jnp.int32)
    causal = (steps_index[None, :] <= steps_index[:, None])[None, :, None, :]
    fresh_scores = jnp.where(causal, fresh_scores, masked_score)
    new_top = jnp.maximum(highest, jnp.max(fresh_scores, axis=-1))
    carry_scale = jnp.exp(highest - new_top)
    fresh_weights = jnp.where(causal, jnp.exp(fresh_scores - new_top[..., None]), 0.0)
    total = total * carry_scale + jnp.sum(fresh_weights, axis=-1)
    weighted = weighted * carry_scale[..., None] + jnp.einsum(
        "rnhm,rmhd->rnhd",
        fresh_weights.astype(jnp.bfloat16),
        fresh_values,
        preferred_element_type=jnp.float32,
    )
    return (
        (weighted / total[..., None])
        .reshape(batch_row_count, decoded, own_heads * head_dim)
        .astype(jnp.bfloat16)
    )


def solution(mesh):
    placed = (
        P("rep", None, None),
        P(None, ("tp", "fsdp")),
        P("rep", None),
        P("rep", ("tp", "fsdp")),
        P(),
        P("rep", "fsdp", "tp"),
        P("rep", "fsdp", "tp"),
        P("rep", None, "tp"),
        P("rep", None, "tp"),
        P("rep"),
    )
    return jax.shard_map(
        on_device,
        mesh=mesh,
        in_specs=placed,
        out_specs=P("rep", None, ("tp", "fsdp")),
        check_vma=False,
    )
```

profile of v0, /device:TPU:6, one launch (start us, length us, event | category | flops | bytes accessed | tf_op | source)
XLA Modules:
  0.0 142.2 jit_solution(9758089188162637597)
XLA Ops:
  0.0 0.0 copy-start
  0.0 47.3 %all-gather.3 = bf16[16,320,64]{1,2,0:T(8,128)(2,1)S(1)} all-gather(bf16[1,320,64]{1,2,0:T(8,128)(2,1)} %bitcast.117), channel_id=1, replica_groups=mesh['rep'=16,'tp'=8,'fsdp'=4] {'rep'}, dimensions={0}, use_global_device_ids=true | all-gather | bytes 696320 | tf_op jit(solution)/shard_map/all_gather | solution.py:61
  47.3 0.5 copy.32
  47.7 0.0 copy-start.2
  47.7 0.6 reshape.179
  48.4 30.1 %all-gather.4 = bf16[16,4,256]{2,1,0:T(4,128)(2,1)S(1)} all-gather(bf16[1,4,256]{2,1,0:T(4,128)(2,1)} %bitcast.119), channel_id=1, replica_groups=mesh['rep'=16,'tp'=8,'fsdp'=4] {'rep'}, dimensions={0}, use_global_device_ids=true | all-gather | bytes 34816 | tf_op jit(solution)/shard_map/all_gather | solution.py:62
  78.4 0.0 copy-start.4
  78.5 0.0 copy-start.3
  78.5 0.0 copy-start.1
  78.5 5.0 %fusion.5 = f32[5120,256]{1,0:T(8,128)} fusion(bf16[5120,64]{0,1:T(8,128)(2,1)S(1)} %reshape.179, bf16[64,256]{1,0:T(8,128)(2,1)S(1)} %reshape.181, bf16[5120,256]{1,0:T(8,128)(2,1)} %param.15), kind=kOutput, calls=%fused_computation.11 | convolution fusion | flops 171704320 | bytes 8552448 | tf_op jit(solution)/shard_map/dot_general | solution.py:38
  83.5 0.0 copy-done.2
  83.5 0.0 copy-start.5
  83.5 0.0 copy-start.6
  83.5 4.2 %convolution_bitcast_fusion.2 = f32[4,256]{1,0:T(4,128)S(1)} fusion(f32[5120,256]{1,0:T(8,128)} %fusion.5, bf16[4,5120]{1,0:T(4,128)(2,1)S(1)} %reshape.157), kind=kOutput, calls=%fused_computation.23 | convolution fusion | flops 62914560 | bytes 5287936 | tf_op jit(solution)/shard_map/dot_general | solution.py:40
  87.8 0.1 multiply_reduce_fusion
  87.9 0.1 mul.118
  88.0 0.0 copy-done.4
  88.0 11.6 %all_gather.29 = bf16[2,2,1024]{2,1,0:T(2,128)(2,1)S(1)} all-gather(bf16[2,2,256]{2,1,0:T(2,128)(2,1)S(1)} %multiply_convert_fusion.1), channel_id=1, replica_groups=mesh['rep'=16,'tp'=8,'fsdp'=4] {'fsdp'}, dimensions={2}, use_global_device_ids=true | all-gather | bytes 10240 | tf_op jit(solution)/shard_map/all_gather | solution.py:68
  99.6 0.0 copy-done.3
  99.6 0.1 broadcast_compare_fusion
  99.7 0.0 copy-done
  99.7 0.3 fusion.34
  100.0 0.0 copy-done.1
  100.0 0.3 convolution_bitcast_fusion
  100.3 13.7 %all-gather.2 = f32[8,2,1,8,128]{4,3,2,1,0:T(8,128)S(1)} all-gather(f32[2,2,1,8,128]{4,3,2,1,0:T(8,128)S(1)} %convolution_bitcast_fusion), channel_id=4, replica_groups=mesh['rep'=16,'tp'=8,'fsdp'=4] {'fsdp'}, dimensions={0}, use_global_device_ids=true | all-gather | bytes 81920 | tf_op jit(solution)/shard_map/all_gather | solution.py:12
  114.0 0.2 fusion.18
  114.2 12.6 %all-gather.1 = f32[8,2,8]{2,1,0:T(2,128)S(1)} all-gather(f32[2,2,8]{2,1,0:T(2,128)S(1)} %fusion.18), channel_id=3, replica_groups=mesh['rep'=16,'tp'=8,'fsdp'=4] {'fsdp'}, dimensions={0}, use_global_device_ids=true | all-gather | bytes 640 | tf_op jit(solution)/shard_map/all_gather | solution.py:12
  126.8 13.6 %all-gather = f32[8,2,8]{2,1,0:T(2,128)S(1)} all-gather(f32[2,2,8]{2,1,0:T(2,128)S(1)} %get-tuple-element.89), channel_id=2, replica_groups=mesh['rep'=16,'tp'=8,'fsdp'=4] {'fsdp'}, dimensions={0}, use_global_device_ids=true | all-gather | bytes 640 | tf_op jit(solution)/shard_map/all_gather | solution.py:12
  140.4 0.4 while.14
  140.4 0.1 fusion.46
  140.6 0.1 fusion.46
  140.7 0.1 fusion.46
  140.8 0.1 dynamic-slice_bitcast_fusion
  140.8 0.1 copy.40
  140.9 0.1 multiply_convert_fusion
  141.1 0.0 copy-done.5
  141.1 0.2 fusion.35
  141.3 0.1 copy.42
  141.4 0.0 copy-done.6
  141.4 0.8 fusion.14
  (31 shorter events, 0.3 us)
Async XLA Ops:
  0.0 99.7 %copy-start = (bf16[2,1024,128]{2,1,0:T(8,128)(2,1)S(1)}, bf16[2,1024,128]{2,1,0:T(8,128)(2,1)}, u32[]{:S(2)}) copy-start(bf16[2,1024,128]{2,1,0:T(8,128)(2,1)} %param.19) | copy-start | bytes 1572868
  47.7 35.7 %copy-start.2 = (bf16[2,2,5120]{2,1,0:T(2,128)(2,1)S(1)}, bf16[2,2,5120]{2,1,0:T(2,128)(2,1)}, u32[]{:S(2)}) copy-start(bf16[2,2,5120]{2,1,0:T(2,128)(2,1)} %param.14) | copy-start | bytes 122884
  78.4 9.5 %copy-start.4 = (f32[128]{0:T(128)S(1)}, f32[128]{0:T(128)}, u32[]{:S(2)}) copy-start(f32[128]{0:T(128)} %param.18) | copy-start | bytes 1540
  78.5 21.2 %copy-start.3 = (s32[2]{0:T(128)S(1)}, s32[2]{0:T(128)}, u32[]{:S(2)}) copy-start(s32[2]{0:T(128)} %param.23) | copy-start | bytes 28
  78.5 21.6 %copy-start.1 = (bf16[2,1024,128]{2,1,0:T(8,128)(2,1)S(1)}, bf16[2,1024,128]{2,1,0:T(8,128)(2,1)}, u32[]{:S(2)}) copy-start(bf16[2,1024,128]{2,1,0:T(8,128)(2,1)} %param.20) | copy-start | bytes 1572868
  83.5 57.6 %copy-start.5 = (bf16[2,2,128]{2,1,0:T(2,128)(2,1)S(1)}, bf16[2,2,128]{2,1,0:T(2,128)(2,1)}, u32[]{:S(2)}) copy-start(bf16[2,2,128]{2,1,0:T(2,128)(2,1)} %param.21) | copy-start | bytes 3076
  83.5 58.0 %copy-start.6 = (bf16[2,2,128]{2,1,0:T(2,128)(2,1)S(1)}, bf16[2,2,128]{2,1,0:T(2,128)(2,1)}, u32[]{:S(2)}) copy-start(bf16[2,2,128]{2,1,0:T(2,128)(2,1)} %param.22) | copy-start | bytes 3076
where the time goes:
time: 143 us; the launch traced here: 142 us
  blocking collectives  129 us (90%)
  matrix products  10.8 us (8%)
  local copies, waits for them, and re-layouts  1.59 us (1%)
    all_gather x1, blocking collectives, on_device(): lax.all_gather(factor_down, 'rep', axis=0, tiled=True)  47.3 us
    all_gather x3, blocking collectives, merged(): pieces = jax.tree.map(lambda part: lax.all_gather(part, axis), value)  39.9 us
    all_gather x1, blocking collectives, on_device(): lax.all_gather(factor_up, 'rep', axis=0, tiled=True)  30.1 us
    all_gather x1, blocking collectives, on_device(): lax.all_gather(normed.reshape(batch_row_count, decoded, own_heads * head_...  11.6 us
    dot_general x1, matrix products, apply_factors(): jnp.dot(full_down, full_up, preferred_element_type=jnp.float32)  5 us
    dot_general x1, matrix products, apply_factors(): jnp.dot(tokens_flat.astype(jnp.float32), combined_matrix, precision=lax.P...  4.24 us

commit v1 on v0

v1 whole, which is shorter than its diff:
```python
import jax
import jax.numpy as jnp
from jax import lax
from jax.experimental import pallas as pl
from jax.experimental.pallas import tpu as pltpu
from jax.sharding import PartitionSpec as P

adapter_scale = 2.0
norm_epsilon = 1e-06
masked_score = -1e30

NT = (((1,), (1,)), ((), ()))
NN = (((1,), (0,)), ((), ()))
f32, bf16 = jnp.float32, jnp.bfloat16


def dot(a, b, dims):
    return lax.dot_general(a, b, dims, preferred_element_type=f32)


def iota(shape, axis):
    return lax.broadcasted_iota(jnp.int32, shape, axis)


def split3(x):
    hi = x.astype(bf16)
    rest = x - hi.astype(f32)
    mid = rest.astype(bf16)
    lo = (rest - mid.astype(f32)).astype(bf16)
    return hi, mid, lo


def pack_factors(down_ref, up_ref, out_ref, padded):
    f = lax.axis_index("fsdp")
    odd = lax.rem(lax.axis_index("rep"), 2)
    padded[0:320, :] = down_ref[...]
    padded[320:384, :] = jnp.zeros((64, 64), bf16)
    pick = (iota((16, 64), 1) == iota((16, 64), 0) + 16 * f).astype(f32).astype(bf16)
    columns = dot(pick, padded[...], NT)
    spread = (iota((16, 4), 0) % 4 == iota((16, 4), 1)).astype(f32).astype(bf16)
    rows = dot(spread, up_ref[...], NN)
    rows = jnp.where(iota((16, 256), 1) // 64 == iota((16, 256), 0) // 4, rows, 0.0)
    rows = rows[:, :128] + rows[:, 128:]
    rows = rows + pltpu.roll(rows, 64, 1)
    last = jnp.where(iota((16, 128), 1) >= 64, rows, columns[:, 256:])
    whole = jnp.concatenate([columns[:, :256], last], axis=1)
    whole = jnp.where(odd == 1, pltpu.roll(whole, 64, 1), whole).astype(bf16)
    for i in range(16):
        out_ref[i] = whole


def pack_queries(hidden_ref, frozen_ref, factors_ref, out_ref, tokens, spread):
    f = lax.axis_index("fsdp")
    tokens[0:2, :] = hidden_ref[0].astype(f32)
    tokens[2:4, :] = hidden_ref[1].astype(f32)
    lane = iota((16, 384), 1)
    half = iota((16, 128), 1)
    row = iota((16, 256), 0)
    group = iota((16, 256), 1) // 64
    low = jnp.zeros((4, 16), f32)
    for rep in range(16):
        start = 640 * (rep // 2) + 256 * (rep % 2)
        part = factors_ref[rep].astype(f32)
        if rep % 2 == 0:
            columns = jnp.where(lane < 320, part, 0.0)
            rows = jnp.where(half >= 64, part[:, 256:], 0.0)
        else:
            columns = jnp.where(lane >= 64, part, 0.0)
            rows = jnp.where(half < 64, part[:, :128], 0.0)
        low += dot(tokens[:, start : start + 384].astype(bf16), columns.astype(bf16), NT)
        rows = rows + pltpu.roll(rows, 64, 1)
        rows = jnp.concatenate([rows, rows], axis=1)
        spread[16 * rep : 16 * rep + 16, :] = jnp.where(group == row // 4, rows, 0.0).astype(bf16)
    line, place = iota((64, 256), 0), iota((64, 256), 1)
    pick = ((place // 16 == line // 4) & (place % 4 == line % 4)).astype(f32).astype(bf16)
    out_ref[0:64, :] = dot(pick, spread[...], NN).astype(bf16)
    own = frozen_ref[...]
    terms = [t.astype(f32) for t in split3(own)]
    lanes = jnp.zeros((4, 256), f32)
    for i, term in enumerate(split3(low)):
        put = (iota((16, 256), 1) == iota((16, 256), 0) + 16 * f + 64 * i).astype(f32).astype(bf16)
        lanes += dot(term, put, NN)
    out_ref[64:80, :] = jnp.concatenate(terms + [lanes], axis=0).astype(bf16)


def attend(parts_ref, gain_ref, keys_ref, values_ref, new_keys_ref, new_values_ref, lengths_ref, out_ref, queries, fresh_k, fresh_v):
    f = lax.axis_index("fsdp")
    gain = gain_ref[...]
    tails = [parts_ref[i, 64:80, :].astype(f32) for i in range(4)]
    low = tails[0][12:16] + tails[1][12:16] + tails[2][12:16] + tails[3][12:16]
    low = low.astype(bf16)
    for i in range(4):
        up = parts_ref[i, 0:64, :]
        up = jnp.concatenate([up] * 4, axis=0)
        tail = tails[i]
        query = tail[0:4] + tail[4:8] + tail[8:12] + adapter_scale * dot(low, up, NN)
        for j in range(2):
            head = query[:, 128 * j : 128 * j + 128]
            mean = jnp.mean(head * head, axis=-1, keepdims=True)
            at = 8 * i + 4 * j
            queries[at : at + 4, :] = head * lax.rsqrt(mean + norm_epsilon) * gain
    normed = queries[...].astype(bf16)
    span = keys_ref.shape[1]
    fresh_k[...] = jnp.zeros_like(fresh_k)
    fresh_v[...] = jnp.zeros_like(fresh_v)
    for i in range(2):
        fresh_k[2 * i : 2 * i + 2, :] = new_keys_ref[i].astype(f32)
        fresh_v[2 * i : 2 * i + 2, :] = new_values_ref[i].astype(f32)
    scale = 128 ** (-0.5)
    first = iota((32, span), 0) % 4 < 2
    scores = jnp.where(first, dot(normed, keys_ref[0], NT), dot(normed, keys_ref[1], NT)) * scale
    limit = jnp.where(first, lengths_ref[0], lengths_ref[1])
    valid = iota((32, span), 1) + f * span < limit
    scores = jnp.where(valid, scores, masked_score)
    line, place = iota((32, 128), 0), iota((32, 128), 1)
    fresh = dot(normed, fresh_k[...].astype(bf16), NT) * scale
    fresh_valid = (place // 2 == (line % 4) // 2) & (place % 2 <= line % 2) & (f == 0)
    fresh = jnp.where(fresh_valid, fresh, masked_score)
    top = jnp.maximum(jnp.max(scores, axis=-1, keepdims=True), jnp.max(fresh, axis=-1, keepdims=True))
    weights = jnp.where(valid, jnp.exp(scores - top), 0.0)
    fresh_weights = jnp.where(fresh_valid, jnp.exp(fresh - top), 0.0)
    total = jnp.sum(weights, axis=-1, keepdims=True) + jnp.sum(fresh_weights, axis=-1, keepdims=True)
    mixed = (
        dot(jnp.where(first, weights, 0.0).astype(bf16), values_ref[0], NN)
        + dot(jnp.where(first, 0.0, weights).astype(bf16), values_ref[1], NN)
        + dot(fresh_weights.astype(bf16), fresh_v[...].astype(bf16), NN)
    )
    stats = jnp.where(iota((32, 128), 1) < 64, top, total)
    for i in range(4):
        out_ref[i, 0:8, :] = mixed[8 * i : 8 * i + 8]
        out_ref[i, 8:16, :] = stats[8 * i : 8 * i + 8]


def merge(parts_ref, out_ref):
    tops = [parts_ref[i, 8:16, 0:1] for i in range(4)]
    top = jnp.maximum(jnp.maximum(tops[0], tops[1]), jnp.maximum(tops[2], tops[3]))
    total = jnp.zeros((8, 1), f32)
    mixed = jnp.zeros((8, 128), f32)
    for i in range(4):
        scale = jnp.exp(tops[i] - top)
        total += scale * parts_ref[i, 8:16, 64:65]
        mixed += scale * parts_ref[i, 0:8, :]
    result = mixed / total
    for i in range(2):
        for j in range(2):
            out_ref[i, :, 128 * j : 128 * j + 128] = result[4 * j + 2 * i : 4 * j + 2 * i + 2].astype(bf16)


def whole(n):
    return [pl.BlockSpec(memory_space=pltpu.VMEM)] * n


def on_device(
    hidden_in,
    frozen_query_matrix,
    factor_down,
    factor_up,
    query_gain,
    key_cache,
    value_cache,
    new_keys,
    new_values,
    cache_lengths,
):
    packed = pl.pallas_call(
        pack_factors,
        out_shape=jax.ShapeDtypeStruct((16, 16, 384), bf16),
        in_specs=whole(2),
        out_specs=whole(1)[0],
        scratch_shapes=[pltpu.VMEM((384, 64), bf16)],
        name="pack_factors",
    )(factor_down, factor_up)
    factors = lax.all_to_all(packed, "rep", 0, 0)
    frozen = jnp.dot(
        hidden_in.reshape(4, 5120), frozen_query_matrix, preferred_element_type=f32
    )
    sent = pl.pallas_call(
        pack_queries,
        out_shape=jax.ShapeDtypeStruct((80, 256), bf16),
        in_specs=whole(3),
        out_specs=whole(1)[0],
        scratch_shapes=[pltpu.VMEM((4, 5120), f32), pltpu.VMEM((256, 256), bf16)],
        name="pack_queries",
    )(hidden_in, frozen, factors)
    parts = lax.all_to_all(jnp.broadcast_to(sent, (4, 80, 256)), "fsdp", 0, 0)
    partial = pl.pallas_call(
        attend,
        out_shape=jax.ShapeDtypeStruct((4, 16, 128), f32),
        in_specs=whole(6) + [pl.BlockSpec(memory_space=pltpu.SMEM)],
        out_specs=whole(1)[0],
        scratch_shapes=[pltpu.VMEM((32, 128), f32)] + [pltpu.VMEM((128, 128), f32)] * 2,
        name="attend",
    )(parts, query_gain.reshape(1, 128), key_cache, value_cache, new_keys, new_values, cache_lengths)
    partial = lax.all_to_all(partial, "fsdp", 0, 0)
    return pl.pallas_call(
        merge,
        out_shape=jax.ShapeDtypeStruct((2, 2, 256), bf16),
        in_specs=whole(1),
        out_specs=whole(1)[0],
        name="merge",
    )(partial)


def solution(mesh):
    placed = (
        P("rep", None, None),
        P(None, ("tp", "fsdp")),
        P("rep", None),
        P("rep", ("tp", "fsdp")),
        P(),
        P("rep", "fsdp", "tp"),
        P("rep", "fsdp", "tp"),
        P("rep", None, "tp"),
        P("rep", None, "tp"),
        P("rep"),
    )
    return jax.shard_map(
        on_device,
        mesh=mesh,
        in_specs=placed,
        out_specs=P("rep", None, ("tp", "fsdp")),
        check_vma=False,
    )
```

time: 143 us -> 60.4 us (0.42)
  blocking collectives: 129 us -> 26.9 us
  starting transfers between devices: 0 us -> 11.4 us
  matrix products: 10.8 us -> 1.04 us
  waiting for transfers between devices: 0 us -> 8.39 us
  Pallas kernels: 0 us -> 8.07 us
  local copies, waits for them, and re-layouts: 1.59 us -> 3.94 us
    all_gather x6 -> x0, blocking collectives: 129 us -> none  [the longest x1 47.3 us: on_device(): lax.all_gather(factor_down, 'rep', axis=0, tiled=True)]
    all_to_all x0 -> x2, blocking collectives: none -> 26.9 us  [the longest x1 15.1 us: on_device(): parts = lax.all_to_all(jnp.broadcast_to(sent, (4, 80, 256)), 'fsdp', 0, 0)]
    all_to_all x0 -> x1, starting transfers between devices: none -> 11.4 us  [on_device(): factors = lax.all_to_all(packed, 'rep', 0, 0)]
    dot_general x6 -> x1, matrix products: 10.8 us -> 1.04 us  [on_device(): jnp.dot(hidden_in.reshape(4, 5120), frozen_query_matrix, preferred_elemen...]
    all_to_all x0 -> x1, waiting for transfers between devices: none -> 8.39 us  [on_device(): factors = lax.all_to_all(packed, 'rep', 0, 0)]
    pallas_call x0 -> x4, Pallas kernels: none -> 8.07 us  [the longest x1 2.7 us: on_device(): pl.pallas_call(attend, out_shape=jax.ShapeDtypeStruct((4, 16, 128), f32),...]
    unnamed x16 -> x5, local copies, waits for them, and re-layouts: 0.68 us -> 2.35 us
  transfers between devices with their start and end apart: 0 -> 1, of which waited for: 0 -> 1; matrix products, arithmetic and copies ran while one was open for 0% -> 3% of each run, Pallas kernels for 0% -> 0%
where the time goes in v1:
time: 60.4 us; the launch traced here: 59.8 us
  blocking collectives  26.9 us (45%)
  starting transfers between devices  11.4 us (19%)
  waiting for transfers between devices  8.39 us (14%)
  Pallas kernels  8.07 us (13%)
  local copies, waits for them, and re-layouts  3.94 us (7%)
  matrix products  1.04 us (2%)
    all_to_all x1, blocking collectives, on_device(): parts = lax.all_to_all(jnp.broadcast_to(sent, (4, 80, 256)), 'fsdp', 0, 0)  15.1 us
    all_to_all x1, blocking collectives, on_device(): partial = lax.all_to_all(partial, 'fsdp', 0, 0)  11.8 us
    all_to_all x1, starting transfers between devices, on_device(): factors = lax.all_to_all(packed, 'rep', 0, 0)  11.4 us
    all_to_all x1, waiting for transfers between devices, on_device(): factors = lax.all_to_all(packed, 'rep', 0, 0)  8.39 us
    pallas_call x1, Pallas kernels, on_device(): pl.pallas_call(attend, out_shape=jax.ShapeDtypeStruct((4, 16, 128), f32),...  2.7 us
    unnamed x5, local copies, waits for them, and re-layouts  2.35 us
    pallas_call x1, Pallas kernels, on_device(): pl.pallas_call(pack_queries, out_shape=jax.ShapeDtypeStruct((80, 256), bf...  1.99 us
    pallas_call x1, Pallas kernels, on_device(): pl.pallas_call(pack_factors, out_shape=jax.ShapeDtypeStruct((16, 16, 384)...  1.89 us
  transfers between devices with their start and end apart: 1, of which 1 were waited for; matrix products, arithmetic and copies ran while one was open for 3% of the time, Pallas kernels for 0%

profile of v1, /device:TPU:6, one launch (start us, length us, event | category | flops | bytes accessed | tf_op | source)
XLA Modules:
  0.0 59.8 jit_solution(8158350437833304457)
XLA Ops:
  0.0 0.0 copy-start
  0.0 1.7 %copy.11.down_ref = bf16[320,64]{1,0:T(8,128)(2,1)} copy(bf16[320,64]{0,1:T(8,128)(2,1)} %param.12) | data formatting | bytes 81920 | tf_op args[2]
  1.7 1.9 %pack_factors.1 = bf16[16,16,384]{2,1,0:T(8,128)(2,1)} custom-call(bf16[320,64]{1,0:T(8,128)(2,1)} %copy.11.down_ref, bf16[4,256]{1,0:T(4,128)(2,1)} %up_ref.1), custom_call_target="tpu_custom_call" | custom-call | tf_op jit(solution)/shard_map/pack_factors/pallas_call | solution.py:165
  3.6 11.4 %all-to-all-start = ((bf16[16,16,384]{2,1,0:T(8,128)(2,1)}), bf16[16,16,384]{2,1,0:T(8,128)(2,1)S(1)}, u32[]{:S(2)}, u32[]{:S(2)}) async-start(bf16[16,16,384]{2,1,0:T(8,128)(2,1)} %pack_factors.1), calls=%async_computation | async-start | bytes 393216 | tf_op jit(solution)/shard_map/all_to_all | solution.py:173
  15.0 0.8 %reshape.6 = bf16[4,5120]{1,0:T(4,128)(2,1)S(1)} reshape(bf16[2,2,5120]{2,1,0:T(2,128)(2,1)} %hidden_ref.1) | data formatting | bytes 81920 | tf_op jit(solution)/shard_map/reshape | solution.py:175
  15.8 0.0 copy-done
  15.8 1.0 %fusion.frozen_ref = f32[4,256]{1,0:T(4,128)} fusion(bf16[4,5120]{1,0:T(4,128)(2,1)S(1)} %reshape.6, bf16[5120,256]{1,0:T(8,128)(2,1)S(1)} %copy-done), kind=kOutput, calls=%fused_computation | convolution fusion | flops 10485760 | bytes 2666496 | tf_op jit(solution)/shard_map/dot_general | solution.py:174
  16.9 8.4 %all-to-all-done.factors_ref = bf16[16,16,384]{2,1,0:T(8,128)(2,1)S(1)} async-done(((bf16[16,16,384]{2,1,0:T(8,128)(2,1)}), bf16[16,16,384]{2,1,0:T(8,128)(2,1)S(1)}, u32[]{:S(2)}, u32[]{:S(2)}) %all-to-all-start) | async-done | bytes 196640 | tf_op jit(solution)/shard_map/all_to_all | solution.py:173
  25.3 0.0 copy-start.1
  25.3 0.7 %copy-done.1 = bf16[16,16,384]{2,1,0:T(8,128)(2,1)} copy-done((bf16[16,16,384]{2,1,0:T(8,128)(2,1)}, bf16[16,16,384]{2,1,0:T(8,128)(2,1)S(1)}, u32[]{:S(2)}) %copy-start.1) | copy-done | bytes 196632
  25.9 2.0 %pack_queries.1 = bf16[80,256]{1,0:T(8,128)(2,1)} custom-call(bf16[2,2,5120]{2,1,0:T(2,128)(2,1)} %hidden_ref.1, f32[4,256]{1,0:T(4,128)} %fusion.frozen_ref, bf16[16,16,384]{2,1,0:T(8,128)(2,1)} %copy-done.1), custom_call_target="tpu_custom_call" | custom-call | tf_op jit(solution)/shard_map/pack_queries/pallas_call | solution.py:177
  27.9 0.8 %broadcast_in_dim.3 = bf16[4,80,256]{2,1,0:T(8,128)(2,1)S(1)} broadcast(bf16[80,256]{1,0:T(8,128)(2,1)} %pack_queries.1), dimensions={1,2} | broadcast | bytes 204800 | tf_op jit(solution)/shard_map/broadcast_in_dim | solution.py:185
  28.7 15.1 %all_to_all.15.parts_ref = bf16[4,80,256]{2,1,0:T(8,128)(2,1)} all-to-all(bf16[4,80,256]{2,1,0:T(8,128)(2,1)S(1)} %broadcast_in_dim.3), channel_id=1, replica_groups=mesh['rep'=16,'tp'=8,'fsdp'=4] {'fsdp'}, dimensions={0} | all-to-all | bytes 327680 | tf_op jit(solution)/shard_map/all_to_all | solution.py:185
  43.8 2.7 %attend.1 = f32[4,16,128]{2,1,0:T(8,128)} custom-call(bf16[4,80,256]{2,1,0:T(8,128)(2,1)} %all_to_all.15.parts_ref, f32[1,128]{1,0:T(1,128)} %bitcast.3, bf16[2,1024,128]{2,1,0:T(8,128)(2,1)} %keys_ref.1, bf16[2,1024,128]{2,1,0:T(8,128)(2,1)} %values_ref.1, bf16[2,2,128]{2,1,0:T(2,128)(2,1)} %new_keys_ref.1, bf16[2,2,128]{2,1,0:T(2,128)(2,1)} %new_values_ref.1, ...), custom_call_target="tpu_custom_call" | custom-call | tf_op jit(solution)/shard_map/attend/pallas_call | solution.py:186
  46.5 11.8 %all_to_all.16.parts_ref = f32[4,16,128]{2,1,0:T(8,128)} all-to-all(f32[4,16,128]{2,1,0:T(8,128)} %attend.1), channel_id=1, replica_groups=mesh['rep'=16,'tp'=8,'fsdp'=4] {'fsdp'}, dimensions={0} | all-to-all | bytes 65536 | tf_op jit(solution)/shard_map/all_to_all | solution.py:194
  58.3 1.5 %merge.1 = bf16[2,2,256]{2,1,0:T(2,128)(2,1)} custom-call(f32[4,16,128]{2,1,0:T(8,128)} %all_to_all.16.parts_ref), custom_call_target="tpu_custom_call" | custom-call | tf_op jit(solution)/shard_map/merge/pallas_call | solution.py:195
Async XLA Ops:
  0.0 15.8 %copy-start = (bf16[5120,256]{1,0:T(8,128)(2,1)S(1)}, bf16[5120,256]{1,0:T(8,128)(2,1)}, u32[]{:S(2)}) copy-start(bf16[5120,256]{1,0:T(8,128)(2,1)} %param.11) | copy-start | bytes 7864324
  3.6 21.7 %all-to-all-start = ((bf16[16,16,384]{2,1,0:T(8,128)(2,1)}), bf16[16,16,384]{2,1,0:T(8,128)(2,1)S(1)}, u32[]{:S(2)}, u32[]{:S(2)}) async-start(bf16[16,16,384]{2,1,0:T(8,128)(2,1)} %pack_factors.1), calls=%async_computation | async-start | bytes 393216 | tf_op jit(solution)/shard_map/all_to_all | solution.py:173
  25.3 0.7 %copy-start.1 = (bf16[16,16,384]{2,1,0:T(8,128)(2,1)}, bf16[16,16,384]{2,1,0:T(8,128)(2,1)S(1)}, u32[]{:S(2)}) copy-start(bf16[16,16,384]{2,1,0:T(8,128)(2,1)S(1)} %all-to-all-done.factors_ref) | copy-start | bytes 589828

commit v2 on v1

--- a/solution.py
+++ b/solution.py
@@ -30,57 +30,55 @@
     return hi, mid, lo
 
 
-def pack_factors(down_ref, up_ref, out_ref, padded):
-    f = lax.axis_index("fsdp")
+def pack_factors(down_ref, up_ref, out_ref):
+    start = pl.multiple_of(16 * lax.axis_index("fsdp"), 16)
     odd = lax.rem(lax.axis_index("rep"), 2)
-    padded[0:320, :] = down_ref[...]
-    padded[320:384, :] = jnp.zeros((64, 64), bf16)
-    pick = (iota((16, 64), 1) == iota((16, 64), 0) + 16 * f).astype(f32).astype(bf16)
-    columns = dot(pick, padded[...], NT)
+    columns = down_ref[pl.ds(start, 16), :].astype(f32)
     spread = (iota((16, 4), 0) % 4 == iota((16, 4), 1)).astype(f32).astype(bf16)
     rows = dot(spread, up_ref[...], NN)
     rows = jnp.where(iota((16, 256), 1) // 64 == iota((16, 256), 0) // 4, rows, 0.0)
     rows = rows[:, :128] + rows[:, 128:]
     rows = rows + pltpu.roll(rows, 64, 1)
-    last = jnp.where(iota((16, 128), 1) >= 64, rows, columns[:, 256:])
-    whole = jnp.concatenate([columns[:, :256], last], axis=1)
-    whole = jnp.where(odd == 1, pltpu.roll(whole, 64, 1), whole).astype(bf16)
-    for i in range(16):
-        out_ref[i] = whole
-
-
-def pack_queries(hidden_ref, frozen_ref, factors_ref, out_ref, tokens, spread):
+    last = jnp.concatenate([columns[:, 256:], rows[:, :64]], axis=1)
+    even_tiles = [columns[:, :128], columns[:, 128:256], last]
+    turned = [pltpu.roll(tile, 64, 1) for tile in even_tiles]
+    low = iota((16, 128), 1) < 64
+    odd_tiles = [jnp.where(low, turned[i - 1], turned[i]) for i in range(3)]
+    for i in range(3):
+        tile = jnp.where(odd == 1, odd_tiles[i], even_tiles[i]).astype(bf16)
+        for peer in range(16):
+            out_ref[peer, :, 128 * i : 128 * i + 128] = tile
+
+
+def pack_queries(tokens_ref, frozen_ref, factors_ref, out_ref, columns, spread):
     f = lax.axis_index("fsdp")
-    tokens[0:2, :] = hidden_ref[0].astype(f32)
-    tokens[2:4, :] = hidden_ref[1].astype(f32)
-    lane = iota((16, 384), 1)
-    half = iota((16, 128), 1)
-    row = iota((16, 256), 0)
-    group = iota((16, 256), 1) // 64
-    low = jnp.zeros((4, 16), f32)
-    for rep in range(16):
-        start = 640 * (rep // 2) + 256 * (rep % 2)
-        part = factors_ref[rep].astype(f32)
-        if rep % 2 == 0:
-            columns = jnp.where(lane < 320, part, 0.0)
-            rows = jnp.where(half >= 64, part[:, 256:], 0.0)
-        else:
-            columns = jnp.where(lane >= 64, part, 0.0)
-            rows = jnp.where(half < 64, part[:, :128], 0.0)
-        low += dot(tokens[:, start : start + 384].astype(bf16), columns.astype(bf16), NT)
-        rows = rows + pltpu.roll(rows, 64, 1)
-        rows = jnp.concatenate([rows, rows], axis=1)
-        spread[16 * rep : 16 * rep + 16, :] = jnp.where(group == row // 4, rows, 0.0).astype(bf16)
+    low_half = iota((16, 128), 1) < 64
+    here = iota((16, 256), 1) // 64 == iota((16, 256), 0) // 4
+    for pair in range(8):
+        even, odd = factors_ref.at[2 * pair], factors_ref.at[2 * pair + 1]
+        at = 640 * pair
+        columns[:, at : at + 256] = even[:, 0:256]
+        columns[:, at + 384 : at + 640] = odd[:, 128:384]
+        last, first = even[:, 256:384].astype(f32), odd[:, 0:128].astype(f32)
+        columns[:, at + 256 : at + 384] = jnp.where(low_half, last, first).astype(bf16)
+        rows = jnp.where(low_half, first, last)
+        turned = pltpu.roll(rows, 64, 1)
+        for i, tile in enumerate((jnp.where(low_half, turned, rows), jnp.where(low_half, rows, turned))):
+            tile = jnp.where(here, jnp.concatenate([tile, tile], axis=1), 0.0)
+            spread[32 * pair + 16 * i : 32 * pair + 16 * i + 16, :] = tile.astype(bf16)
+    low = dot(tokens_ref[...], columns[...], NT)
     line, place = iota((64, 256), 0), iota((64, 256), 1)
     pick = ((place // 16 == line // 4) & (place % 4 == line % 4)).astype(f32).astype(bf16)
-    out_ref[0:64, :] = dot(pick, spread[...], NN).astype(bf16)
-    own = frozen_ref[...]
-    terms = [t.astype(f32) for t in split3(own)]
+    up = dot(pick, spread[...], NN).astype(bf16)
+    terms = [t.astype(f32) for t in split3(frozen_ref[...])]
     lanes = jnp.zeros((4, 256), f32)
     for i, term in enumerate(split3(low)):
         put = (iota((16, 256), 1) == iota((16, 256), 0) + 16 * f + 64 * i).astype(f32).astype(bf16)
         lanes += dot(term, put, NN)
-    out_ref[64:80, :] = jnp.concatenate(terms + [lanes], axis=0).astype(bf16)
+    tail = jnp.concatenate(terms + [lanes], axis=0).astype(bf16)
+    for peer in range(4):
+        out_ref[peer, 0:64, :] = up
+        out_ref[peer, 64:80, :] = tail
 
 
 def attend(parts_ref, gain_ref, keys_ref, values_ref, new_keys_ref, new_values_ref, lengths_ref, out_ref, queries, fresh_k, fresh_v):
@@ -146,6 +144,9 @@
             out_ref[i, :, 128 * j : 128 * j + 128] = result[4 * j + 2 * i : 4 * j + 2 * i + 2].astype(bf16)
 
 
+room = pltpu.CompilerParams(vmem_limit_bytes=8 * 2**20)
+
+
 def whole(n):
     return [pl.BlockSpec(memory_space=pltpu.VMEM)] * n
 
@@ -167,28 +168,29 @@
         out_shape=jax.ShapeDtypeStruct((16, 16, 384), bf16),
         in_specs=whole(2),
         out_specs=whole(1)[0],
-        scratch_shapes=[pltpu.VMEM((384, 64), bf16)],
+        compiler_params=room,
         name="pack_factors",
-    )(factor_down, factor_up)
+    )(factor_down.T, factor_up)
     factors = lax.all_to_all(packed, "rep", 0, 0)
-    frozen = jnp.dot(
-        hidden_in.reshape(4, 5120), frozen_query_matrix, preferred_element_type=f32
-    )
+    tokens = hidden_in.reshape(4, 5120)
+    frozen = jnp.dot(tokens, frozen_query_matrix, preferred_element_type=f32)
     sent = pl.pallas_call(
         pack_queries,
-        out_shape=jax.ShapeDtypeStruct((80, 256), bf16),
+        out_shape=jax.ShapeDtypeStruct((4, 80, 256), bf16),
         in_specs=whole(3),
         out_specs=whole(1)[0],
-        scratch_shapes=[pltpu.VMEM((4, 5120), f32), pltpu.VMEM((256, 256), bf16)],
+        scratch_shapes=[pltpu.VMEM((16, 5120), bf16), pltpu.VMEM((256, 256), bf16)],
+        compiler_params=room,
         name="pack_queries",
-    )(hidden_in, frozen, factors)
-    parts = lax.all_to_all(jnp.broadcast_to(sent, (4, 80, 256)), "fsdp", 0, 0)
+    )(tokens, frozen, factors)
+    parts = lax.all_to_all(sent, "fsdp", 0, 0)
     partial = pl.pallas_call(
         attend,
         out_shape=jax.ShapeDtypeStruct((4, 16, 128), f32),
         in_specs=whole(6) + [pl.BlockSpec(memory_space=pltpu.SMEM)],
         out_specs=whole(1)[0],
         scratch_shapes=[pltpu.VMEM((32, 128), f32)] + [pltpu.VMEM((128, 128), f32)] * 2,
+        compiler_params=room,
         name="attend",
     )(parts, query_gain.reshape(1, 128), key_cache, value_cache, new_keys, new_values, cache_lengths)
     partial = lax.all_to_all(partial, "fsdp", 0, 0)
@@ -197,6 +199,7 @@
         out_shape=jax.ShapeDtypeStruct((2, 2, 256), bf16),
         in_specs=whole(1),
         out_specs=whole(1)[0],
+        compiler_params=room,
         name="merge",
     )(partial)
 

time: 60.4 us -> 53.5 us (0.89)
  Pallas kernels: 8.07 us -> 3.47 us
  blocking collectives: 26.9 us -> 25.2 us
    pallas_call x1, Pallas kernels: 1.99 us -> 0.37 us  [on_device(): pl.pallas_call(pack_queries, out_shape=jax.ShapeDtypeStruct((4, 80, 256),...]
    all_to_all x1, blocking collectives: 11.8 us -> 10.2 us  [on_device(): partial = lax.all_to_all(partial, 'fsdp', 0, 0)]
    pallas_call x1, Pallas kernels: 2.7 us -> 1.34 us  [on_device(): pl.pallas_call(attend, out_shape=jax.ShapeDtypeStruct((4, 16, 128), f32),...]
    pallas_call x1, Pallas kernels: 1.89 us -> 1.03 us  [on_device(): pl.pallas_call(pack_factors, out_shape=jax.ShapeDtypeStruct((16, 16, 384)...]
    broadcast_in_dim x1 -> x0, local copies, waits for them, and re-layouts: 0.79 us -> none  [on_device(): parts = lax.all_to_all(jnp.broadcast_to(sent, (4, 80, 256)), 'fsdp', 0, 0)]
    pallas_call x1, Pallas kernels: 1.49 us -> 0.73 us  [on_device(): pl.pallas_call(merge, out_shape=jax.ShapeDtypeStruct((2, 2, 256), bf16),...]
    unnamed x5 -> x18, local copies, waits for them, and re-layouts: 2.35 us -> 2.7 us
  transfers between devices with their start and end apart: 1 -> 1, of which waited for: 1 -> 1; matrix products, arithmetic and copies ran while one was open for 3% -> 2% of each run, Pallas kernels for 0% -> 0%
where the time goes in v2:
time: 53.5 us; the launch traced here: 53.1 us
  blocking collectives  25.2 us (47%)
  starting transfers between devices  11.4 us (21%)
  waiting for transfers between devices  8.99 us (17%)
  local copies, waits for them, and re-layouts  3.5 us (7%)
  Pallas kernels  3.47 us (6%)
    all_to_all x1, blocking collectives, on_device(): parts = lax.all_to_all(sent, 'fsdp', 0, 0)  15 us
    all_to_all x1, starting transfers between devices, on_device(): factors = lax.all_to_all(packed, 'rep', 0, 0)  11.4 us
    all_to_all x1, blocking collectives, on_device(): partial = lax.all_to_all(partial, 'fsdp', 0, 0)  10.2 us
    all_to_all x1, waiting for transfers between devices, on_device(): factors = lax.all_to_all(packed, 'rep', 0, 0)  8.99 us
    unnamed x18, local copies, waits for them, and re-layouts  2.7 us
    pallas_call x1, Pallas kernels, on_device(): pl.pallas_call(attend, out_shape=jax.ShapeDtypeStruct((4, 16, 128), f32),...  1.34 us
  transfers between devices with their start and end apart: 1, of which 1 were waited for; matrix products, arithmetic and copies ran while one was open for 2% of the time, Pallas kernels for 0%

profile of v2, /device:TPU:6, one launch (start us, length us, event | category | flops | bytes accessed | tf_op | source)
XLA Modules:
  0.0 53.1 jit_solution(17582404468203457446)
XLA Ops:
  0.0 0.0 copy-start
  0.0 0.0 copy-start.1
  0.0 0.0 copy-start.3
  0.0 0.9 %copy-done.3 = bf16[320,64]{0,1:T(8,128)(2,1)S(1)} copy-done((bf16[320,64]{0,1:T(8,128)(2,1)S(1)}, bf16[320,64]{0,1:T(8,128)(2,1)}, u32[]{:S(2)}) %copy-start.3) | copy-done | bytes 40984
  1.0 0.0 copy-start.4
  1.0 0.7 %copy-done.4 = bf16[4,256]{1,0:T(4,128)(2,1)S(1)} copy-done((bf16[4,256]{1,0:T(4,128)(2,1)S(1)}, bf16[4,256]{1,0:T(4,128)(2,1)}, u32[]{:S(2)}) %copy-start.4) | copy-done | bytes 2072
  1.7 0.0 copy-start.5
  1.7 0.0 copy-start.6
  1.7 0.0 copy-start.7
  1.7 0.0 copy-start.8
  1.7 1.0 %pack_factors.1 = bf16[16,16,384]{2,1,0:T(8,128)(2,1)} custom-call(bf16[64,320]{1,0:T(8,128)(2,1)S(1)} %bitcast.4, bf16[4,256]{1,0:T(4,128)(2,1)S(1)} %copy-done.4), custom_call_target="tpu_custom_call" | custom-call | tf_op jit(solution)/shard_map/pack_factors/pallas_call | solution.py:166
  2.7 11.4 %all-to-all-start = ((bf16[16,16,384]{2,1,0:T(8,128)(2,1)}), bf16[16,16,384]{2,1,0:T(8,128)(2,1)S(1)}, u32[]{:S(2)}, u32[]{:S(2)}) async-start(bf16[16,16,384]{2,1,0:T(8,128)(2,1)} %pack_factors.1), calls=%async_computation | async-start | bytes 393216 | tf_op jit(solution)/shard_map/all_to_all | solution.py:174
  14.1 0.8 %reshape.6.tokens_ref = bf16[4,5120]{1,0:T(4,128)(2,1)S(1)} reshape(bf16[2,2,5120]{2,1,0:T(2,128)(2,1)} %param.10) | data formatting | bytes 81920 | tf_op jit(solution)/shard_map/reshape | solution.py:175
  14.9 0.0 copy-done
  14.9 0.4 fusion.frozen_ref
  15.4 9.0 %all-to-all-done.factors_ref = bf16[16,16,384]{2,1,0:T(8,128)(2,1)S(1)} async-done(((bf16[16,16,384]{2,1,0:T(8,128)(2,1)}), bf16[16,16,384]{2,1,0:T(8,128)(2,1)S(1)}, u32[]{:S(2)}, u32[]{:S(2)}) %all-to-all-start) | async-done | bytes 196640 | tf_op jit(solution)/shard_map/all_to_all | solution.py:174
  24.4 0.4 pack_queries.1
  24.7 15.0 %all_to_all.15.parts_ref = bf16[4,80,256]{2,1,0:T(8,128)(2,1)S(1)} all-to-all(bf16[4,80,256]{2,1,0:T(8,128)(2,1)S(1)} %pack_queries.1), channel_id=1, replica_groups=mesh['rep'=16,'tp'=8,'fsdp'=4] {'fsdp'}, dimensions={0} | all-to-all | bytes 327680 | tf_op jit(solution)/shard_map/all_to_all | solution.py:186
  39.7 0.0 copy-done.1
  39.7 0.0 copy-done.5
  39.7 0.0 copy-done.6
  39.7 0.0 copy-done.7
  39.8 0.0 copy-done.8
  39.8 0.0 copy-start.2
  39.8 1.0 %copy-done.2 = bf16[2,1024,128]{2,1,0:T(8,128)(2,1)S(1)} copy-done((bf16[2,1024,128]{2,1,0:T(8,128)(2,1)S(1)}, bf16[2,1024,128]{2,1,0:T(8,128)(2,1)}, u32[]{:S(2)}) %copy-start.2) | copy-done | bytes 524312
  40.8 1.3 %attend.1 = f32[4,16,128]{2,1,0:T(8,128)S(1)} custom-call(bf16[4,80,256]{2,1,0:T(8,128)(2,1)S(1)} %all_to_all.15.parts_ref, f32[1,128]{1,0:T(1,128)S(1)} %bitcast.5, bf16[2,1024,128]{2,1,0:T(8,128)(2,1)S(1)} %copy-done.1, bf16[2,1024,128]{2,1,0:T(8,128)(2,1)S(1)} %copy-done.2, bf16[2,2,128]{2,1,0:T(2,128)(2,1)S(1)} %copy-done.5, ...), custom_call_target="tpu_custom_call" | custom-call | tf_op jit(solution)/shard_map/attend/pallas_call | solution.py:187
  42.2 10.2 %all_to_all.16.parts_ref = f32[4,16,128]{2,1,0:T(8,128)S(1)} all-to-all(f32[4,16,128]{2,1,0:T(8,128)S(1)} %attend.1), channel_id=1, replica_groups=mesh['rep'=16,'tp'=8,'fsdp'=4] {'fsdp'}, dimensions={0} | all-to-all | bytes 65536 | tf_op jit(solution)/shard_map/all_to_all | solution.py:196
  52.4 0.7 %merge.1 = bf16[2,2,256]{2,1,0:T(2,128)(2,1)} custom-call(f32[4,16,128]{2,1,0:T(8,128)S(1)} %all_to_all.16.parts_ref), custom_call_target="tpu_custom_call" | custom-call | tf_op jit(solution)/shard_map/merge/pallas_call | solution.py:197
Async XLA Ops:
  0.0 14.9 %copy-start = (bf16[5120,256]{1,0:T(8,128)(2,1)S(1)}, bf16[5120,256]{1,0:T(8,128)(2,1)}, u32[]{:S(2)}) copy-start(bf16[5120,256]{1,0:T(8,128)(2,1)} %param.11) | copy-start | bytes 7864324
  0.0 39.7 %copy-start.1 = (bf16[2,1024,128]{2,1,0:T(8,128)(2,1)S(1)}, bf16[2,1024,128]{2,1,0:T(8,128)(2,1)}, u32[]{:S(2)}) copy-start(bf16[2,1024,128]{2,1,0:T(8,128)(2,1)} %keys_ref.1) | copy-start | bytes 1572868
  0.0 0.9 %copy-start.3 = (bf16[320,64]{0,1:T(8,128)(2,1)S(1)}, bf16[320,64]{0,1:T(8,128)(2,1)}, u32[]{:S(2)}) copy-start(bf16[320,64]{0,1:T(8,128)(2,1)} %param.12) | copy-start | bytes 122884
  1.0 0.7 %copy-start.4 = (bf16[4,256]{1,0:T(4,128)(2,1)S(1)}, bf16[4,256]{1,0:T(4,128)(2,1)}, u32[]{:S(2)}) copy-start(bf16[4,256]{1,0:T(4,128)(2,1)} %up_ref.1) | copy-start | bytes 6148
  1.7 38.1 %copy-start.5 = (bf16[2,2,128]{2,1,0:T(2,128)(2,1)S(1)}, bf16[2,2,128]{2,1,0:T(2,128)(2,1)}, u32[]{:S(2)}) copy-start(bf16[2,2,128]{2,1,0:T(2,128)(2,1)} %new_keys_ref.1) | copy-start | bytes 3076
  1.7 38.1 %copy-start.6 = (bf16[2,2,128]{2,1,0:T(2,128)(2,1)S(1)}, bf16[2,2,128]{2,1,0:T(2,128)(2,1)}, u32[]{:S(2)}) copy-start(bf16[2,2,128]{2,1,0:T(2,128)(2,1)} %new_values_ref.1) | copy-start | bytes 3076
  1.7 38.1 %copy-start.7 = (f32[128]{0:T(128)S(1)}, f32[128]{0:T(128)}, u32[]{:S(2)}) copy-start(f32[128]{0:T(128)} %param.14) | copy-start | bytes 1540
  1.7 38.1 %copy-start.8 = (s32[2]{0:T(128)S(1)}, s32[2]{0:T(128)}, u32[]{:S(2)}) copy-start(s32[2]{0:T(128)} %lengths_ref.1) | copy-start | bytes 28
  2.7 21.7 %all-to-all-start = ((bf16[16,16,384]{2,1,0:T(8,128)(2,1)}), bf16[16,16,384]{2,1,0:T(8,128)(2,1)S(1)}, u32[]{:S(2)}, u32[]{:S(2)}) async-start(bf16[16,16,384]{2,1,0:T(8,128)(2,1)} %pack_factors.1), calls=%async_computation | async-start | bytes 393216 | tf_op jit(solution)/shard_map/all_to_all | solution.py:174
  39.8 1.0 %copy-start.2 = (bf16[2,1024,128]{2,1,0:T(8,128)(2,1)S(1)}, bf16[2,1024,128]{2,1,0:T(8,128)(2,1)}, u32[]{:S(2)}) copy-start(bf16[2,1024,128]{2,1,0:T(8,128)(2,1)} %values_ref.1) | copy-start | bytes 1572868

commit v3 on v2

--- a/solution.py
+++ b/solution.py
@@ -30,27 +30,49 @@
     return hi, mid, lo
 
 
-def pack_factors(down_ref, up_ref, out_ref):
+def pack_factors(down_hbm, up_hbm, out_ref, down_ref, up_ref, rows_ref, sems):
     start = pl.multiple_of(16 * lax.axis_index("fsdp"), 16)
     odd = lax.rem(lax.axis_index("rep"), 2)
-    columns = down_ref[pl.ds(start, 16), :].astype(f32)
-    spread = (iota((16, 4), 0) % 4 == iota((16, 4), 1)).astype(f32).astype(bf16)
-    rows = dot(spread, up_ref[...], NN)
-    rows = jnp.where(iota((16, 256), 1) // 64 == iota((16, 256), 0) // 4, rows, 0.0)
-    rows = rows[:, :128] + rows[:, 128:]
-    rows = rows + pltpu.roll(rows, 64, 1)
-    last = jnp.concatenate([columns[:, 256:], rows[:, :64]], axis=1)
-    even_tiles = [columns[:, :128], columns[:, 128:256], last]
-    turned = [pltpu.roll(tile, 64, 1) for tile in even_tiles]
+    down_copy = pltpu.make_async_copy(down_hbm.at[pl.ds(start, 16), :], down_ref, sems.at[0])
+    up_copy = pltpu.make_async_copy(up_hbm, up_ref, sems.at[1])
+    down_copy.start()
+    up_copy.start()
+    up_copy.wait()
+    up = up_ref[...].astype(f32)
+    for i in range(2):
+        half = up[:, 128 * i : 128 * i + 128]
+        turned = pltpu.roll(half, 64, 1)
+        rows_ref[8 * i : 8 * i + 4, :] = jnp.where(odd == 1, half, turned)
+        rows_ref[8 * i + 4 : 8 * i + 8, :] = jnp.where(odd == 1, turned, half)
+    down_copy.wait()
+    columns = down_ref[...].astype(f32)
+    last = jnp.concatenate([columns[:, 256:], jnp.zeros((16, 64), f32)], axis=1)
     low = iota((16, 128), 1) < 64
-    odd_tiles = [jnp.where(low, turned[i - 1], turned[i]) for i in range(3)]
+    even_tiles = [columns[:, :128], columns[:, 128:256], jnp.where(low, last, rows_ref[...])]
+    turned = [pltpu.roll(tile, 64, 1) for tile in (columns[:, :128], columns[:, 128:256], last)]
+    odd_tiles = [jnp.where(low, rows_ref[...], turned[0])]
+    odd_tiles += [jnp.where(low, turned[i - 1], turned[i]) for i in (1, 2)]
     for i in range(3):
         tile = jnp.where(odd == 1, odd_tiles[i], even_tiles[i]).astype(bf16)
         for peer in range(16):
             out_ref[peer, :, 128 * i : 128 * i + 128] = tile
 
 
-def pack_queries(tokens_ref, frozen_ref, factors_ref, out_ref, columns, spread):
+def project(hidden_ref, frozen_ref, keys_hbm, values_hbm, tokens_ref, terms_ref, keys_ref, values_ref, sems):
+    keys_copy = pltpu.make_async_copy(keys_hbm, keys_ref, sems.at[0])
+    values_copy = pltpu.make_async_copy(values_hbm, values_ref, sems.at[1])
+    keys_copy.start()
+    values_copy.start()
+    tokens = jnp.concatenate([hidden_ref[0].astype(f32), hidden_ref[1].astype(f32)], axis=0)
+    tokens = tokens.astype(bf16)
+    tokens_ref[...] = tokens
+    terms = [t.astype(f32) for t in split3(dot(tokens, frozen_ref[...], NN))]
+    terms_ref[...] = jnp.concatenate(terms + [jnp.zeros((4, 256), f32)], axis=0)
+    keys_copy.wait()
+    values_copy.wait()
+
+
+def pack_queries(tokens_ref, terms_ref, factors_ref, out_ref, columns, spread):
     f = lax.axis_index("fsdp")
     low_half = iota((16, 128), 1) < 64
     here = iota((16, 256), 1) // 64 == iota((16, 256), 0) // 4
@@ -70,12 +92,11 @@
     line, place = iota((64, 256), 0), iota((64, 256), 1)
     pick = ((place // 16 == line // 4) & (place % 4 == line % 4)).astype(f32).astype(bf16)
     up = dot(pick, spread[...], NN).astype(bf16)
-    terms = [t.astype(f32) for t in split3(frozen_ref[...])]
     lanes = jnp.zeros((4, 256), f32)
     for i, term in enumerate(split3(low)):
         put = (iota((16, 256), 1) == iota((16, 256), 0) + 16 * f + 64 * i).astype(f32).astype(bf16)
         lanes += dot(term, put, NN)
-    tail = jnp.concatenate(terms + [lanes], axis=0).astype(bf16)
+    tail = jnp.concatenate([terms_ref[0:12, :], lanes], axis=0).astype(bf16)
     for peer in range(4):
         out_ref[peer, 0:64, :] = up
         out_ref[peer, 64:80, :] = tail
@@ -166,14 +187,32 @@
     packed = pl.pallas_call(
         pack_factors,
         out_shape=jax.ShapeDtypeStruct((16, 16, 384), bf16),
-        in_specs=whole(2),
-        out_specs=whole(1)[0],
-        compiler_params=room,
+        in_specs=[pl.BlockSpec(memory_space=pltpu.HBM)] * 2,
+        out_specs=whole(1)[0],
+        scratch_shapes=[
+            pltpu.VMEM((16, 320), bf16),
+            pltpu.VMEM((4, 256), bf16),
+            pltpu.VMEM((16, 128), f32),
+            pltpu.SemaphoreType.DMA((2,)),
+        ],
         name="pack_factors",
     )(factor_down.T, factor_up)
     factors = lax.all_to_all(packed, "rep", 0, 0)
-    tokens = hidden_in.reshape(4, 5120)
-    frozen = jnp.dot(tokens, frozen_query_matrix, preferred_element_type=f32)
+    tokens, terms, keys, values = pl.pallas_call(
+        project,
+        out_shape=(
+            jax.ShapeDtypeStruct((4, 5120), bf16),
+            jax.ShapeDtypeStruct((16, 256), f32),
+            jax.ShapeDtypeStruct(key_cache.shape, bf16),
+            jax.ShapeDtypeStruct(value_cache.shape, bf16),
+        ),
+        in_specs=whole(2) + [pl.BlockSpec(memory_space=pltpu.HBM)] * 2,
+        out_specs=tuple(whole(4)),
+        scratch_shapes=[pltpu.SemaphoreType.DMA((2,))],
+        compiler_params=room,
+        cost_estimate=pl.CostEstimate(flops=2 * 4 * 5120 * 256, bytes_accessed=8 * 2**20, transcendentals=0),
+        name="project",
+    )(hidden_in, frozen_query_matrix, key_cache, value_cache)
     sent = pl.pallas_call(
         pack_queries,
         out_shape=jax.ShapeDtypeStruct((4, 80, 256), bf16),
@@ -182,7 +221,7 @@
         scratch_shapes=[pltpu.VMEM((16, 5120), bf16), pltpu.VMEM((256, 256), bf16)],
         compiler_params=room,
         name="pack_queries",
-    )(tokens, frozen, factors)
+    )(tokens, terms, factors)
     parts = lax.all_to_all(sent, "fsdp", 0, 0)
     partial = pl.pallas_call(
         attend,
@@ -192,7 +231,7 @@
         scratch_shapes=[pltpu.VMEM((32, 128), f32)] + [pltpu.VMEM((128, 128), f32)] * 2,
         compiler_params=room,
         name="attend",
-    )(parts, query_gain.reshape(1, 128), key_cache, value_cache, new_keys, new_values, cache_lengths)
+    )(parts, query_gain.reshape(1, 128), keys, values, new_keys, new_values, cache_lengths)
     partial = lax.all_to_all(partial, "fsdp", 0, 0)
     return pl.pallas_call(
         merge,

time: 53.5 us -> 51.5 us (0.963)
  waiting for transfers between devices: 8.99 us -> 5.08 us
  Pallas kernels: 3.47 us -> 4.61 us
  local copies, waits for them, and re-layouts: 3.5 us -> 4.61 us
    all_to_all x1, waiting for transfers between devices: 8.99 us -> 5.08 us  [on_device(): factors = lax.all_to_all(packed, 'rep', 0, 0)]
    unnamed x18 -> x16, local copies, waits for them, and re-layouts: 2.7 us -> 4.61 us
    reshape x1 -> x0, local copies, waits for them, and re-layouts: 0.8 us -> none  [on_device(): tokens = hidden_in.reshape(4, 5120)]
    pallas_call x1, Pallas kernels: 1.03 us -> 1.61 us  [on_device(): pl.pallas_call(pack_factors, out_shape=jax.ShapeDtypeStruct((16, 16, 384)...]
    pallas_call x0 -> x1, Pallas kernels: none -> 0.55 us  [on_device(): pl.pallas_call(project, out_shape=(jax.ShapeDtypeStruct((4, 5120), bf16),...]
  transfers between devices with their start and end apart: 1 -> 1, of which waited for: 1 -> 1; matrix products, arithmetic and copies ran while one was open for 2% -> 0% of each run, Pallas kernels for 0% -> 1%
where the time goes in v3:
time: 51.5 us; the launch traced here: 51 us
  blocking collectives  25.2 us (49%)
  starting transfers between devices  11.4 us (22%)
  waiting for transfers between devices  5.08 us (10%)
  local copies, waits for them, and re-layouts  4.61 us (9%)
  Pallas kernels  4.61 us (9%)
    all_to_all x1, blocking collectives, on_device(): parts = lax.all_to_all(sent, 'fsdp', 0, 0)  15 us
    all_to_all x1, starting transfers between devices, on_device(): factors = lax.all_to_all(packed, 'rep', 0, 0)  11.4 us
    all_to_all x1, blocking collectives, on_device(): partial = lax.all_to_all(partial, 'fsdp', 0, 0)  10.2 us
    all_to_all x1, waiting for transfers between devices, on_device(): factors = lax.all_to_all(packed, 'rep', 0, 0)  5.08 us
    unnamed x16, local copies, waits for them, and re-layouts  4.61 us
    pallas_call x1, Pallas kernels, on_device(): pl.pallas_call(pack_factors, out_shape=jax.ShapeDtypeStruct((16, 16, 384)...  1.61 us
    pallas_call x1, Pallas kernels, on_device(): pl.pallas_call(attend, out_shape=jax.ShapeDtypeStruct((4, 16, 128), f32),...  1.34 us
  transfers between devices with their start and end apart: 1, of which 1 were waited for; matrix products, arithmetic and copies ran while one was open for 0% of the time, Pallas kernels for 1%

profile of v3, /device:TPU:6, one launch (start us, length us, event | category | flops | bytes accessed | tf_op | source)
XLA Modules:
  0.0 51.0 jit_solution(10890779674653193735)
XLA Ops:
  0.0 0.0 copy-start.7
  0.0 0.0 copy-start.5
  0.0 0.0 copy-start.4
  0.0 0.0 copy-start.6
  0.0 1.6 %pack_factors.1 = bf16[16,16,384]{2,1,0:T(8,128)(2,1)} custom-call(bf16[64,320]{1,0:T(8,128)(2,1)} %bitcast.3, bf16[4,256]{1,0:T(4,128)(2,1)} %up_hbm.1), custom_call_target="tpu_custom_call" | custom-call | tf_op jit(solution)/shard_map/pack_factors/pallas_call | solution.py:187
  1.6 11.4 %all-to-all-start = ((bf16[16,16,384]{2,1,0:T(8,128)(2,1)}), bf16[16,16,384]{2,1,0:T(8,128)(2,1)S(1)}, u32[]{:S(2)}, u32[]{:S(2)}) async-start(bf16[16,16,384]{2,1,0:T(8,128)(2,1)} %pack_factors.1), calls=%async_computation | async-start | bytes 393216 | tf_op jit(solution)/shard_map/all_to_all | solution.py:200
  13.1 0.0 copy-start
  13.1 1.7 %copy-done = bf16[5120,256]{1,0:T(8,128)(2,1)S(1)} copy-done((bf16[5120,256]{1,0:T(8,128)(2,1)S(1)}, bf16[5120,256]{1,0:T(8,128)(2,1)}, u32[]{:S(2)}) %copy-start) | copy-done | bytes 2621464
  14.8 0.0 copy-start.1
  14.8 1.0 %copy-done.1 = bf16[2,1024,128]{2,1,0:T(8,128)(2,1)S(1)} copy-done((bf16[2,1024,128]{2,1,0:T(8,128)(2,1)S(1)}, bf16[2,1024,128]{2,1,0:T(8,128)(2,1)}, u32[]{:S(2)}) %copy-start.1) | copy-done | bytes 524312
  15.9 0.0 copy-start.2
  15.9 1.0 %copy-done.2 = bf16[2,1024,128]{2,1,0:T(8,128)(2,1)S(1)} copy-done((bf16[2,1024,128]{2,1,0:T(8,128)(2,1)S(1)}, bf16[2,1024,128]{2,1,0:T(8,128)(2,1)}, u32[]{:S(2)}) %copy-start.2) | copy-done | bytes 524312
  16.9 0.0 copy-start.3
  16.9 0.8 %copy-done.3 = bf16[2,2,5120]{2,1,0:T(2,128)(2,1)S(1)} copy-done((bf16[2,2,5120]{2,1,0:T(2,128)(2,1)S(1)}, bf16[2,2,5120]{2,1,0:T(2,128)(2,1)}, u32[]{:S(2)}) %copy-start.3) | copy-done | bytes 40984
  17.7 0.6 %project.1 = (bf16[4,5120]{1,0:T(4,128)(2,1)S(1)}, f32[16,256]{1,0:T(8,128)S(1)}, bf16[2,1024,128]{2,1,0:T(8,128)(2,1)S(1)}, bf16[2,1024,128]{2,1,0:T(8,128)(2,1)S(1)}) custom-call(bf16[2,2,5120]{2,1,0:T(2,128)(2,1)S(1)} %copy-done.3, bf16[5120,256]{1,0:T(8,128)(2,1)S(1)} %copy-done, bf16[2,1024,128]{2,1,0:T(8,128)(2,1)S(1)} %copy-done.1, ...), custom_call_target="tpu_custom_call" | custom-call | flops 10485760 | bytes 8388608 | tf_op jit(solution)/shard_map/project/pallas_call | solution.py:201
  18.3 5.1 %all-to-all-done.factors_ref = bf16[16,16,384]{2,1,0:T(8,128)(2,1)S(1)} async-done(((bf16[16,16,384]{2,1,0:T(8,128)(2,1)}), bf16[16,16,384]{2,1,0:T(8,128)(2,1)S(1)}, u32[]{:S(2)}, u32[]{:S(2)}) %all-to-all-start) | async-done | bytes 196640 | tf_op jit(solution)/shard_map/all_to_all | solution.py:200
  23.3 0.4 pack_queries.1
  23.7 15.0 %all_to_all.15.parts_ref = bf16[4,80,256]{2,1,0:T(8,128)(2,1)S(1)} all-to-all(bf16[4,80,256]{2,1,0:T(8,128)(2,1)S(1)} %pack_queries.1), channel_id=1, replica_groups=mesh['rep'=16,'tp'=8,'fsdp'=4] {'fsdp'}, dimensions={0} | all-to-all | bytes 327680 | tf_op jit(solution)/shard_map/all_to_all | solution.py:225
  38.7 0.0 copy-done.7
  38.7 0.0 copy-done.5
  38.7 0.0 copy-done.4
  38.7 0.0 copy-done.6
  38.7 1.3 %attend.1 = f32[4,16,128]{2,1,0:T(8,128)S(1)} custom-call(bf16[4,80,256]{2,1,0:T(8,128)(2,1)S(1)} %all_to_all.15.parts_ref, f32[1,128]{1,0:T(1,128)S(1)} %bitcast.2, bf16[2,1024,128]{2,1,0:T(8,128)(2,1)S(1)} %get-tuple-element.11.keys_ref, bf16[2,1024,128]{2,1,0:T(8,128)(2,1)S(1)} %get-tuple-element.12.values_ref, bf16[2,2,128]{2,1,0:T(2,128)(2,1)S(1)} %copy-done.4, ...), custom_call_target="tpu_custom_call" | custom-call | tf_op jit(solution)/shard_map/attend/pallas_call | solution.py:226
  40.1 10.2 %all_to_all.16.parts_ref = f32[4,16,128]{2,1,0:T(8,128)S(1)} all-to-all(f32[4,16,128]{2,1,0:T(8,128)S(1)} %attend.1), channel_id=1, replica_groups=mesh['rep'=16,'tp'=8,'fsdp'=4] {'fsdp'}, dimensions={0} | all-to-all | bytes 65536 | tf_op jit(solution)/shard_map/all_to_all | solution.py:235
  50.3 0.7 %merge.1 = bf16[2,2,256]{2,1,0:T(2,128)(2,1)} custom-call(f32[4,16,128]{2,1,0:T(8,128)S(1)} %all_to_all.16.parts_ref), custom_call_target="tpu_custom_call" | custom-call | tf_op jit(solution)/shard_map/merge/pallas_call | solution.py:236
Async XLA Ops:
  0.0 38.7 %copy-start.7 = (s32[2]{0:T(128)S(1)}, s32[2]{0:T(128)}, u32[]{:S(2)}) copy-start(s32[2]{0:T(128)} %lengths_ref.1) | copy-start | bytes 28
  0.0 38.7 %copy-start.5 = (bf16[2,2,128]{2,1,0:T(2,128)(2,1)S(1)}, bf16[2,2,128]{2,1,0:T(2,128)(2,1)}, u32[]{:S(2)}) copy-start(bf16[2,2,128]{2,1,0:T(2,128)(2,1)} %new_values_ref.1) | copy-start | bytes 3076
  0.0 38.7 %copy-start.4 = (bf16[2,2,128]{2,1,0:T(2,128)(2,1)S(1)}, bf16[2,2,128]{2,1,0:T(2,128)(2,1)}, u32[]{:S(2)}) copy-start(bf16[2,2,128]{2,1,0:T(2,128)(2,1)} %new_keys_ref.1) | copy-start | bytes 3076
  0.0 38.7 %copy-start.6 = (f32[128]{0:T(128)S(1)}, f32[128]{0:T(128)}, u32[]{:S(2)}) copy-start(f32[128]{0:T(128)} %param.14) | copy-start | bytes 1540
  1.6 21.7 %all-to-all-start = ((bf16[16,16,384]{2,1,0:T(8,128)(2,1)}), bf16[16,16,384]{2,1,0:T(8,128)(2,1)S(1)}, u32[]{:S(2)}, u32[]{:S(2)}) async-start(bf16[16,16,384]{2,1,0:T(8,128)(2,1)} %pack_factors.1), calls=%async_computation | async-start | bytes 393216 | tf_op jit(solution)/shard_map/all_to_all | solution.py:200
  13.1 1.7 %copy-start = (bf16[5120,256]{1,0:T(8,128)(2,1)S(1)}, bf16[5120,256]{1,0:T(8,128)(2,1)}, u32[]{:S(2)}) copy-start(bf16[5120,256]{1,0:T(8,128)(2,1)} %frozen_ref.1) | copy-start | bytes 7864324
  14.8 1.0 %copy-start.1 = (bf16[2,1024,128]{2,1,0:T(8,128)(2,1)S(1)}, bf16[2,1024,128]{2,1,0:T(8,128)(2,1)}, u32[]{:S(2)}) copy-start(bf16[2,1024,128]{2,1,0:T(8,128)(2,1)} %keys_hbm.1) | copy-start | bytes 1572868
  15.9 1.0 %copy-start.2 = (bf16[2,1024,128]{2,1,0:T(8,128)(2,1)S(1)}, bf16[2,1024,128]{2,1,0:T(8,128)(2,1)}, u32[]{:S(2)}) copy-start(bf16[2,1024,128]{2,1,0:T(8,128)(2,1)} %values_hbm.1) | copy-start | bytes 1572868
  16.9 0.8 %copy-start.3 = (bf16[2,2,5120]{2,1,0:T(2,128)(2,1)S(1)}, bf16[2,2,5120]{2,1,0:T(2,128)(2,1)}, u32[]{:S(2)}) copy-start(bf16[2,2,5120]{2,1,0:T(2,128)(2,1)} %hidden_ref.1) | copy-start | bytes 122884

commit v4 on v3

v4 whole, which is shorter than its diff:
```python
import jax
import jax.numpy as jnp
from jax import lax
from jax.experimental import pallas as pl
from jax.experimental.pallas import tpu as pltpu
from jax.sharding import PartitionSpec as P

adapter_scale = 2.0
norm_epsilon = 1e-06
masked_score = -1e30

NT = (((1,), (1,)), ((), ()))
NN = (((1,), (0,)), ((), ()))
f32, bf16 = jnp.float32, jnp.bfloat16


def dot(a, b, dims):
    return lax.dot_general(a, b, dims, preferred_element_type=f32)


def iota(shape, axis):
    return lax.broadcasted_iota(jnp.int32, shape, axis)


def split3(x):
    hi = x.astype(bf16)
    rest = x - hi.astype(f32)
    mid = rest.astype(bf16)
    lo = (rest - mid.astype(f32)).astype(bf16)
    return hi, mid, lo


def pack_factors(down_hbm, up_hbm, out_ref, down_ref, up_ref, rows_ref, sems):
    start = pl.multiple_of(16 * lax.axis_index("fsdp"), 16)
    down_copy = pltpu.make_async_copy(down_hbm.at[pl.ds(start, 16), :], down_ref, sems.at[0])
    up_copy = pltpu.make_async_copy(up_hbm, up_ref, sems.at[1])
    down_copy.start()
    up_copy.start()
    up_copy.wait()
    up = up_ref[...].astype(f32)
    for i in range(2):
        half = up[:, 128 * i : 128 * i + 128]
        rows_ref[8 * i : 8 * i + 4, :] = pltpu.roll(half, 64, 1)
        rows_ref[8 * i + 4 : 8 * i + 8, :] = half
    down_copy.wait()
    columns = down_ref[...].astype(f32)
    last = jnp.concatenate([columns[:, 256:], jnp.zeros((16, 64), f32)], axis=1)
    last = jnp.where(iota((16, 128), 1) < 64, last, rows_ref[...])
    whole = jnp.concatenate([columns[:, :256], last], axis=1).astype(bf16)
    for peer in range(8):
        out_ref[peer] = whole


def project(hidden_hbm, frozen_hbm, keys_hbm, values_hbm, terms_ref, keys_ref, values_ref, hidden_ref, frozen_ref, sems):
    copies = [
        pltpu.make_async_copy(source, target, sems.at[i])
        for i, (source, target) in enumerate(
            (
                (hidden_hbm, hidden_ref),
                (frozen_hbm, frozen_ref),
                (keys_hbm, keys_ref),
                (values_hbm, values_ref),
            )
        )
    ]
    for copy in copies:
        copy.start()
    copies[0].wait()
    tokens = jnp.concatenate([hidden_ref[0].astype(f32), hidden_ref[1].astype(f32)], axis=0)
    copies[1].wait()
    terms = [t.astype(f32) for t in split3(dot(tokens.astype(bf16), frozen_ref[...], NN))]
    terms_ref[...] = jnp.concatenate(terms + [jnp.zeros((4, 256), f32)], axis=0)
    copies[2].wait()
    copies[3].wait()


def align(hidden_ref, other_ref, out_ref, tokens):
    upper = lax.axis_index("ylo") == 1
    for i in range(2):
        tokens[2 * i : 2 * i + 2, :] = hidden_ref[i].astype(f32)
        tokens[4 + 2 * i : 6 + 2 * i, :] = other_ref[i].astype(f32)
    low = iota((8, 128), 1) < 64
    for z in range(8):
        tiles = [tokens[:, 640 * z + 128 * i : 640 * z + 128 * i + 128] for i in range(5)]
        turned = [pltpu.roll(tile, 64, 1) for tile in tiles[2:]] + [jnp.zeros((8, 128), f32)]
        for i in range(3):
            shifted = jnp.where(low, turned[i], turned[i + 1])
            plain = tiles[i] if i < 2 else jnp.where(low, tiles[2], 0.0)
            at = 384 * z + 128 * i
            out_ref[:, at : at + 128] = jnp.where(upper, shifted, plain).astype(bf16)


def pack_queries(tokens_ref, terms_ref, factors_ref, out_ref, columns, spread):
    f, ylo = lax.axis_index("fsdp"), lax.axis_index("ylo")
    low_half = iota((16, 128), 1) < 64
    here = iota((16, 256), 1) // 64 == iota((16, 256), 0) // 4
    for z in range(8):
        columns[:, 384 * z : 384 * z + 384] = factors_ref[z]
        last = factors_ref[z, :, 256:384].astype(f32)
        rows = jnp.where(low_half, pltpu.roll(last, 64, 1), last)
        rows = jnp.where(here, jnp.concatenate([rows, rows], axis=1), 0.0)
        spread[16 * z : 16 * z + 16, :] = rows.astype(bf16)
    low = dot(tokens_ref[...], columns[...], NT)
    line, place = iota((32, 128), 0), iota((32, 128), 1)
    pick = ((place // 16 == line // 4) & (place % 4 == line % 4)).astype(f32).astype(bf16)
    up = dot(pick, spread[...], NN).astype(bf16)
    rank = iota((16, 256), 0) + 16 * f
    rank = 32 * (rank // 4 % 2) + 4 * (rank // 8) + rank % 4
    lanes = jnp.zeros((8, 256), f32)
    for i, term in enumerate(split3(low)):
        put = (iota((16, 256), 1) == rank + 64 * i).astype(f32).astype(bf16)
        lanes += dot(term, put, NN)
    for y in range(2):
        part = jnp.where(ylo == y, lanes[0:4], lanes[4:8])
        tail = jnp.concatenate([terms_ref[0:12, :], part], axis=0).astype(bf16)
        for peer in range(4):
            out_ref[2 * peer + y, 0:32, :] = up
            out_ref[2 * peer + y, 32:48, :] = tail


def attend(parts_ref, gain_ref, keys_ref, values_ref, new_keys_ref, new_values_ref, lengths_ref, out_ref, queries, fresh_k, fresh_v):
    f = lax.axis_index("fsdp")
    upper = lax.axis_index("ylo") == 1
    gain = gain_ref[...]
    tails = [parts_ref[i, 32:48, :].astype(f32) for i in range(8)]
    low = [tails[y][12:16] + tails[2 + y][12:16] + tails[4 + y][12:16] + tails[6 + y][12:16] for y in range(2)]
    low = jnp.concatenate(low, axis=0).astype(bf16)
    for i in range(4):
        up = jnp.concatenate([parts_ref[2 * i, 0:32, :], parts_ref[2 * i + 1, 0:32, :]] * 4, axis=0)
        tail = jnp.where(upper, tails[2 * i + 1], tails[2 * i])
        adapter = dot(low, up, NN)
        adapter = adapter[0:4] + adapter[4:8]
        query = tail[0:4] + tail[4:8] + tail[8:12] + adapter_scale * adapter
        for j in range(2):
            head = query[:, 128 * j : 128 * j + 128]
            mean = jnp.mean(head * head, axis=-1, keepdims=True)
            at = 8 * i + 4 * j
            queries[at : at + 4, :] = head * lax.rsqrt(mean + norm_epsilon) * gain
    normed = queries[...].astype(bf16)
    span = keys_ref.shape[1]
    fresh_k[...] = jnp.zeros_like(fresh_k)
    fresh_v[...] = jnp.zeros_like(fresh_v)
    for i in range(2):
        fresh_k[2 * i : 2 * i + 2, :] = new_keys_ref[i].astype(f32)
        fresh_v[2 * i : 2 * i + 2, :] = new_values_ref[i].astype(f32)
    scale = 128 ** (-0.5)
    first = iota((32, span), 0) % 4 < 2
    scores = jnp.where(first, dot(normed, keys_ref[0], NT), dot(normed, keys_ref[1], NT)) * scale
    limit = jnp.where(first, lengths_ref[0], lengths_ref[1])
    valid = iota((32, span), 1) + f * span < limit
    scores = jnp.where(valid, scores, masked_score)
    line, place = iota((32, 128), 0), iota((32, 128), 1)
    fresh = dot(normed, fresh_k[...].astype(bf16), NT) * scale
    fresh_valid = (place // 2 == (line % 4) // 2) & (place % 2 <= line % 2) & (f == 0)
    fresh = jnp.where(fresh_valid, fresh, masked_score)
    top = jnp.maximum(jnp.max(scores, axis=-1, keepdims=True), jnp.max(fresh, axis=-1, keepdims=True))
    weights = jnp.where(valid, jnp.exp(scores - top), 0.0)
    fresh_weights = jnp.where(fresh_valid, jnp.exp(fresh - top), 0.0)
    total = jnp.sum(weights, axis=-1, keepdims=True) + jnp.sum(fresh_weights, axis=-1, keepdims=True)
    mixed = (
        dot(jnp.where(first, weights, 0.0).astype(bf16), values_ref[0], NN)
        + dot(jnp.where(first, 0.0, weights).astype(bf16), values_ref[1], NN)
        + dot(fresh_weights.astype(bf16), fresh_v[...].astype(bf16), NN)
    )
    stats = jnp.where(iota((32, 128), 1) < 64, top, total)
    for i in range(4):
        out_ref[i, 0:8, :] = mixed[8 * i : 8 * i + 8]
        out_ref[i, 8:16, :] = stats[8 * i : 8 * i + 8]


def merge(parts_ref, out_ref):
    tops = [parts_ref[i, 8:16, 0:1] for i in range(4)]
    top = jnp.maximum(jnp.maximum(tops[0], tops[1]), jnp.maximum(tops[2], tops[3]))
    total = jnp.zeros((8, 1), f32)
    mixed = jnp.zeros((8, 128), f32)
    for i in range(4):
        scale = jnp.exp(tops[i] - top)
        total += scale * parts_ref[i, 8:16, 64:65]
        mixed += scale * parts_ref[i, 0:8, :]
    result = mixed / total
    for i in range(2):
        for j in range(2):
            out_ref[i, :, 128 * j : 128 * j + 128] = result[4 * j + 2 * i : 4 * j + 2 * i + 2].astype(bf16)


room = pltpu.CompilerParams(vmem_limit_bytes=8 * 2**20)


def whole(n):
    return [pl.BlockSpec(memory_space=pltpu.VMEM)] * n


def hbm(n):
    return [pl.BlockSpec(memory_space=pltpu.HBM)] * n


def far(x):
    return pltpu.with_memory_space_constraint(x, pltpu.HBM)


def on_device(
    hidden_in,
    frozen_query_matrix,
    factor_down,
    factor_up,
    query_gain,
    key_cache,
    value_cache,
    new_keys,
    new_values,
    cache_lengths,
):
    packed = pl.pallas_call(
        pack_factors,
        out_shape=jax.ShapeDtypeStruct((8, 16, 384), bf16),
        in_specs=hbm(2),
        out_specs=whole(1)[0],
        scratch_shapes=[
            pltpu.VMEM((16, 320), bf16),
            pltpu.VMEM((4, 256), bf16),
            pltpu.VMEM((16, 128), f32),
            pltpu.SemaphoreType.DMA((2,)),
        ],
        compiler_params=room,
        name="pack_factors",
    )(far(factor_down.T), far(factor_up))
    factors = lax.all_to_all(packed, "z", 0, 0)
    other = lax.ppermute(hidden_in, "ylo", ((0, 1), (1, 0)))
    terms, keys, values = pl.pallas_call(
        project,
        out_shape=(
            jax.ShapeDtypeStruct((16, 256), f32),
            pltpu.VMEM(key_cache.shape, bf16),
            pltpu.VMEM(value_cache.shape, bf16),
        ),
        in_specs=hbm(4),
        out_specs=tuple(whole(3)),
        scratch_shapes=[
            pltpu.VMEM((2, 2, 5120), bf16),
            pltpu.VMEM((5120, 256), bf16),
            pltpu.SemaphoreType.DMA((4,)),
        ],
        compiler_params=room,
        cost_estimate=pl.CostEstimate(flops=2 * 4 * 5120 * 256, bytes_accessed=8 * 2**20, transcendentals=0),
        name="project",
    )(far(hidden_in), far(frozen_query_matrix), far(key_cache), far(value_cache))
    aligned = pl.pallas_call(
        align,
        out_shape=jax.ShapeDtypeStruct((8, 8 * 384), bf16),
        in_specs=whole(2),
        out_specs=whole(1)[0],
        scratch_shapes=[pltpu.VMEM((8, 5120), f32)],
        compiler_params=room,
        name="align",
    )(hidden_in, other)
    sent = pl.pallas_call(
        pack_queries,
        out_shape=jax.ShapeDtypeStruct((8, 48, 256), bf16),
        in_specs=whole(3),
        out_specs=whole(1)[0],
        scratch_shapes=[pltpu.VMEM((16, 8 * 384), bf16), pltpu.VMEM((128, 256), bf16)],
        compiler_params=room,
        name="pack_queries",
    )(aligned, terms, factors)
    parts = lax.all_to_all(sent, ("fsdp", "ylo"), 0, 0)
    partial = pl.pallas_call(
        attend,
        out_shape=jax.ShapeDtypeStruct((4, 16, 128), f32),
        in_specs=whole(6) + [pl.BlockSpec(memory_space=pltpu.SMEM)],
        out_specs=whole(1)[0],
        scratch_shapes=[pltpu.VMEM((32, 128), f32)] + [pltpu.VMEM((128, 128), f32)] * 2,
        compiler_params=room,
        name="attend",
    )(parts, query_gain.reshape(1, 128), keys, values, new_keys, new_values, cache_lengths)
    partial = lax.all_to_all(partial, "fsdp", 0, 0)
    return pl.pallas_call(
        merge,
        out_shape=jax.ShapeDtypeStruct((2, 2, 256), bf16),
        in_specs=whole(1),
        out_specs=whole(1)[0],
        compiler_params=room,
        name="merge",
    )(partial)


def solution(mesh):
    rep = ("z", "ylo")
    lines = mesh.devices.reshape(mesh.devices.shape[0] // 2, 2, *mesh.devices.shape[1:])
    lines = jax.sharding.Mesh(lines, rep + mesh.axis_names[1:])
    placed = (
        P(rep, None, None),
        P(None, ("tp", "fsdp")),
        P(rep, None),
        P(rep, ("tp", "fsdp")),
        P(),
        P(rep, "fsdp", "tp"),
        P(rep, "fsdp", "tp"),
        P(rep, None, "tp"),
        P(rep, None, "tp"),
        P(rep),
    )
    return jax.shard_map(
        on_device,
        mesh=lines,
        in_specs=placed,
        out_specs=P(rep, None, ("tp", "fsdp")),
        check_vma=False,
    )
```

time: 51.5 us -> 50.2 us (0.975)
  local copies, waits for them, and re-layouts: 4.61 us -> 0.02 us
  starting transfers between devices: 11.4 us -> 13.8 us
  waiting for transfers between devices: 5.08 us -> 2.84 us
  blocking collectives: 25.2 us -> 26.9 us
  Pallas kernels: 4.61 us -> 6.28 us
    unnamed x16 -> x10, local copies, waits for them, and re-layouts: 4.61 us -> 0.02 us
    ppermute x0 -> x1, starting transfers between devices: none -> 3.47 us  [on_device(): other = lax.ppermute(hidden_in, 'ylo', ((0, 1), (1, 0)))]
    all_to_all x1, waiting for transfers between devices: 5.08 us -> 2.5 us  [on_device(): factors = lax.all_to_all(packed, 'z', 0, 0)]
    all_to_all x1, blocking collectives: 15 us -> 16.7 us  [on_device(): parts = lax.all_to_all(sent, ('fsdp', 'ylo'), 0, 0)]
    pallas_call x3 -> x4, Pallas kernels: 2.53 us -> 4.2 us  [the longest x1 2.27 us: on_device(): pl.pallas_call(project, out_shape=(jax.ShapeDtypeStruct((16, 256), f32),...]
    all_to_all x1, starting transfers between devices: 11.4 us -> 10.3 us  [on_device(): factors = lax.all_to_all(packed, 'z', 0, 0)]
  transfers between devices with their start and end apart: 1 -> 2, of which waited for: 1 -> 2; matrix products, arithmetic and copies ran while one was open for 0% -> 0% of each run, Pallas kernels for 1% -> 5%
where the time goes in v4:
time: 50.2 us; the launch traced here: 49.9 us
  blocking collectives  26.9 us (54%)
  starting transfers between devices  13.8 us (27%)
  Pallas kernels  6.28 us (13%)
  waiting for transfers between devices  2.84 us (6%)
    all_to_all x1, blocking collectives, on_device(): parts = lax.all_to_all(sent, ('fsdp', 'ylo'), 0, 0)  16.7 us
    all_to_all x1, starting transfers between devices, on_device(): factors = lax.all_to_all(packed, 'z', 0, 0)  10.3 us
    all_to_all x1, blocking collectives, on_device(): partial = lax.all_to_all(partial, 'fsdp', 0, 0)  10.2 us
    ppermute x1, starting transfers between devices, on_device(): other = lax.ppermute(hidden_in, 'ylo', ((0, 1), (1, 0)))  3.47 us
    all_to_all x1, waiting for transfers between devices, on_device(): factors = lax.all_to_all(packed, 'z', 0, 0)  2.5 us
    pallas_call x1, Pallas kernels, on_device(): pl.pallas_call(project, out_shape=(jax.ShapeDtypeStruct((16, 256), f32),...  2.27 us
    pallas_call x1, Pallas kernels, on_device(): pl.pallas_call(pack_factors, out_shape=jax.ShapeDtypeStruct((8, 16, 384),...  1.48 us
    pallas_call x1, Pallas kernels, on_device(): pl.pallas_call(attend, out_shape=jax.ShapeDtypeStruct((4, 16, 128), f32),...  1.35 us
  transfers between devices with their start and end apart: 2, of which 2 were waited for; matrix products, arithmetic and copies ran while one was open for 0% of the time, Pallas kernels for 5%

profile of v4, /device:TPU:6, one launch (start us, length us, event | category | flops | bytes accessed | tf_op | source)
XLA Modules:
  0.0 49.9 jit_solution(2499842591449362811)
XLA Ops:
  0.0 0.0 copy-start
  0.0 0.0 copy-start.4
  0.0 0.0 copy-start.2
  0.0 0.0 copy-start.1
  0.0 0.0 copy-start.3
  0.0 1.5 %pack_factors.1 = bf16[8,16,384]{2,1,0:T(8,128)(2,1)} custom-call(bf16[64,320]{1,0:T(8,128)(2,1)} %bitcast.3, bf16[4,256]{1,0:T(4,128)(2,1)} %up_hbm.1), custom_call_target="tpu_custom_call" | custom-call | tf_op jit(solution)/shard_map/pack_factors/pallas_call | solution.py:213
  1.5 10.3 %all-to-all-start = ((bf16[8,16,384]{2,1,0:T(8,128)(2,1)}), bf16[8,16,384]{2,1,0:T(8,128)(2,1)S(1)}, u32[]{:S(2)}, u32[]{:S(2)}) async-start(bf16[8,16,384]{2,1,0:T(8,128)(2,1)} %pack_factors.1), calls=%async_computation | async-start | bytes 196608 | tf_op jit(solution)/shard_map/all_to_all | solution.py:227
  11.8 3.5 %collective-permute-start = (bf16[2,2,5120]{2,1,0:T(2,128)(2,1)}, bf16[2,2,5120]{2,1,0:T(2,128)(2,1)S(1)}, u32[]{:S(2)}, u32[]{:S(2)}) collective-permute-start(bf16[2,2,5120]{2,1,0:T(2,128)(2,1)} %hidden_hbm.1), channel_id=1, source_target_pairs={{0,32},{32,0},{1,33},{33,1},{2,34},{34,2},{3,35},{35,3},{4,36},{36... | collective-permute-start | bytes 122888 | tf_op jit(solution)/shard_map/ppermute | solution.py:228
  15.3 2.3 %project.1 = (f32[16,256]{1,0:T(8,128)S(1)}, bf16[2,1024,128]{2,1,0:T(8,128)(2,1)S(1)}, bf16[2,1024,128]{2,1,0:T(8,128)(2,1)S(1)}) custom-call(bf16[2,2,5120]{2,1,0:T(2,128)(2,1)} %hidden_hbm.1, bf16[5120,256]{1,0:T(8,128)(2,1)} %frozen_hbm.1, bf16[2,1024,128]{2,1,0:T(8,128)(2,1)} %keys_hbm.1, bf16[2,1024,128]{2,1,0:T(8,128)(2,1)} %values_hbm.1), custom_call_target="tpu_custom_call" | custom-call | flops 10485760 | bytes 8388608 | tf_op jit(solution)/shard_map/project/pallas_call | solution.py:229
  17.6 0.3 collective-permute-done.other_ref
  17.9 0.0 copy-done
  17.9 0.1 align.1.tokens_ref
  18.1 2.5 %all-to-all-done.factors_ref = bf16[8,16,384]{2,1,0:T(8,128)(2,1)S(1)} async-done(((bf16[8,16,384]{2,1,0:T(8,128)(2,1)}), bf16[8,16,384]{2,1,0:T(8,128)(2,1)S(1)}, u32[]{:S(2)}, u32[]{:S(2)}) %all-to-all-start) | async-done | bytes 98336 | tf_op jit(solution)/shard_map/all_to_all | solution.py:227
  20.6 0.3 pack_queries.1
  20.9 16.7 %all_to_all.15.parts_ref = bf16[8,48,256]{2,1,0:T(8,128)(2,1)S(1)} all-to-all(bf16[8,48,256]{2,1,0:T(8,128)(2,1)S(1)} %pack_queries.1), channel_id=1, replica_groups=mesh['z'=8,'ylo'=2,'tp'=8,'fsdp'=4] {'fsdp','ylo'}, dimensions={0} | all-to-all | bytes 393216 | tf_op jit(solution)/shard_map/all_to_all | solution.py:265
  37.6 0.0 copy-done.4
  37.6 0.0 copy-done.2
  37.6 0.0 copy-done.1
  37.6 0.0 copy-done.3
  37.6 1.3 %attend.1 = f32[4,16,128]{2,1,0:T(8,128)S(1)} custom-call(bf16[8,48,256]{2,1,0:T(8,128)(2,1)S(1)} %all_to_all.15.parts_ref, f32[1,128]{1,0:T(1,128)S(1)} %bitcast.2, bf16[2,1024,128]{2,1,0:T(8,128)(2,1)S(1)} %get-tuple-element.9.keys_ref, bf16[2,1024,128]{2,1,0:T(8,128)(2,1)S(1)} %get-tuple-element.10.values_ref, bf16[2,2,128]{2,1,0:T(2,128)(2,1)S(1)} %copy-done.1, ...), custom_call_target="tpu_custom_call" | custom-call | tf_op jit(solution)/shard_map/attend/pallas_call | solution.py:266
  38.9 10.2 %all_to_all.16.parts_ref = f32[4,16,128]{2,1,0:T(8,128)S(1)} all-to-all(f32[4,16,128]{2,1,0:T(8,128)S(1)} %attend.1), channel_id=1, replica_groups=mesh['z'=8,'ylo'=2,'tp'=8,'fsdp'=4] {'fsdp'}, dimensions={0} | all-to-all | bytes 65536 | tf_op jit(solution)/shard_map/all_to_all | solution.py:275
  49.2 0.7 %merge.1 = bf16[2,2,256]{2,1,0:T(2,128)(2,1)} custom-call(f32[4,16,128]{2,1,0:T(8,128)S(1)} %all_to_all.16.parts_ref), custom_call_target="tpu_custom_call" | custom-call | tf_op jit(solution)/shard_map/merge/pallas_call | solution.py:276
Async XLA Ops:
  0.0 17.9 %copy-start = (bf16[2,2,5120]{2,1,0:T(2,128)(2,1)S(1)}, bf16[2,2,5120]{2,1,0:T(2,128)(2,1)}, u32[]{:S(2)}) copy-start(bf16[2,2,5120]{2,1,0:T(2,128)(2,1)} %hidden_hbm.1) | copy-start | bytes 122884
  0.0 37.6 %copy-start.4 = (s32[2]{0:T(128)S(1)}, s32[2]{0:T(128)}, u32[]{:S(2)}) copy-start(s32[2]{0:T(128)} %lengths_ref.1) | copy-start | bytes 28
  0.0 37.6 %copy-start.2 = (bf16[2,2,128]{2,1,0:T(2,128)(2,1)S(1)}, bf16[2,2,128]{2,1,0:T(2,128)(2,1)}, u32[]{:S(2)}) copy-start(bf16[2,2,128]{2,1,0:T(2,128)(2,1)} %new_values_ref.1) | copy-start | bytes 3076
  0.0 37.6 %copy-start.1 = (bf16[2,2,128]{2,1,0:T(2,128)(2,1)S(1)}, bf16[2,2,128]{2,1,0:T(2,128)(2,1)}, u32[]{:S(2)}) copy-start(bf16[2,2,128]{2,1,0:T(2,128)(2,1)} %new_keys_ref.1) | copy-start | bytes 3076
  0.0 37.6 %copy-start.3 = (f32[128]{0:T(128)S(1)}, f32[128]{0:T(128)}, u32[]{:S(2)}) copy-start(f32[128]{0:T(128)} %param.14) | copy-start | bytes 1540
  1.5 19.1 %all-to-all-start = ((bf16[8,16,384]{2,1,0:T(8,128)(2,1)}), bf16[8,16,384]{2,1,0:T(8,128)(2,1)S(1)}, u32[]{:S(2)}, u32[]{:S(2)}) async-start(bf16[8,16,384]{2,1,0:T(8,128)(2,1)} %pack_factors.1), calls=%async_computation | async-start | bytes 196608 | tf_op jit(solution)/shard_map/all_to_all | solution.py:227
  11.8 6.1 %collective-permute-start = (bf16[2,2,5120]{2,1,0:T(2,128)(2,1)}, bf16[2,2,5120]{2,1,0:T(2,128)(2,1)S(1)}, u32[]{:S(2)}, u32[]{:S(2)}) collective-permute-start(bf16[2,2,5120]{2,1,0:T(2,128)(2,1)} %hidden_hbm.1), channel_id=1, source_target_pairs={{0,32},{32,0},{1,33},{33,1},{2,34},{34,2},{3,35},{35,3},{4,36},{36... | collective-permute-start | bytes 122888 | tf_op jit(solution)/shard_map/ppermute | solution.py:228

commit v5 on v4

--- a/solution.py
+++ b/solution.py
@@ -8,6 +8,10 @@
 adapter_scale = 2.0
 norm_epsilon = 1e-06
 masked_score = -1e30
+
+z_order = (6, 7, 0, 1, 2, 3, 4, 5)
+y_order = (5, 6, 7, 0, 1, 2, 3, 4)
+fsdp_order = (2, 3, 0, 1)
 
 NT = (((1,), (1,)), ((), ()))
 NN = (((1,), (0,)), ((), ()))
@@ -80,13 +84,13 @@
         tokens[2 * i : 2 * i + 2, :] = hidden_ref[i].astype(f32)
         tokens[4 + 2 * i : 6 + 2 * i, :] = other_ref[i].astype(f32)
     low = iota((8, 128), 1) < 64
-    for z in range(8):
+    for peer, z in enumerate(z_order):
         tiles = [tokens[:, 640 * z + 128 * i : 640 * z + 128 * i + 128] for i in range(5)]
         turned = [pltpu.roll(tile, 64, 1) for tile in tiles[2:]] + [jnp.zeros((8, 128), f32)]
         for i in range(3):
             shifted = jnp.where(low, turned[i], turned[i + 1])
             plain = tiles[i] if i < 2 else jnp.where(low, tiles[2], 0.0)
-            at = 384 * z + 128 * i
+            at = 384 * peer + 128 * i
             out_ref[:, at : at + 128] = jnp.where(upper, shifted, plain).astype(bf16)
 
 
@@ -102,7 +106,10 @@
         spread[16 * z : 16 * z + 16, :] = rows.astype(bf16)
     low = dot(tokens_ref[...], columns[...], NT)
     line, place = iota((32, 128), 0), iota((32, 128), 1)
-    pick = ((place // 16 == line // 4) & (place % 4 == line % 4)).astype(f32).astype(bf16)
+    pick = jnp.zeros((32, 128), jnp.bool_)
+    for peer, z in enumerate(z_order):
+        pick |= (place // 16 == peer) & (line // 4 == z) & (place % 4 == line % 4)
+    pick = pick.astype(f32).astype(bf16)
     up = dot(pick, spread[...], NN).astype(bf16)
     rank = iota((16, 256), 0) + 16 * f
     rank = 32 * (rank // 4 % 2) + 4 * (rank // 8) + rank % 4
@@ -110,23 +117,25 @@
     for i, term in enumerate(split3(low)):
         put = (iota((16, 256), 1) == rank + 64 * i).astype(f32).astype(bf16)
         lanes += dot(term, put, NN)
+    tails = []
     for y in range(2):
         part = jnp.where(ylo == y, lanes[0:4], lanes[4:8])
-        tail = jnp.concatenate([terms_ref[0:12, :], part], axis=0).astype(bf16)
-        for peer in range(4):
-            out_ref[2 * peer + y, 0:32, :] = up
-            out_ref[2 * peer + y, 32:48, :] = tail
+        tails.append(jnp.concatenate([terms_ref[0:12, :], part], axis=0).astype(bf16))
+    for peer, y in enumerate(y_order):
+        out_ref[peer, 0:32, :] = up
+        out_ref[peer, 32:48, :] = tails[y % 2]
 
 
 def attend(parts_ref, gain_ref, keys_ref, values_ref, new_keys_ref, new_values_ref, lengths_ref, out_ref, queries, fresh_k, fresh_v):
     f = lax.axis_index("fsdp")
     upper = lax.axis_index("ylo") == 1
     gain = gain_ref[...]
-    tails = [parts_ref[i, 32:48, :].astype(f32) for i in range(8)]
+    peers = [y_order.index(y) for y in range(8)]
+    tails = [parts_ref[i, 32:48, :].astype(f32) for i in peers]
     low = [tails[y][12:16] + tails[2 + y][12:16] + tails[4 + y][12:16] + tails[6 + y][12:16] for y in range(2)]
     low = jnp.concatenate(low, axis=0).astype(bf16)
     for i in range(4):
-        up = jnp.concatenate([parts_ref[2 * i, 0:32, :], parts_ref[2 * i + 1, 0:32, :]] * 4, axis=0)
+        up = jnp.concatenate([parts_ref[peers[2 * i], 0:32, :], parts_ref[peers[2 * i + 1], 0:32, :]] * 4, axis=0)
         tail = jnp.where(upper, tails[2 * i + 1], tails[2 * i])
         adapter = dot(low, up, NN)
         adapter = adapter[0:4] + adapter[4:8]
@@ -163,9 +172,9 @@
         + dot(fresh_weights.astype(bf16), fresh_v[...].astype(bf16), NN)
     )
     stats = jnp.where(iota((32, 128), 1) < 64, top, total)
-    for i in range(4):
-        out_ref[i, 0:8, :] = mixed[8 * i : 8 * i + 8]
-        out_ref[i, 8:16, :] = stats[8 * i : 8 * i + 8]
+    for peer, i in enumerate(fsdp_order):
+        out_ref[peer, 0:8, :] = mixed[8 * i : 8 * i + 8]
+        out_ref[peer, 8:16, :] = stats[8 * i : 8 * i + 8]
 
 
 def merge(parts_ref, out_ref):
@@ -184,6 +193,10 @@
 
 
 room = pltpu.CompilerParams(vmem_limit_bytes=8 * 2**20)
+
+
+def exchange(x, axis, order):
+    return lax.all_to_all(x, axis, 0, 0, axis_index_groups=[list(order)])
 
 
 def whole(n):
@@ -224,7 +237,7 @@
         compiler_params=room,
         name="pack_factors",
     )(far(factor_down.T), far(factor_up))
-    factors = lax.all_to_all(packed, "z", 0, 0)
+    factors = exchange(packed, "z", z_order)
     other = lax.ppermute(hidden_in, "ylo", ((0, 1), (1, 0)))
     terms, keys, values = pl.pallas_call(
         project,
@@ -262,7 +275,7 @@
         compiler_params=room,
         name="pack_queries",
     )(aligned, terms, factors)
-    parts = lax.all_to_all(sent, ("fsdp", "ylo"), 0, 0)
+    parts = exchange(sent, ("fsdp", "ylo"), y_order)
     partial = pl.pallas_call(
         attend,
         out_shape=jax.ShapeDtypeStruct((4, 16, 128), f32),
@@ -272,7 +285,7 @@
         compiler_params=room,
         name="attend",
     )(parts, query_gain.reshape(1, 128), keys, values, new_keys, new_values, cache_lengths)
-    partial = lax.all_to_all(partial, "fsdp", 0, 0)
+    partial = exchange(partial, "fsdp", fsdp_order)
     return pl.pallas_call(
         merge,
         out_shape=jax.ShapeDtypeStruct((2, 2, 256), bf16),

time: 50.2 us -> 45.1 us (0.90)
  blocking collectives: 26.9 us -> 22.2 us
  waiting for transfers between devices: 2.84 us -> 0.34 us
  starting transfers between devices: 13.8 us -> 15.8 us
    all_to_all x2, blocking collectives: 26.9 us -> 22.2 us  [exchange(): return lax.all_to_all(x, axis, 0, 0, axis_index_groups=[list(order)])]
    all_to_all x1, waiting for transfers between devices: 2.5 us -> 0.01 us  [exchange(): return lax.all_to_all(x, axis, 0, 0, axis_index_groups=[list(order)])]
    all_to_all x1, starting transfers between devices: 10.3 us -> 12.3 us  [exchange(): return lax.all_to_all(x, axis, 0, 0, axis_index_groups=[list(order)])]
  transfers between devices with their start and end apart: 2 -> 2, of which waited for: 2 -> 1; matrix products, arithmetic and copies ran while one was open for 0% -> 0% of each run, Pallas kernels for 5% -> 5%
where the time goes in v5:
time: 45.1 us; the launch traced here: 44.7 us
  blocking collectives  22.2 us (49%)
  starting transfers between devices  15.8 us (35%)
  Pallas kernels  6.28 us (14%)
    all_to_all x2, blocking collectives, exchange(): return lax.all_to_all(x, axis, 0, 0, axis_index_groups=[list(order)])  22.2 us
    all_to_all x1, starting transfers between devices, exchange(): return lax.all_to_all(x, axis, 0, 0, axis_index_groups=[list(order)])  12.3 us
    ppermute x1, starting transfers between devices, on_device(): other = lax.ppermute(hidden_in, 'ylo', ((0, 1), (1, 0)))  3.47 us
    pallas_call x1, Pallas kernels, on_device(): pl.pallas_call(project, out_shape=(jax.ShapeDtypeStruct((16, 256), f32),...  2.27 us
    pallas_call x1, Pallas kernels, on_device(): pl.pallas_call(pack_factors, out_shape=jax.ShapeDtypeStruct((8, 16, 384),...  1.48 us
    pallas_call x1, Pallas kernels, on_device(): pl.pallas_call(attend, out_shape=jax.ShapeDtypeStruct((4, 16, 128), f32),...  1.34 us
  transfers between devices with their start and end apart: 2, of which 1 were waited for; matrix products, arithmetic and copies ran while one was open for 0% of the time, Pallas kernels for 5%

profile of v5, /device:TPU:6, one launch (start us, length us, event | category | flops | bytes accessed | tf_op | source)
XLA Modules:
  0.0 44.7 jit_solution(186486503569908309)
XLA Ops:
  0.0 0.0 copy-start
  0.0 0.0 copy-start.4
  0.0 0.0 copy-start.2
  0.0 0.0 copy-start.1
  0.0 0.0 copy-start.3
  0.0 1.5 %pack_factors.1 = bf16[8,16,384]{2,1,0:T(8,128)(2,1)} custom-call(bf16[64,320]{1,0:T(8,128)(2,1)} %bitcast.3, bf16[4,256]{1,0:T(4,128)(2,1)} %up_hbm.1), custom_call_target="tpu_custom_call" | custom-call | tf_op jit(solution)/shard_map/pack_factors/pallas_call | solution.py:226
  1.5 12.3 %all-to-all-start = ((bf16[8,16,384]{2,1,0:T(8,128)(2,1)}), bf16[8,16,384]{2,1,0:T(8,128)(2,1)S(1)}, u32[]{:S(2)}, u32[]{:S(2)}) async-start(bf16[8,16,384]{2,1,0:T(8,128)(2,1)} %pack_factors.1), calls=%async_computation | async-start | bytes 196608 | tf_op jit(solution)/shard_map/all_to_all | solution.py:199
  13.8 3.5 %collective-permute-start = (bf16[2,2,5120]{2,1,0:T(2,128)(2,1)}, bf16[2,2,5120]{2,1,0:T(2,128)(2,1)S(1)}, u32[]{:S(2)}, u32[]{:S(2)}) collective-permute-start(bf16[2,2,5120]{2,1,0:T(2,128)(2,1)} %hidden_hbm.1), channel_id=1, source_target_pairs={{0,32},{32,0},{1,33},{33,1},{2,34},{34,2},{3,35},{35,3},{4,36},{36... | collective-permute-start | bytes 122888 | tf_op jit(solution)/shard_map/ppermute | solution.py:241
  17.3 2.3 %project.1 = (f32[16,256]{1,0:T(8,128)S(1)}, bf16[2,1024,128]{2,1,0:T(8,128)(2,1)S(1)}, bf16[2,1024,128]{2,1,0:T(8,128)(2,1)S(1)}) custom-call(bf16[2,2,5120]{2,1,0:T(2,128)(2,1)} %hidden_hbm.1, bf16[5120,256]{1,0:T(8,128)(2,1)} %frozen_hbm.1, bf16[2,1024,128]{2,1,0:T(8,128)(2,1)} %keys_hbm.1, bf16[2,1024,128]{2,1,0:T(8,128)(2,1)} %values_hbm.1), custom_call_target="tpu_custom_call" | custom-call | flops 10485760 | bytes 8388608 | tf_op jit(solution)/shard_map/project/pallas_call | solution.py:242
  19.6 0.3 collective-permute-done.other_ref
  19.9 0.0 copy-done
  19.9 0.1 align.1.tokens_ref
  20.1 0.0 all-to-all-done.factors_ref
  20.1 0.3 pack_queries.1
  20.4 12.6 %all_to_all.15.parts_ref = bf16[8,48,256]{2,1,0:T(8,128)(2,1)S(1)} all-to-all(bf16[8,48,256]{2,1,0:T(8,128)(2,1)S(1)} %pack_queries.1), channel_id=1, replica_groups={{34,3,35,0,32,1,33,2},{38,7,39,4,36,5,37,6},{42,11,43,8,40,9,41,10},{46..., dimensions={0} | all-to-all | bytes 393216 | tf_op jit(solution)/shard_map/all_to_all | solution.py:199
  33.0 0.0 copy-done.4
  33.0 0.0 copy-done.2
  33.0 0.0 copy-done.1
  33.0 0.0 copy-done.3
  33.0 1.3 %attend.1 = f32[4,16,128]{2,1,0:T(8,128)S(1)} custom-call(bf16[8,48,256]{2,1,0:T(8,128)(2,1)S(1)} %all_to_all.15.parts_ref, f32[1,128]{1,0:T(1,128)S(1)} %bitcast.2, bf16[2,1024,128]{2,1,0:T(8,128)(2,1)S(1)} %get-tuple-element.9.keys_ref, bf16[2,1024,128]{2,1,0:T(8,128)(2,1)S(1)} %get-tuple-element.10.values_ref, bf16[2,2,128]{2,1,0:T(2,128)(2,1)S(1)} %copy-done.1, ...), custom_call_target="tpu_custom_call" | custom-call | tf_op jit(solution)/shard_map/attend/pallas_call | solution.py:279
  34.4 9.6 %all_to_all.16.parts_ref = f32[4,16,128]{2,1,0:T(8,128)S(1)} all-to-all(f32[4,16,128]{2,1,0:T(8,128)S(1)} %attend.1), channel_id=1, replica_groups={{2,3,0,1},{6,7,4,5},{10,11,8,9},{14,15,12,13},{18,19,16,17},{22,23,20,2..., dimensions={0} | all-to-all | bytes 65536 | tf_op jit(solution)/shard_map/all_to_all | solution.py:199
  44.0 0.7 %merge.1 = bf16[2,2,256]{2,1,0:T(2,128)(2,1)} custom-call(f32[4,16,128]{2,1,0:T(8,128)S(1)} %all_to_all.16.parts_ref), custom_call_target="tpu_custom_call" | custom-call | tf_op jit(solution)/shard_map/merge/pallas_call | solution.py:289
Async XLA Ops:
  0.0 19.9 %copy-start = (bf16[2,2,5120]{2,1,0:T(2,128)(2,1)S(1)}, bf16[2,2,5120]{2,1,0:T(2,128)(2,1)}, u32[]{:S(2)}) copy-start(bf16[2,2,5120]{2,1,0:T(2,128)(2,1)} %hidden_hbm.1) | copy-start | bytes 122884
  0.0 33.0 %copy-start.4 = (s32[2]{0:T(128)S(1)}, s32[2]{0:T(128)}, u32[]{:S(2)}) copy-start(s32[2]{0:T(128)} %lengths_ref.1) | copy-start | bytes 28
  0.0 33.0 %copy-start.2 = (bf16[2,2,128]{2,1,0:T(2,128)(2,1)S(1)}, bf16[2,2,128]{2,1,0:T(2,128)(2,1)}, u32[]{:S(2)}) copy-start(bf16[2,2,128]{2,1,0:T(2,128)(2,1)} %new_values_ref.1) | copy-start | bytes 3076
  0.0 33.0 %copy-start.1 = (bf16[2,2,128]{2,1,0:T(2,128)(2,1)S(1)}, bf16[2,2,128]{2,1,0:T(2,128)(2,1)}, u32[]{:S(2)}) copy-start(bf16[2,2,128]{2,1,0:T(2,128)(2,1)} %new_keys_ref.1) | copy-start | bytes 3076
  0.0 33.0 %copy-start.3 = (f32[128]{0:T(128)S(1)}, f32[128]{0:T(128)}, u32[]{:S(2)}) copy-start(f32[128]{0:T(128)} %param.14) | copy-start | bytes 1540
  1.5 18.5 %all-to-all-start = ((bf16[8,16,384]{2,1,0:T(8,128)(2,1)}), bf16[8,16,384]{2,1,0:T(8,128)(2,1)S(1)}, u32[]{:S(2)}, u32[]{:S(2)}) async-start(bf16[8,16,384]{2,1,0:T(8,128)(2,1)} %pack_factors.1), calls=%async_computation | async-start | bytes 196608 | tf_op jit(solution)/shard_map/all_to_all | solution.py:199
  13.8 6.1 %collective-permute-start = (bf16[2,2,5120]{2,1,0:T(2,128)(2,1)}, bf16[2,2,5120]{2,1,0:T(2,128)(2,1)S(1)}, u32[]{:S(2)}, u32[]{:S(2)}) collective-permute-start(bf16[2,2,5120]{2,1,0:T(2,128)(2,1)} %hidden_hbm.1), channel_id=1, source_target_pairs={{0,32},{32,0},{1,33},{33,1},{2,34},{34,2},{3,35},{35,3},{4,36},{36... | collective-permute-start | bytes 122888 | tf_op jit(solution)/shard_map/ppermute | solution.py:241

commit v6 on v5

--- a/solution.py
+++ b/solution.py
@@ -129,23 +129,24 @@
 def attend(parts_ref, gain_ref, keys_ref, values_ref, new_keys_ref, new_values_ref, lengths_ref, out_ref, queries, fresh_k, fresh_v):
     f = lax.axis_index("fsdp")
     upper = lax.axis_index("ylo") == 1
-    gain = gain_ref[...]
     peers = [y_order.index(y) for y in range(8)]
     tails = [parts_ref[i, 32:48, :].astype(f32) for i in peers]
     low = [tails[y][12:16] + tails[2 + y][12:16] + tails[4 + y][12:16] + tails[6 + y][12:16] for y in range(2)]
-    low = jnp.concatenate(low, axis=0).astype(bf16)
+    low = jnp.concatenate(low, axis=0)
+    low = jnp.concatenate([low[:, :128], low[:, 128:]], axis=0).astype(bf16)
     for i in range(4):
-        up = jnp.concatenate([parts_ref[peers[2 * i], 0:32, :], parts_ref[peers[2 * i + 1], 0:32, :]] * 4, axis=0)
+        up = jnp.concatenate([parts_ref[peers[2 * i], 0:32, :], parts_ref[peers[2 * i + 1], 0:32, :]] * 2, axis=0)
         tail = jnp.where(upper, tails[2 * i + 1], tails[2 * i])
         adapter = dot(low, up, NN)
+        adapter = adapter[0:8] + adapter[8:16]
         adapter = adapter[0:4] + adapter[4:8]
         query = tail[0:4] + tail[4:8] + tail[8:12] + adapter_scale * adapter
         for j in range(2):
-            head = query[:, 128 * j : 128 * j + 128]
-            mean = jnp.mean(head * head, axis=-1, keepdims=True)
             at = 8 * i + 4 * j
-            queries[at : at + 4, :] = head * lax.rsqrt(mean + norm_epsilon) * gain
-    normed = queries[...].astype(bf16)
+            queries[at : at + 4, :] = query[:, 128 * j : 128 * j + 128]
+    query = queries[...]
+    mean = jnp.mean(query * query, axis=-1, keepdims=True)
+    normed = (query * lax.rsqrt(mean + norm_epsilon) * gain_ref[...]).astype(bf16)
     span = keys_ref.shape[1]
     fresh_k[...] = jnp.zeros_like(fresh_k)
     fresh_v[...] = jnp.zeros_like(fresh_v)
@@ -153,38 +154,39 @@
         fresh_k[2 * i : 2 * i + 2, :] = new_keys_ref[i].astype(f32)
         fresh_v[2 * i : 2 * i + 2, :] = new_values_ref[i].astype(f32)
     scale = 128 ** (-0.5)
-    first = iota((32, span), 0) % 4 < 2
-    scores = jnp.where(first, dot(normed, keys_ref[0], NT), dot(normed, keys_ref[1], NT)) * scale
-    limit = jnp.where(first, lengths_ref[0], lengths_ref[1])
-    valid = iota((32, span), 1) + f * span < limit
-    scores = jnp.where(valid, scores, masked_score)
-    line, place = iota((32, 128), 0), iota((32, 128), 1)
+    first = iota((32, 128), 0) % 4 < 2
+    nothing = jnp.zeros_like(normed)
+    both = jnp.concatenate([jnp.where(first, normed, nothing), jnp.where(first, nothing, normed)], axis=1)
+    scores = dot(both, jnp.concatenate([keys_ref[0], keys_ref[1]], axis=1), NT) * scale
+    lengths = lengths_ref[...]
+    limit = jnp.where(iota((32, 1), 0) % 4 < 2, lengths[:, 0:1], lengths[:, 1:2]) - f * span
+    scores = jnp.where(iota((32, span), 1) < limit, scores, masked_score)
+    line, place = iota((32, 16), 0), iota((32, 16), 1)
     fresh = dot(normed, fresh_k[...].astype(bf16), NT) * scale
     fresh_valid = (place // 2 == (line % 4) // 2) & (place % 2 <= line % 2) & (f == 0)
     fresh = jnp.where(fresh_valid, fresh, masked_score)
     top = jnp.maximum(jnp.max(scores, axis=-1, keepdims=True), jnp.max(fresh, axis=-1, keepdims=True))
-    weights = jnp.where(valid, jnp.exp(scores - top), 0.0)
-    fresh_weights = jnp.where(fresh_valid, jnp.exp(fresh - top), 0.0)
+    weights = jnp.exp(scores - top)
+    fresh_weights = jnp.exp(fresh - top)
     total = jnp.sum(weights, axis=-1, keepdims=True) + jnp.sum(fresh_weights, axis=-1, keepdims=True)
-    mixed = (
-        dot(jnp.where(first, weights, 0.0).astype(bf16), values_ref[0], NN)
-        + dot(jnp.where(first, 0.0, weights).astype(bf16), values_ref[1], NN)
-        + dot(fresh_weights.astype(bf16), fresh_v[...].astype(bf16), NN)
-    )
-    stats = jnp.where(iota((32, 128), 1) < 64, top, total)
+    mixed = dot(weights.astype(bf16), jnp.concatenate([values_ref[0], values_ref[1]], axis=1), NN)
+    mixed = jnp.where(first, mixed[:, :128], mixed[:, 128:])
+    mixed += dot(fresh_weights.astype(bf16), fresh_v[...].astype(bf16), NN)
+    tops, totals = jnp.broadcast_to(top, (32, 128)), jnp.broadcast_to(total, (32, 128))
     for peer, i in enumerate(fsdp_order):
         out_ref[peer, 0:8, :] = mixed[8 * i : 8 * i + 8]
-        out_ref[peer, 8:16, :] = stats[8 * i : 8 * i + 8]
+        out_ref[peer, 8:16, :] = tops[8 * i : 8 * i + 8]
+        out_ref[peer, 16:24, :] = totals[8 * i : 8 * i + 8]
 
 
 def merge(parts_ref, out_ref):
-    tops = [parts_ref[i, 8:16, 0:1] for i in range(4)]
+    tops = [parts_ref[i, 8:16, :] for i in range(4)]
     top = jnp.maximum(jnp.maximum(tops[0], tops[1]), jnp.maximum(tops[2], tops[3]))
-    total = jnp.zeros((8, 1), f32)
+    total = jnp.zeros((8, 128), f32)
     mixed = jnp.zeros((8, 128), f32)
     for i in range(4):
         scale = jnp.exp(tops[i] - top)
-        total += scale * parts_ref[i, 8:16, 64:65]
+        total += scale * parts_ref[i, 16:24, :]
         mixed += scale * parts_ref[i, 0:8, :]
     result = mixed / total
     for i in range(2):
@@ -278,13 +280,13 @@
     parts = exchange(sent, ("fsdp", "ylo"), y_order)
     partial = pl.pallas_call(
         attend,
-        out_shape=jax.ShapeDtypeStruct((4, 16, 128), f32),
-        in_specs=whole(6) + [pl.BlockSpec(memory_space=pltpu.SMEM)],
-        out_specs=whole(1)[0],
-        scratch_shapes=[pltpu.VMEM((32, 128), f32)] + [pltpu.VMEM((128, 128), f32)] * 2,
+        out_shape=jax.ShapeDtypeStruct((4, 24, 128), f32),
+        in_specs=whole(7),
+        out_specs=whole(1)[0],
+        scratch_shapes=[pltpu.VMEM((32, 128), f32)] + [pltpu.VMEM((16, 128), f32)] * 2,
         compiler_params=room,
         name="attend",
-    )(parts, query_gain.reshape(1, 128), keys, values, new_keys, new_values, cache_lengths)
+    )(parts, query_gain.reshape(1, 128), keys, values, new_keys, new_values, cache_lengths.reshape(1, 2))
     partial = exchange(partial, "fsdp", fsdp_order)
     return pl.pallas_call(
         merge,

time: 45.1 us -> 44.5 us (0.987)
  Pallas kernels: 6.28 us -> 5.61 us
    pallas_call x1, Pallas kernels: 1.34 us -> 0.8 us  [on_device(): pl.pallas_call(attend, out_shape=jax.ShapeDtypeStruct((4, 24, 128), f32),...]
where the time goes in v6:
time: 44.5 us; the launch traced here: 44 us
  blocking collectives  22.2 us (50%)
  starting transfers between devices  15.8 us (36%)
  Pallas kernels  5.61 us (13%)
    all_to_all x2, blocking collectives, exchange(): return lax.all_to_all(x, axis, 0, 0, axis_index_groups=[list(order)])  22.2 us
    all_to_all x1, starting transfers between devices, exchange(): return lax.all_to_all(x, axis, 0, 0, axis_index_groups=[list(order)])  12.3 us
    ppermute x1, starting transfers between devices, on_device(): other = lax.ppermute(hidden_in, 'ylo', ((0, 1), (1, 0)))  3.47 us
    pallas_call x1, Pallas kernels, on_device(): pl.pallas_call(project, out_shape=(jax.ShapeDtypeStruct((16, 256), f32),...  2.27 us
    pallas_call x1, Pallas kernels, on_device(): pl.pallas_call(pack_factors, out_shape=jax.ShapeDtypeStruct((8, 16, 384),...  1.48 us
  transfers between devices with their start and end apart: 2, of which 1 were waited for; matrix products, arithmetic and copies ran while one was open for 0% of the time, Pallas kernels for 5%

profile of v6, /device:TPU:6, one launch (start us, length us, event | category | flops | bytes accessed | tf_op | source)
XLA Modules:
  0.0 44.0 jit_solution(11278821523944090628)
XLA Ops:
  0.0 0.0 copy-start
  0.0 0.0 copy-start.4
  0.0 0.0 copy-start.2
  0.0 0.0 copy-start.1
  0.0 0.0 copy-start.3
  0.0 1.5 %pack_factors.1 = bf16[8,16,384]{2,1,0:T(8,128)(2,1)} custom-call(bf16[64,320]{1,0:T(8,128)(2,1)} %bitcast.5, bf16[4,256]{1,0:T(4,128)(2,1)} %up_hbm.1), custom_call_target="tpu_custom_call" | custom-call | tf_op jit(solution)/shard_map/pack_factors/pallas_call | solution.py:228
  1.5 12.3 %all-to-all-start = ((bf16[8,16,384]{2,1,0:T(8,128)(2,1)}), bf16[8,16,384]{2,1,0:T(8,128)(2,1)S(1)}, u32[]{:S(2)}, u32[]{:S(2)}) async-start(bf16[8,16,384]{2,1,0:T(8,128)(2,1)} %pack_factors.1), calls=%async_computation | async-start | bytes 196608 | tf_op jit(solution)/shard_map/all_to_all | solution.py:201
  13.8 3.5 %collective-permute-start = (bf16[2,2,5120]{2,1,0:T(2,128)(2,1)}, bf16[2,2,5120]{2,1,0:T(2,128)(2,1)S(1)}, u32[]{:S(2)}, u32[]{:S(2)}) collective-permute-start(bf16[2,2,5120]{2,1,0:T(2,128)(2,1)} %hidden_hbm.1), channel_id=1, source_target_pairs={{0,32},{32,0},{1,33},{33,1},{2,34},{34,2},{3,35},{35,3},{4,36},{36... | collective-permute-start | bytes 122888 | tf_op jit(solution)/shard_map/ppermute | solution.py:243
  17.3 2.3 %project.1 = (f32[16,256]{1,0:T(8,128)S(1)}, bf16[2,1024,128]{2,1,0:T(8,128)(2,1)S(1)}, bf16[2,1024,128]{2,1,0:T(8,128)(2,1)S(1)}) custom-call(bf16[2,2,5120]{2,1,0:T(2,128)(2,1)} %hidden_hbm.1, bf16[5120,256]{1,0:T(8,128)(2,1)} %frozen_hbm.1, bf16[2,1024,128]{2,1,0:T(8,128)(2,1)} %keys_hbm.1, bf16[2,1024,128]{2,1,0:T(8,128)(2,1)} %values_hbm.1), custom_call_target="tpu_custom_call" | custom-call | flops 10485760 | bytes 8388608 | tf_op jit(solution)/shard_map/project/pallas_call | solution.py:244
  19.6 0.3 collective-permute-done.other_ref
  19.9 0.0 copy-done
  19.9 0.1 align.1.tokens_ref
  20.1 0.0 all-to-all-done.factors_ref
  20.1 0.3 pack_queries.1
  20.4 12.6 %all_to_all.15.parts_ref = bf16[8,48,256]{2,1,0:T(8,128)(2,1)S(1)} all-to-all(bf16[8,48,256]{2,1,0:T(8,128)(2,1)S(1)} %pack_queries.1), channel_id=1, replica_groups={{34,3,35,0,32,1,33,2},{38,7,39,4,36,5,37,6},{42,11,43,8,40,9,41,10},{46..., dimensions={0} | all-to-all | bytes 393216 | tf_op jit(solution)/shard_map/all_to_all | solution.py:201
  33.0 0.0 copy-done.4
  33.0 0.0 copy-done.2
  33.0 0.0 copy-done.1
  33.0 0.0 copy-done.3
  33.0 0.8 %attend.1 = f32[4,24,128]{2,1,0:T(8,128)S(1)} custom-call(bf16[8,48,256]{2,1,0:T(8,128)(2,1)S(1)} %all_to_all.15.parts_ref, f32[1,128]{1,0:T(1,128)S(1)} %bitcast.3, bf16[2,1024,128]{2,1,0:T(8,128)(2,1)S(1)} %get-tuple-element.9.keys_ref, bf16[2,1024,128]{2,1,0:T(8,128)(2,1)S(1)} %get-tuple-element.10.values_ref, bf16[2,2,128]{2,1,0:T(2,128)(2,1)S(1)} %copy-done.1, ...), custom_call_target="tpu_custom_call" | custom-call | tf_op jit(solution)/shard_map/attend/pallas_call | solution.py:281
  33.8 9.6 %all_to_all.16.parts_ref = f32[4,24,128]{2,1,0:T(8,128)S(1)} all-to-all(f32[4,24,128]{2,1,0:T(8,128)S(1)} %attend.1), channel_id=1, replica_groups={{2,3,0,1},{6,7,4,5},{10,11,8,9},{14,15,12,13},{18,19,16,17},{22,23,20,2..., dimensions={0} | all-to-all | bytes 98304 | tf_op jit(solution)/shard_map/all_to_all | solution.py:201
  43.4 0.6 %merge.1 = bf16[2,2,256]{2,1,0:T(2,128)(2,1)} custom-call(f32[4,24,128]{2,1,0:T(8,128)S(1)} %all_to_all.16.parts_ref), custom_call_target="tpu_custom_call" | custom-call | tf_op jit(solution)/shard_map/merge/pallas_call | solution.py:291
Async XLA Ops:
  0.0 19.9 %copy-start = (bf16[2,2,5120]{2,1,0:T(2,128)(2,1)S(1)}, bf16[2,2,5120]{2,1,0:T(2,128)(2,1)}, u32[]{:S(2)}) copy-start(bf16[2,2,5120]{2,1,0:T(2,128)(2,1)} %hidden_hbm.1) | copy-start | bytes 122884
  0.0 33.0 %copy-start.4 = (s32[2]{0:T(128)S(1)}, s32[2]{0:T(128)}, u32[]{:S(2)}) copy-start(s32[2]{0:T(128)} %param.19) | copy-start | bytes 28
  0.0 33.0 %copy-start.2 = (bf16[2,2,128]{2,1,0:T(2,128)(2,1)S(1)}, bf16[2,2,128]{2,1,0:T(2,128)(2,1)}, u32[]{:S(2)}) copy-start(bf16[2,2,128]{2,1,0:T(2,128)(2,1)} %new_values_ref.1) | copy-start | bytes 3076
  0.0 33.0 %copy-start.1 = (bf16[2,2,128]{2,1,0:T(2,128)(2,1)S(1)}, bf16[2,2,128]{2,1,0:T(2,128)(2,1)}, u32[]{:S(2)}) copy-start(bf16[2,2,128]{2,1,0:T(2,128)(2,1)} %new_keys_ref.1) | copy-start | bytes 3076
  0.0 33.0 %copy-start.3 = (f32[128]{0:T(128)S(1)}, f32[128]{0:T(128)}, u32[]{:S(2)}) copy-start(f32[128]{0:T(128)} %param.14) | copy-start | bytes 1540
  1.5 18.5 %all-to-all-start = ((bf16[8,16,384]{2,1,0:T(8,128)(2,1)}), bf16[8,16,384]{2,1,0:T(8,128)(2,1)S(1)}, u32[]{:S(2)}, u32[]{:S(2)}) async-start(bf16[8,16,384]{2,1,0:T(8,128)(2,1)} %pack_factors.1), calls=%async_computation | async-start | bytes 196608 | tf_op jit(solution)/shard_map/all_to_all | solution.py:201
  13.8 6.1 %collective-permute-start = (bf16[2,2,5120]{2,1,0:T(2,128)(2,1)}, bf16[2,2,5120]{2,1,0:T(2,128)(2,1)S(1)}, u32[]{:S(2)}, u32[]{:S(2)}) collective-permute-start(bf16[2,2,5120]{2,1,0:T(2,128)(2,1)} %hidden_hbm.1), channel_id=1, source_target_pairs={{0,32},{32,0},{1,33},{33,1},{2,34},{34,2},{3,35},{35,3},{4,36},{36... | collective-permute-start | bytes 122888 | tf_op jit(solution)/shard_map/ppermute | solution.py:243

commit v7 on v6

--- a/solution.py
+++ b/solution.py
@@ -34,12 +34,13 @@
     return hi, mid, lo
 
 
-def pack_factors(down_hbm, up_hbm, out_ref, down_ref, up_ref, rows_ref, sems):
-    start = pl.multiple_of(16 * lax.axis_index("fsdp"), 16)
-    down_copy = pltpu.make_async_copy(down_hbm.at[pl.ds(start, 16), :], down_ref, sems.at[0])
+def pack_factors(down_hbm, up_hbm, hidden_hbm, out_hbm, own_ref, other_ref, down_ref, up_ref, hidden_ref, rows_ref, packed, tokens, sems):
+    down_copy = pltpu.make_async_copy(down_hbm, down_ref, sems.at[0])
     up_copy = pltpu.make_async_copy(up_hbm, up_ref, sems.at[1])
+    hidden_copy = pltpu.make_async_copy(hidden_hbm, hidden_ref, sems.at[2])
     down_copy.start()
     up_copy.start()
+    hidden_copy.start()
     up_copy.wait()
     up = up_ref[...].astype(f32)
     for i in range(2):
@@ -47,23 +48,39 @@
         rows_ref[8 * i : 8 * i + 4, :] = pltpu.roll(half, 64, 1)
         rows_ref[8 * i + 4 : 8 * i + 8, :] = half
     down_copy.wait()
-    columns = down_ref[...].astype(f32)
+    start = pl.multiple_of(16 * lax.axis_index("fsdp"), 16)
+    columns = down_ref[pl.ds(start, 16), :].astype(f32)
     last = jnp.concatenate([columns[:, 256:], jnp.zeros((16, 64), f32)], axis=1)
     last = jnp.where(iota((16, 128), 1) < 64, last, rows_ref[...])
-    whole = jnp.concatenate([columns[:, :256], last], axis=1).astype(bf16)
-    for peer in range(8):
-        out_ref[peer] = whole
-
-
-def project(hidden_hbm, frozen_hbm, keys_hbm, values_hbm, terms_ref, keys_ref, values_ref, hidden_ref, frozen_ref, sems):
+    packed[...] = jnp.concatenate([columns[:, :256], last], axis=1).astype(bf16)
+    out_copies = [pltpu.make_async_copy(packed, out_hbm.at[peer], sems.at[3 + peer]) for peer in range(8)]
+    for copy in out_copies:
+        copy.start()
+    hidden_copy.wait()
+    upper = lax.axis_index("ylo") == 1
+    for i in range(2):
+        tokens[2 * i : 2 * i + 2, :] = hidden_ref[i].astype(f32)
+    low = iota((4, 128), 1) < 64
+    for peer, z in enumerate(z_order):
+        tiles = [tokens[:, 640 * z + 128 * i : 640 * z + 128 * i + 128] for i in range(5)]
+        turned = [pltpu.roll(tile, 64, 1) for tile in tiles[2:]] + [jnp.zeros((4, 128), f32)]
+        for i in range(3):
+            shifted = jnp.where(low, turned[i], turned[i + 1])
+            plain = tiles[i] if i < 2 else jnp.where(low, tiles[2], 0.0)
+            at = 384 * peer + 128 * i
+            own_ref[:, at : at + 128] = jnp.where(upper, shifted, plain).astype(bf16)
+            other_ref[:, at : at + 128] = jnp.where(upper, plain, shifted).astype(bf16)
+    for copy in out_copies:
+        copy.wait()
+
+
+def project(hidden_hbm, frozen_hbm, terms_ref, hidden_ref, frozen_ref, sems):
     copies = [
         pltpu.make_async_copy(source, target, sems.at[i])
         for i, (source, target) in enumerate(
             (
                 (hidden_hbm, hidden_ref),
                 (frozen_hbm, frozen_ref),
-                (keys_hbm, keys_ref),
-                (values_hbm, values_ref),
             )
         )
     ]
@@ -74,27 +91,9 @@
     copies[1].wait()
     terms = [t.astype(f32) for t in split3(dot(tokens.astype(bf16), frozen_ref[...], NN))]
     terms_ref[...] = jnp.concatenate(terms + [jnp.zeros((4, 256), f32)], axis=0)
-    copies[2].wait()
-    copies[3].wait()
-
-
-def align(hidden_ref, other_ref, out_ref, tokens):
-    upper = lax.axis_index("ylo") == 1
-    for i in range(2):
-        tokens[2 * i : 2 * i + 2, :] = hidden_ref[i].astype(f32)
-        tokens[4 + 2 * i : 6 + 2 * i, :] = other_ref[i].astype(f32)
-    low = iota((8, 128), 1) < 64
-    for peer, z in enumerate(z_order):
-        tiles = [tokens[:, 640 * z + 128 * i : 640 * z + 128 * i + 128] for i in range(5)]
-        turned = [pltpu.roll(tile, 64, 1) for tile in tiles[2:]] + [jnp.zeros((8, 128), f32)]
-        for i in range(3):
-            shifted = jnp.where(low, turned[i], turned[i + 1])
-            plain = tiles[i] if i < 2 else jnp.where(low, tiles[2], 0.0)
-            at = 384 * peer + 128 * i
-            out_ref[:, at : at + 128] = jnp.where(upper, shifted, plain).astype(bf16)
-
-
-def pack_queries(tokens_ref, terms_ref, factors_ref, out_ref, columns, spread):
+
+
+def pack_queries(own_ref, other_ref, terms_ref, factors_ref, out_ref, columns, spread):
     f, ylo = lax.axis_index("fsdp"), lax.axis_index("ylo")
     low_half = iota((16, 128), 1) < 64
     here = iota((16, 256), 1) // 64 == iota((16, 256), 0) // 4
@@ -104,7 +103,8 @@
         rows = jnp.where(low_half, pltpu.roll(last, 64, 1), last)
         rows = jnp.where(here, jnp.concatenate([rows, rows], axis=1), 0.0)
         spread[16 * z : 16 * z + 16, :] = rows.astype(bf16)
-    low = dot(tokens_ref[...], columns[...], NT)
+    tokens = jnp.concatenate([own_ref[...].astype(f32), other_ref[...].astype(f32)], axis=0).astype(bf16)
+    low = dot(tokens, columns[...], NT)
     line, place = iota((32, 128), 0), iota((32, 128), 1)
     pick = jnp.zeros((32, 128), jnp.bool_)
     for peer, z in enumerate(z_order):
@@ -225,58 +225,52 @@
     new_values,
     cache_lengths,
 ):
-    packed = pl.pallas_call(
+    packed, own, lent = pl.pallas_call(
         pack_factors,
-        out_shape=jax.ShapeDtypeStruct((8, 16, 384), bf16),
+        out_shape=(
+            jax.ShapeDtypeStruct((8, 16, 384), bf16),
+            pltpu.VMEM((4, 8 * 384), bf16),
+            jax.ShapeDtypeStruct((4, 8 * 384), bf16),
+        ),
+        in_specs=hbm(3),
+        out_specs=(hbm(1)[0], *whole(2)),
+        scratch_shapes=[
+            pltpu.VMEM((64, 320), bf16),
+            pltpu.VMEM((4, 256), bf16),
+            pltpu.VMEM((2, 2, 5120), bf16),
+            pltpu.VMEM((16, 128), f32),
+            pltpu.VMEM((16, 384), bf16),
+            pltpu.VMEM((4, 5120), f32),
+            pltpu.SemaphoreType.DMA((11,)),
+        ],
+        compiler_params=room,
+        name="pack_factors",
+    )(far(factor_down.T), far(factor_up), far(hidden_in))
+    factors = exchange(packed, "z", z_order)
+    other = lax.ppermute(lent, "ylo", ((0, 1), (1, 0)))
+    terms = pl.pallas_call(
+        project,
+        out_shape=jax.ShapeDtypeStruct((16, 256), f32),
         in_specs=hbm(2),
         out_specs=whole(1)[0],
         scratch_shapes=[
-            pltpu.VMEM((16, 320), bf16),
-            pltpu.VMEM((4, 256), bf16),
-            pltpu.VMEM((16, 128), f32),
+            pltpu.VMEM((2, 2, 5120), bf16),
+            pltpu.VMEM((5120, 256), bf16),
             pltpu.SemaphoreType.DMA((2,)),
         ],
         compiler_params=room,
-        name="pack_factors",
-    )(far(factor_down.T), far(factor_up))
-    factors = exchange(packed, "z", z_order)
-    other = lax.ppermute(hidden_in, "ylo", ((0, 1), (1, 0)))
-    terms, keys, values = pl.pallas_call(
-        project,
-        out_shape=(
-            jax.ShapeDtypeStruct((16, 256), f32),
-            pltpu.VMEM(key_cache.shape, bf16),
-            pltpu.VMEM(value_cache.shape, bf16),
-        ),
-        in_specs=hbm(4),
-        out_specs=tuple(whole(3)),
-        scratch_shapes=[
-            pltpu.VMEM((2, 2, 5120), bf16),
-            pltpu.VMEM((5120, 256), bf16),
-            pltpu.SemaphoreType.DMA((4,)),
-        ],
-        compiler_params=room,
         cost_estimate=pl.CostEstimate(flops=2 * 4 * 5120 * 256, bytes_accessed=8 * 2**20, transcendentals=0),
         name="project",
-    )(far(hidden_in), far(frozen_query_matrix), far(key_cache), far(value_cache))
-    aligned = pl.pallas_call(
-        align,
-        out_shape=jax.ShapeDtypeStruct((8, 8 * 384), bf16),
-        in_specs=whole(2),
-        out_specs=whole(1)[0],
-        scratch_shapes=[pltpu.VMEM((8, 5120), f32)],
-        compiler_params=room,
-        name="align",
-    )(hidden_in, other)
+    )(far(hidden_in), far(frozen_query_matrix))
     sent = pl.pallas_call(
         pack_queries,
         out_shape=jax.ShapeDtypeStruct((8, 48, 256), bf16),
-        in_specs=whole(3),
+        in_specs=whole(4),
         out_specs=whole(1)[0],
         scratch_shapes=[pltpu.VMEM((16, 8 * 384), bf16), pltpu.VMEM((128, 256), bf16)],
         compiler_params=room,
         name="pack_queries",
-    )(aligned, terms, factors)
+    )(own, other, terms, factors)
     parts = exchange(sent, ("fsdp", "ylo"), y_order)
     partial = pl.pallas_call(
         attend,
@@ -286,7 +280,7 @@
         scratch_shapes=[pltpu.VMEM((32, 128), f32)] + [pltpu.VMEM((16, 128), f32)] * 2,
         compiler_params=room,
         name="attend",
-    )(parts, query_gain.reshape(1, 128), keys, values, new_keys, new_values, cache_lengths.reshape(1, 2))
+    )(parts, query_gain.reshape(1, 128), key_cache, value_cache, new_keys, new_values, cache_lengths.reshape(1, 2))
     partial = exchange(partial, "fsdp", fsdp_order)
     return pl.pallas_call(
         merge,

time: 44.5 us -> 44.4 us (level)
    pallas_call x3 -> x2, Pallas kernels: 3.88 us -> 3.88 us  [the longest x1 2.25 us: on_device(): pl.pallas_call(project, out_shape=jax.ShapeDtypeStruct((16, 256), f32), i...]
  transfers between devices with their start and end apart: 2 -> 2, of which waited for: 1 -> 0; matrix products, arithmetic and copies ran while one was open for 0% -> 0% of each run, Pallas kernels for 5% -> 5%
where the time goes in v7:
time: 44.4 us; the launch traced here: 43.8 us
  blocking collectives  22.2 us (50%)
  starting transfers between devices  15.8 us (36%)
  Pallas kernels  5.61 us (13%)
    all_to_all x2, blocking collectives, exchange(): return lax.all_to_all(x, axis, 0, 0, axis_index_groups=[list(order)])  22.2 us
    all_to_all x1, starting transfers between devices, exchange(): return lax.all_to_all(x, axis, 0, 0, axis_index_groups=[list(order)])  12.3 us
    ppermute x1, starting transfers between devices, on_device(): other = lax.ppermute(lent, 'ylo', ((0, 1), (1, 0)))  3.47 us
    pallas_call x1, Pallas kernels, on_device(): pl.pallas_call(project, out_shape=jax.ShapeDtypeStruct((16, 256), f32), i...  2.25 us
    pallas_call x1, Pallas kernels, on_device(): pl.pallas_call(pack_factors, out_shape=(jax.ShapeDtypeStruct((8, 16, 384)...  1.63 us
  transfers between devices with their start and end apart: 2, of which 0 were waited for; matrix products, arithmetic and copies ran while one was open for 0% of the time, Pallas kernels for 5%

profile of v7, /device:TPU:6, one launch (start us, length us, event | category | flops | bytes accessed | tf_op | source)
XLA Modules:
  0.0 43.8 jit_solution(3151525300741991694)
XLA Ops:
  0.0 0.0 copy-start.5
  0.0 0.0 copy-start.3
  0.0 0.0 copy-start.2
  0.0 0.0 copy-start.1
  0.0 0.0 copy-start
  0.0 0.0 copy-start.4
  0.0 1.6 %pack_factors.1 = (bf16[8,16,384]{2,1,0:T(8,128)(2,1)}, bf16[4,3072]{1,0:T(4,128)(2,1)S(1)}, bf16[4,3072]{1,0:T(4,128)(2,1)S(1)}) custom-call(bf16[64,320]{1,0:T(8,128)(2,1)} %bitcast.5, bf16[4,256]{1,0:T(4,128)(2,1)} %up_hbm.1, bf16[2,2,5120]{2,1,0:T(2,128)(2,1)} %hidden_hbm.3), custom_call_target="tpu_custom_call" | custom-call | tf_op jit(solution)/shard_map/pack_factors/pallas_call | solution.py:228
  1.7 12.3 %all-to-all-start = ((bf16[8,16,384]{2,1,0:T(8,128)(2,1)}), bf16[8,16,384]{2,1,0:T(8,128)(2,1)S(1)}, u32[]{:S(2)}, u32[]{:S(2)}) async-start(bf16[8,16,384]{2,1,0:T(8,128)(2,1)} %get-tuple-element.10), calls=%async_computation | async-start | bytes 196608 | tf_op jit(solution)/shard_map/all_to_all | solution.py:201
  14.0 3.5 %collective-permute-start = (bf16[4,3072]{1,0:T(4,128)(2,1)S(1)}, bf16[4,3072]{1,0:T(4,128)(2,1)S(1)}, u32[]{:S(2)}, u32[]{:S(2)}) collective-permute-start(bf16[4,3072]{1,0:T(4,128)(2,1)S(1)} %get-tuple-element.9), channel_id=1, source_target_pairs={{0,32},{32,0},{1,33},{33,1},{2,34},{34,2},{3,35},{35,3},{4,36},{36... | collective-permute-start | bytes 73736 | tf_op jit(solution)/shard_map/ppermute | solution.py:250
  17.5 2.2 %project.1.terms_ref = f32[16,256]{1,0:T(8,128)S(1)} custom-call(bf16[2,2,5120]{2,1,0:T(2,128)(2,1)} %hidden_hbm.3, bf16[5120,256]{1,0:T(8,128)(2,1)} %frozen_hbm.1), custom_call_target="tpu_custom_call" | custom-call | flops 10485760 | bytes 8388608 | tf_op jit(solution)/shard_map/project/pallas_call | solution.py:251
  19.7 0.0 collective-permute-done.other_ref
  19.7 0.0 all-to-all-done.factors_ref
  19.7 0.3 pack_queries.1
  20.1 12.5 %all_to_all.15.parts_ref = bf16[8,48,256]{2,1,0:T(8,128)(2,1)S(1)} all-to-all(bf16[8,48,256]{2,1,0:T(8,128)(2,1)S(1)} %pack_queries.1), channel_id=1, replica_groups={{34,3,35,0,32,1,33,2},{38,7,39,4,36,5,37,6},{42,11,43,8,40,9,41,10},{46..., dimensions={0} | all-to-all | bytes 393216 | tf_op jit(solution)/shard_map/all_to_all | solution.py:201
  32.5 0.0 copy-done.5
  32.5 0.0 copy-done.3
  32.5 0.0 copy-done.2
  32.5 0.0 copy-done.1
  32.6 0.0 copy-done
  32.6 0.0 copy-done.4
  32.6 0.8 %attend.1 = f32[4,24,128]{2,1,0:T(8,128)S(1)} custom-call(bf16[8,48,256]{2,1,0:T(8,128)(2,1)S(1)} %all_to_all.15.parts_ref, f32[1,128]{1,0:T(1,128)S(1)} %bitcast.3, bf16[2,1024,128]{2,1,0:T(8,128)(2,1)S(1)} %copy-done, bf16[2,1024,128]{2,1,0:T(8,128)(2,1)S(1)} %copy-done.1, bf16[2,2,128]{2,1,0:T(2,128)(2,1)S(1)} %copy-done.2, ...), custom_call_target="tpu_custom_call" | custom-call | tf_op jit(solution)/shard_map/attend/pallas_call | solution.py:275
  33.4 9.8 %all_to_all.16.parts_ref = f32[4,24,128]{2,1,0:T(8,128)S(1)} all-to-all(f32[4,24,128]{2,1,0:T(8,128)S(1)} %attend.1), channel_id=1, replica_groups={{2,3,0,1},{6,7,4,5},{10,11,8,9},{14,15,12,13},{18,19,16,17},{22,23,20,2..., dimensions={0} | all-to-all | bytes 98304 | tf_op jit(solution)/shard_map/all_to_all | solution.py:201
  43.1 0.6 %merge.1 = bf16[2,2,256]{2,1,0:T(2,128)(2,1)} custom-call(f32[4,24,128]{2,1,0:T(8,128)S(1)} %all_to_all.16.parts_ref), custom_call_target="tpu_custom_call" | custom-call | tf_op jit(solution)/shard_map/merge/pallas_call | solution.py:285
Async XLA Ops:
  0.0 32.5 %copy-start.5 = (s32[2]{0:T(128)S(1)}, s32[2]{0:T(128)}, u32[]{:S(2)}) copy-start(s32[2]{0:T(128)} %param.19) | copy-start | bytes 28
  0.0 32.5 %copy-start.3 = (bf16[2,2,128]{2,1,0:T(2,128)(2,1)S(1)}, bf16[2,2,128]{2,1,0:T(2,128)(2,1)}, u32[]{:S(2)}) copy-start(bf16[2,2,128]{2,1,0:T(2,128)(2,1)} %new_values_ref.1) | copy-start | bytes 3076
  0.0 32.5 %copy-start.2 = (bf16[2,2,128]{2,1,0:T(2,128)(2,1)S(1)}, bf16[2,2,128]{2,1,0:T(2,128)(2,1)}, u32[]{:S(2)}) copy-start(bf16[2,2,128]{2,1,0:T(2,128)(2,1)} %new_keys_ref.1) | copy-start | bytes 3076
  0.0 32.5 %copy-start.1 = (bf16[2,1024,128]{2,1,0:T(8,128)(2,1)S(1)}, bf16[2,1024,128]{2,1,0:T(8,128)(2,1)}, u32[]{:S(2)}) copy-start(bf16[2,1024,128]{2,1,0:T(8,128)(2,1)} %values_ref.1) | copy-start | bytes 1572868
  0.0 32.5 %copy-start = (bf16[2,1024,128]{2,1,0:T(8,128)(2,1)S(1)}, bf16[2,1024,128]{2,1,0:T(8,128)(2,1)}, u32[]{:S(2)}) copy-start(bf16[2,1024,128]{2,1,0:T(8,128)(2,1)} %keys_ref.1) | copy-start | bytes 1572868
  0.0 32.5 %copy-start.4 = (f32[128]{0:T(128)S(1)}, f32[128]{0:T(128)}, u32[]{:S(2)}) copy-start(f32[128]{0:T(128)} %param.14) | copy-start | bytes 1540
  1.7 18.1 %all-to-all-start = ((bf16[8,16,384]{2,1,0:T(8,128)(2,1)}), bf16[8,16,384]{2,1,0:T(8,128)(2,1)S(1)}, u32[]{:S(2)}, u32[]{:S(2)}) async-start(bf16[8,16,384]{2,1,0:T(8,128)(2,1)} %get-tuple-element.10), calls=%async_computation | async-start | bytes 196608 | tf_op jit(solution)/shard_map/all_to_all | solution.py:201
  14.0 5.7 %collective-permute-start = (bf16[4,3072]{1,0:T(4,128)(2,1)S(1)}, bf16[4,3072]{1,0:T(4,128)(2,1)S(1)}, u32[]{:S(2)}, u32[]{:S(2)}) collective-permute-start(bf16[4,3072]{1,0:T(4,128)(2,1)S(1)} %get-tuple-element.9), channel_id=1, source_target_pairs={{0,32},{32,0},{1,33},{33,1},{2,34},{34,2},{3,35},{35,3},{4,36},{36... | collective-permute-start | bytes 73736 | tf_op jit(solution)/shard_map/ppermute | solution.py:250

commit v8 on v7

--- a/solution.py
+++ b/solution.py
@@ -10,7 +10,7 @@
 masked_score = -1e30
 
 z_order = (6, 7, 0, 1, 2, 3, 4, 5)
-y_order = (5, 6, 7, 0, 1, 2, 3, 4)
+y_order = (5, 1, 0, 2, 3, 4, 6, 7)
 fsdp_order = (2, 3, 0, 1)
 
 NT = (((1,), (1,)), ((), ()))

time: 44.4 us -> 43.9 us (0.989)
  no operation moved by 1% of the time
where the time goes in v8:
time: 43.9 us; the launch traced here: 43.6 us
  blocking collectives  22.1 us (50%)
  starting transfers between devices  15.8 us (36%)
  Pallas kernels  5.61 us (13%)
    all_to_all x2, blocking collectives, exchange(): return lax.all_to_all(x, axis, 0, 0, axis_index_groups=[list(order)])  22.1 us
    all_to_all x1, starting transfers between devices, exchange(): return lax.all_to_all(x, axis, 0, 0, axis_index_groups=[list(order)])  12.3 us
    ppermute x1, starting transfers between devices, on_device(): other = lax.ppermute(lent, 'ylo', ((0, 1), (1, 0)))  3.47 us
    pallas_call x1, Pallas kernels, on_device(): pl.pallas_call(project, out_shape=jax.ShapeDtypeStruct((16, 256), f32), i...  2.25 us
    pallas_call x1, Pallas kernels, on_device(): pl.pallas_call(pack_factors, out_shape=(jax.ShapeDtypeStruct((8, 16, 384)...  1.63 us
  transfers between devices with their start and end apart: 2, of which 0 were waited for; matrix products, arithmetic and copies ran while one was open for 0% of the time, Pallas kernels for 5%

profile of v8, /device:TPU:6, one launch (start us, length us, event | category | flops | bytes accessed | tf_op | source)
XLA Modules:
  0.0 43.6 jit_solution(14236781381378746447)
XLA Ops:
  0.0 0.0 copy-start.5
  0.0 0.0 copy-start.3
  0.0 0.0 copy-start.2
  0.0 0.0 copy-start.1
  0.0 0.0 copy-start
  0.0 0.0 copy-start.4
  0.0 1.6 %pack_factors.1 = (bf16[8,16,384]{2,1,0:T(8,128)(2,1)}, bf16[4,3072]{1,0:T(4,128)(2,1)S(1)}, bf16[4,3072]{1,0:T(4,128)(2,1)S(1)}) custom-call(bf16[64,320]{1,0:T(8,128)(2,1)} %bitcast.5, bf16[4,256]{1,0:T(4,128)(2,1)} %up_hbm.1, bf16[2,2,5120]{2,1,0:T(2,128)(2,1)} %hidden_hbm.3), custom_call_target="tpu_custom_call" | custom-call | tf_op jit(solution)/shard_map/pack_factors/pallas_call | solution.py:228
  1.7 12.3 %all-to-all-start = ((bf16[8,16,384]{2,1,0:T(8,128)(2,1)}), bf16[8,16,384]{2,1,0:T(8,128)(2,1)S(1)}, u32[]{:S(2)}, u32[]{:S(2)}) async-start(bf16[8,16,384]{2,1,0:T(8,128)(2,1)} %get-tuple-element.10), calls=%async_computation | async-start | bytes 196608 | tf_op jit(solution)/shard_map/all_to_all | solution.py:201
  14.0 3.5 %collective-permute-start = (bf16[4,3072]{1,0:T(4,128)(2,1)S(1)}, bf16[4,3072]{1,0:T(4,128)(2,1)S(1)}, u32[]{:S(2)}, u32[]{:S(2)}) collective-permute-start(bf16[4,3072]{1,0:T(4,128)(2,1)S(1)} %get-tuple-element.9), channel_id=1, source_target_pairs={{0,32},{32,0},{1,33},{33,1},{2,34},{34,2},{3,35},{35,3},{4,36},{36... | collective-permute-start | bytes 73736 | tf_op jit(solution)/shard_map/ppermute | solution.py:250
  17.5 2.2 %project.1.terms_ref = f32[16,256]{1,0:T(8,128)S(1)} custom-call(bf16[2,2,5120]{2,1,0:T(2,128)(2,1)} %hidden_hbm.3, bf16[5120,256]{1,0:T(8,128)(2,1)} %frozen_hbm.1), custom_call_target="tpu_custom_call" | custom-call | flops 10485760 | bytes 8388608 | tf_op jit(solution)/shard_map/project/pallas_call | solution.py:251
  19.7 0.0 collective-permute-done.other_ref
  19.7 0.0 all-to-all-done.factors_ref
  19.7 0.3 pack_queries.1
  20.1 12.6 %all_to_all.15.parts_ref = bf16[8,48,256]{2,1,0:T(8,128)(2,1)S(1)} all-to-all(bf16[8,48,256]{2,1,0:T(8,128)(2,1)S(1)} %pack_queries.1), channel_id=1, replica_groups={{34,32,0,1,33,2,3,35},{38,36,4,5,37,6,7,39},{42,40,8,9,41,10,11,43},{46..., dimensions={0} | all-to-all | bytes 393216 | tf_op jit(solution)/shard_map/all_to_all | solution.py:201
  32.7 0.0 copy-done.5
  32.7 0.0 copy-done.3
  32.7 0.0 copy-done.2
  32.7 0.0 copy-done.1
  32.7 0.0 copy-done
  32.8 0.0 copy-done.4
  32.8 0.8 %attend.1 = f32[4,24,128]{2,1,0:T(8,128)S(1)} custom-call(bf16[8,48,256]{2,1,0:T(8,128)(2,1)S(1)} %all_to_all.15.parts_ref, f32[1,128]{1,0:T(1,128)S(1)} %bitcast.3, bf16[2,1024,128]{2,1,0:T(8,128)(2,1)S(1)} %copy-done, bf16[2,1024,128]{2,1,0:T(8,128)(2,1)S(1)} %copy-done.1, bf16[2,2,128]{2,1,0:T(2,128)(2,1)S(1)} %copy-done.2, ...), custom_call_target="tpu_custom_call" | custom-call | tf_op jit(solution)/shard_map/attend/pallas_call | solution.py:275
  33.6 9.4 %all_to_all.16.parts_ref = f32[4,24,128]{2,1,0:T(8,128)S(1)} all-to-all(f32[4,24,128]{2,1,0:T(8,128)S(1)} %attend.1), channel_id=1, replica_groups={{2,3,0,1},{6,7,4,5},{10,11,8,9},{14,15,12,13},{18,19,16,17},{22,23,20,2..., dimensions={0} | all-to-all | bytes 98304 | tf_op jit(solution)/shard_map/all_to_all | solution.py:201
  43.0 0.6 %merge.1 = bf16[2,2,256]{2,1,0:T(2,128)(2,1)} custom-call(f32[4,24,128]{2,1,0:T(8,128)S(1)} %all_to_all.16.parts_ref), custom_call_target="tpu_custom_call" | custom-call | tf_op jit(solution)/shard_map/merge/pallas_call | solution.py:285
Async XLA Ops:
  0.0 32.7 %copy-start.5 = (s32[2]{0:T(128)S(1)}, s32[2]{0:T(128)}, u32[]{:S(2)}) copy-start(s32[2]{0:T(128)} %param.19) | copy-start | bytes 28
  0.0 32.7 %copy-start.3 = (bf16[2,2,128]{2,1,0:T(2,128)(2,1)S(1)}, bf16[2,2,128]{2,1,0:T(2,128)(2,1)}, u32[]{:S(2)}) copy-start(bf16[2,2,128]{2,1,0:T(2,128)(2,1)} %new_values_ref.1) | copy-start | bytes 3076
  0.0 32.7 %copy-start.2 = (bf16[2,2,128]{2,1,0:T(2,128)(2,1)S(1)}, bf16[2,2,128]{2,1,0:T(2,128)(2,1)}, u32[]{:S(2)}) copy-start(bf16[2,2,128]{2,1,0:T(2,128)(2,1)} %new_keys_ref.1) | copy-start | bytes 3076
  0.0 32.7 %copy-start.1 = (bf16[2,1024,128]{2,1,0:T(8,128)(2,1)S(1)}, bf16[2,1024,128]{2,1,0:T(8,128)(2,1)}, u32[]{:S(2)}) copy-start(bf16[2,1024,128]{2,1,0:T(8,128)(2,1)} %values_ref.1) | copy-start | bytes 1572868
  0.0 32.7 %copy-start = (bf16[2,1024,128]{2,1,0:T(8,128)(2,1)S(1)}, bf16[2,1024,128]{2,1,0:T(8,128)(2,1)}, u32[]{:S(2)}) copy-start(bf16[2,1024,128]{2,1,0:T(8,128)(2,1)} %keys_ref.1) | copy-start | bytes 1572868
  0.0 32.7 %copy-start.4 = (f32[128]{0:T(128)S(1)}, f32[128]{0:T(128)}, u32[]{:S(2)}) copy-start(f32[128]{0:T(128)} %param.14) | copy-start | bytes 1540
  1.7 18.1 %all-to-all-start = ((bf16[8,16,384]{2,1,0:T(8,128)(2,1)}), bf16[8,16,384]{2,1,0:T(8,128)(2,1)S(1)}, u32[]{:S(2)}, u32[]{:S(2)}) async-start(bf16[8,16,384]{2,1,0:T(8,128)(2,1)} %get-tuple-element.10), calls=%async_computation | async-start | bytes 196608 | tf_op jit(solution)/shard_map/all_to_all | solution.py:201
  14.0 5.7 %collective-permute-start = (bf16[4,3072]{1,0:T(4,128)(2,1)S(1)}, bf16[4,3072]{1,0:T(4,128)(2,1)S(1)}, u32[]{:S(2)}, u32[]{:S(2)}) collective-permute-start(bf16[4,3072]{1,0:T(4,128)(2,1)S(1)} %get-tuple-element.9), channel_id=1, source_target_pairs={{0,32},{32,0},{1,33},{33,1},{2,34},{34,2},{3,35},{35,3},{4,36},{36... | collective-permute-start | bytes 73736 | tf_op jit(solution)/shard_map/ppermute | solution.py:250

commit v9 on v8

--- a/solution.py
+++ b/solution.py
@@ -74,7 +74,7 @@
         copy.wait()
 
 
-def project(hidden_hbm, frozen_hbm, terms_ref, hidden_ref, frozen_ref, sems):
+def project(hidden_hbm, frozen_hbm, terms_ref, pick_ref, put_ref, hidden_ref, frozen_ref, sems):
     copies = [
         pltpu.make_async_copy(source, target, sems.at[i])
         for i, (source, target) in enumerate(
@@ -86,6 +86,16 @@
     ]
     for copy in copies:
         copy.start()
+    line, place = iota((32, 128), 0), iota((32, 128), 1)
+    pick = jnp.zeros((32, 128), jnp.bool_)
+    for peer, z in enumerate(z_order):
+        pick |= (place // 16 == peer) & (line // 4 == z) & (place % 4 == line % 4)
+    pick = pick.astype(f32).astype(bf16)
+    pick_ref[...] = pick
+    rank = iota((16, 256), 0) + 16 * lax.axis_index("fsdp")
+    rank = 32 * (rank // 4 % 2) + 4 * (rank // 8) + rank % 4
+    for i in range(3):
+        put_ref[16 * i : 16 * i + 16, :] = (iota((16, 256), 1) == rank + 64 * i).astype(f32).astype(bf16)
     copies[0].wait()
     tokens = jnp.concatenate([hidden_ref[0].astype(f32), hidden_ref[1].astype(f32)], axis=0)
     copies[1].wait()
@@ -93,8 +103,8 @@
     terms_ref[...] = jnp.concatenate(terms + [jnp.zeros((4, 256), f32)], axis=0)
 
 
-def pack_queries(own_ref, other_ref, terms_ref, factors_ref, out_ref, columns, spread):
-    f, ylo = lax.axis_index("fsdp"), lax.axis_index("ylo")
+def pack_queries(own_ref, other_ref, terms_ref, pick_ref, put_ref, factors_ref, out_ref, columns, spread):
+    ylo = lax.axis_index("ylo")
     low_half = iota((16, 128), 1) < 64
     here = iota((16, 256), 1) // 64 == iota((16, 256), 0) // 4
     for z in range(8):
@@ -105,18 +115,10 @@
         spread[16 * z : 16 * z + 16, :] = rows.astype(bf16)
     tokens = jnp.concatenate([own_ref[...].astype(f32), other_ref[...].astype(f32)], axis=0).astype(bf16)
     low = dot(tokens, columns[...], NT)
-    line, place = iota((32, 128), 0), iota((32, 128), 1)
-    pick = jnp.zeros((32, 128), jnp.bool_)
-    for peer, z in enumerate(z_order):
-        pick |= (place // 16 == peer) & (line // 4 == z) & (place % 4 == line % 4)
-    pick = pick.astype(f32).astype(bf16)
-    up = dot(pick, spread[...], NN).astype(bf16)
-    rank = iota((16, 256), 0) + 16 * f
-    rank = 32 * (rank // 4 % 2) + 4 * (rank // 8) + rank % 4
+    up = dot(pick_ref[...], spread[...], NN).astype(bf16)
     lanes = jnp.zeros((8, 256), f32)
     for i, term in enumerate(split3(low)):
-        put = (iota((16, 256), 1) == rank + 64 * i).astype(f32).astype(bf16)
-        lanes += dot(term, put, NN)
+        lanes += dot(term, put_ref[16 * i : 16 * i + 16, :], NN)
     tails = []
     for y in range(2):
         part = jnp.where(ylo == y, lanes[0:4], lanes[4:8])
@@ -248,11 +250,15 @@
     )(far(factor_down.T), far(factor_up), far(hidden_in))
     factors = exchange(packed, "z", z_order)
     other = lax.ppermute(lent, "ylo", ((0, 1), (1, 0)))
-    terms = pl.pallas_call(
+    terms, pick, put = pl.pallas_call(
         project,
-        out_shape=jax.ShapeDtypeStruct((16, 256), f32),
+        out_shape=(
+            jax.ShapeDtypeStruct((16, 256), f32),
+            jax.ShapeDtypeStruct((32, 128), bf16),
+            jax.ShapeDtypeStruct((48, 256), bf16),
+        ),
         in_specs=hbm(2),
-        out_specs=whole(1)[0],
+        out_specs=tuple(whole(3)),
         scratch_shapes=[
             pltpu.VMEM((2, 2, 5120), bf16),
             pltpu.VMEM((5120, 256), bf16),
@@ -265,12 +271,12 @@
     sent = pl.pallas_call(
         pack_queries,
         out_shape=jax.ShapeDtypeStruct((8, 48, 256), bf16),
-        in_specs=whole(4),
+        in_specs=whole(6),
         out_specs=whole(1)[0],
         scratch_shapes=[pltpu.VMEM((16, 8 * 384), bf16), pltpu.VMEM((128, 256), bf16)],
         compiler_params=room,
         name="pack_queries",
-    )(own, other, terms, factors)
+    )(own, other, terms, pick, put, factors)
     parts = exchange(sent, ("fsdp", "ylo"), y_order)
     partial = pl.pallas_call(
         attend,

time: 43.9 us -> 43.9 us (level)
  no operation moved by 1% of the time
where the time goes in v9:
time: 43.9 us; the launch traced here: 43.6 us
  blocking collectives  22.1 us (50%)
  starting transfers between devices  15.8 us (36%)
  Pallas kernels  5.61 us (13%)
    all_to_all x2, blocking collectives, exchange(): return lax.all_to_all(x, axis, 0, 0, axis_index_groups=[list(order)])  22.1 us
    all_to_all x1, starting transfers between devices, exchange(): return lax.all_to_all(x, axis, 0, 0, axis_index_groups=[list(order)])  12.3 us
    ppermute x1, starting transfers between devices, on_device(): other = lax.ppermute(lent, 'ylo', ((0, 1), (1, 0)))  3.47 us
    pallas_call x1, Pallas kernels, on_device(): pl.pallas_call(project, out_shape=(jax.ShapeDtypeStruct((16, 256), f32),...  2.25 us
    pallas_call x1, Pallas kernels, on_device(): pl.pallas_call(pack_factors, out_shape=(jax.ShapeDtypeStruct((8, 16, 384)...  1.64 us
  transfers between devices with their start and end apart: 2, of which 0 were waited for; matrix products, arithmetic and copies ran while one was open for 0% of the time, Pallas kernels for 5%

profile of v9, /device:TPU:6, one launch (start us, length us, event | category | flops | bytes accessed | tf_op | source)
XLA Modules:
  0.0 43.6 jit_solution(11398455758293442336)
XLA Ops:
  0.0 0.0 copy-start.5
  0.0 0.0 copy-start.3
  0.0 0.0 copy-start.2
  0.0 0.0 copy-start.1
  0.0 0.0 copy-start
  0.0 0.0 copy-start.4
  0.0 1.6 %pack_factors.1 = (bf16[8,16,384]{2,1,0:T(8,128)(2,1)}, bf16[4,3072]{1,0:T(4,128)(2,1)S(1)}, bf16[4,3072]{1,0:T(4,128)(2,1)S(1)}) custom-call(bf16[64,320]{1,0:T(8,128)(2,1)} %bitcast.5, bf16[4,256]{1,0:T(4,128)(2,1)} %up_hbm.1, bf16[2,2,5120]{2,1,0:T(2,128)(2,1)} %hidden_hbm.3), custom_call_target="tpu_custom_call" | custom-call | tf_op jit(solution)/shard_map/pack_factors/pallas_call | solution.py:230
  1.7 12.3 %all-to-all-start = ((bf16[8,16,384]{2,1,0:T(8,128)(2,1)}), bf16[8,16,384]{2,1,0:T(8,128)(2,1)S(1)}, u32[]{:S(2)}, u32[]{:S(2)}) async-start(bf16[8,16,384]{2,1,0:T(8,128)(2,1)} %get-tuple-element.16), calls=%async_computation | async-start | bytes 196608 | tf_op jit(solution)/shard_map/all_to_all | solution.py:203
  14.0 3.5 %collective-permute-start = (bf16[4,3072]{1,0:T(4,128)(2,1)S(1)}, bf16[4,3072]{1,0:T(4,128)(2,1)S(1)}, u32[]{:S(2)}, u32[]{:S(2)}) collective-permute-start(bf16[4,3072]{1,0:T(4,128)(2,1)S(1)} %get-tuple-element.12), channel_id=1, source_target_pairs={{0,32},{32,0},{1,33},{33,1},{2,34},{34,2},{3,35},{35,3},{4,36},{36... | collective-permute-start | bytes 73736 | tf_op jit(solution)/shard_map/ppermute | solution.py:252
  17.5 2.2 %project.1 = (f32[16,256]{1,0:T(8,128)S(1)}, bf16[32,128]{1,0:T(8,128)(2,1)S(1)}, bf16[48,256]{1,0:T(8,128)(2,1)S(1)}) custom-call(bf16[2,2,5120]{2,1,0:T(2,128)(2,1)} %hidden_hbm.3, bf16[5120,256]{1,0:T(8,128)(2,1)} %frozen_hbm.1), custom_call_target="tpu_custom_call" | custom-call | flops 10485760 | bytes 8388608 | tf_op jit(solution)/shard_map/project/pallas_call | solution.py:253
  19.7 0.0 collective-permute-done.other_ref
  19.7 0.0 all-to-all-done.factors_ref
  19.8 0.3 pack_queries.1
  20.1 12.7 %all_to_all.15.parts_ref = bf16[8,48,256]{2,1,0:T(8,128)(2,1)S(1)} all-to-all(bf16[8,48,256]{2,1,0:T(8,128)(2,1)S(1)} %pack_queries.1), channel_id=1, replica_groups={{34,32,0,1,33,2,3,35},{38,36,4,5,37,6,7,39},{42,40,8,9,41,10,11,43},{46..., dimensions={0} | all-to-all | bytes 393216 | tf_op jit(solution)/shard_map/all_to_all | solution.py:203
  32.7 0.0 copy-done.5
  32.7 0.0 copy-done.3
  32.7 0.0 copy-done.2
  32.7 0.0 copy-done.1
  32.7 0.0 copy-done
  32.8 0.0 copy-done.4
  32.8 0.8 %attend.1 = f32[4,24,128]{2,1,0:T(8,128)S(1)} custom-call(bf16[8,48,256]{2,1,0:T(8,128)(2,1)S(1)} %all_to_all.15.parts_ref, f32[1,128]{1,0:T(1,128)S(1)} %bitcast.3, bf16[2,1024,128]{2,1,0:T(8,128)(2,1)S(1)} %copy-done, bf16[2,1024,128]{2,1,0:T(8,128)(2,1)S(1)} %copy-done.1, bf16[2,2,128]{2,1,0:T(2,128)(2,1)S(1)} %copy-done.2, ...), custom_call_target="tpu_custom_call" | custom-call | tf_op jit(solution)/shard_map/attend/pallas_call | solution.py:281
  33.6 9.4 %all_to_all.16.parts_ref = f32[4,24,128]{2,1,0:T(8,128)S(1)} all-to-all(f32[4,24,128]{2,1,0:T(8,128)S(1)} %attend.1), channel_id=1, replica_groups={{2,3,0,1},{6,7,4,5},{10,11,8,9},{14,15,12,13},{18,19,16,17},{22,23,20,2..., dimensions={0} | all-to-all | bytes 98304 | tf_op jit(solution)/shard_map/all_to_all | solution.py:203
  43.0 0.6 %merge.1 = bf16[2,2,256]{2,1,0:T(2,128)(2,1)} custom-call(f32[4,24,128]{2,1,0:T(8,128)S(1)} %all_to_all.16.parts_ref), custom_call_target="tpu_custom_call" | custom-call | tf_op jit(solution)/shard_map/merge/pallas_call | solution.py:291
Async XLA Ops:
  0.0 32.7 %copy-start.5 = (s32[2]{0:T(128)S(1)}, s32[2]{0:T(128)}, u32[]{:S(2)}) copy-start(s32[2]{0:T(128)} %param.19) | copy-start | bytes 28
  0.0 32.7 %copy-start.3 = (bf16[2,2,128]{2,1,0:T(2,128)(2,1)S(1)}, bf16[2,2,128]{2,1,0:T(2,128)(2,1)}, u32[]{:S(2)}) copy-start(bf16[2,2,128]{2,1,0:T(2,128)(2,1)} %new_values_ref.1) | copy-start | bytes 3076
  0.0 32.7 %copy-start.2 = (bf16[2,2,128]{2,1,0:T(2,128)(2,1)S(1)}, bf16[2,2,128]{2,1,0:T(2,128)(2,1)}, u32[]{:S(2)}) copy-start(bf16[2,2,128]{2,1,0:T(2,128)(2,1)} %new_keys_ref.1) | copy-start | bytes 3076
  0.0 32.7 %copy-start.1 = (bf16[2,1024,128]{2,1,0:T(8,128)(2,1)S(1)}, bf16[2,1024,128]{2,1,0:T(8,128)(2,1)}, u32[]{:S(2)}) copy-start(bf16[2,1024,128]{2,1,0:T(8,128)(2,1)} %values_ref.1) | copy-start | bytes 1572868
  0.0 32.7 %copy-start = (bf16[2,1024,128]{2,1,0:T(8,128)(2,1)S(1)}, bf16[2,1024,128]{2,1,0:T(8,128)(2,1)}, u32[]{:S(2)}) copy-start(bf16[2,1024,128]{2,1,0:T(8,128)(2,1)} %keys_ref.1) | copy-start | bytes 1572868
  0.0 32.7 %copy-start.4 = (f32[128]{0:T(128)S(1)}, f32[128]{0:T(128)}, u32[]{:S(2)}) copy-start(f32[128]{0:T(128)} %param.14) | copy-start | bytes 1540
  1.7 18.1 %all-to-all-start = ((bf16[8,16,384]{2,1,0:T(8,128)(2,1)}), bf16[8,16,384]{2,1,0:T(8,128)(2,1)S(1)}, u32[]{:S(2)}, u32[]{:S(2)}) async-start(bf16[8,16,384]{2,1,0:T(8,128)(2,1)} %get-tuple-element.16), calls=%async_computation | async-start | bytes 196608 | tf_op jit(solution)/shard_map/all_to_all | solution.py:203
  14.0 5.7 %collective-permute-start = (bf16[4,3072]{1,0:T(4,128)(2,1)S(1)}, bf16[4,3072]{1,0:T(4,128)(2,1)S(1)}, u32[]{:S(2)}, u32[]{:S(2)}) collective-permute-start(bf16[4,3072]{1,0:T(4,128)(2,1)S(1)} %get-tuple-element.12), channel_id=1, source_target_pairs={{0,32},{32,0},{1,33},{33,1},{2,34},{34,2},{3,35},{35,3},{4,36},{36... | collective-permute-start | bytes 73736 | tf_op jit(solution)/shard_map/ppermute | solution.py:252

commit v10 on v9

--- a/solution.py
+++ b/solution.py
@@ -74,13 +74,15 @@
         copy.wait()
 
 
-def project(hidden_hbm, frozen_hbm, terms_ref, pick_ref, put_ref, hidden_ref, frozen_ref, sems):
+def project(hidden_hbm, frozen_hbm, keys_hbm, values_hbm, terms_ref, pick_ref, put_ref, keys_ref, values_ref, hidden_ref, frozen_ref, sems):
     copies = [
         pltpu.make_async_copy(source, target, sems.at[i])
         for i, (source, target) in enumerate(
             (
                 (hidden_hbm, hidden_ref),
                 (frozen_hbm, frozen_ref),
+                (keys_hbm, keys_ref),
+                (values_hbm, values_ref),
             )
         )
     ]
@@ -101,6 +103,8 @@
     copies[1].wait()
     terms = [t.astype(f32) for t in split3(dot(tokens.astype(bf16), frozen_ref[...], NN))]
     terms_ref[...] = jnp.concatenate(terms + [jnp.zeros((4, 256), f32)], axis=0)
+    copies[2].wait()
+    copies[3].wait()
 
 
 def pack_queries(own_ref, other_ref, terms_ref, pick_ref, put_ref, factors_ref, out_ref, columns, spread):
@@ -250,24 +254,26 @@
     )(far(factor_down.T), far(factor_up), far(hidden_in))
     factors = exchange(packed, "z", z_order)
     other = lax.ppermute(lent, "ylo", ((0, 1), (1, 0)))
-    terms, pick, put = pl.pallas_call(
+    terms, pick, put, keys, values = pl.pallas_call(
         project,
         out_shape=(
             jax.ShapeDtypeStruct((16, 256), f32),
             jax.ShapeDtypeStruct((32, 128), bf16),
             jax.ShapeDtypeStruct((48, 256), bf16),
+            pltpu.VMEM(key_cache.shape, bf16),
+            pltpu.VMEM(value_cache.shape, bf16),
         ),
-        in_specs=hbm(2),
-        out_specs=tuple(whole(3)),
+        in_specs=hbm(4),
+        out_specs=tuple(whole(5)),
         scratch_shapes=[
             pltpu.VMEM((2, 2, 5120), bf16),
             pltpu.VMEM((5120, 256), bf16),
-            pltpu.SemaphoreType.DMA((2,)),
+            pltpu.SemaphoreType.DMA((4,)),
         ],
         compiler_params=room,
         cost_estimate=pl.CostEstimate(flops=2 * 4 * 5120 * 256, bytes_accessed=8 * 2**20, transcendentals=0),
         name="project",
-    )(far(hidden_in), far(frozen_query_matrix))
+    )(far(hidden_in), far(frozen_query_matrix), far(key_cache), far(value_cache))
     sent = pl.pallas_call(
         pack_queries,
         out_shape=jax.ShapeDtypeStruct((8, 48, 256), bf16),
@@ -286,7 +292,7 @@
         scratch_shapes=[pltpu.VMEM((32, 128), f32)] + [pltpu.VMEM((16, 128), f32)] * 2,
         compiler_params=room,
         name="attend",
-    )(parts, query_gain.reshape(1, 128), key_cache, value_cache, new_keys, new_values, cache_lengths.reshape(1, 2))
+    )(parts, query_gain.reshape(1, 128), keys, values, new_keys, new_values, cache_lengths.reshape(1, 2))
     partial = exchange(partial, "fsdp", fsdp_order)
     return pl.pallas_call(
         merge,

time: 43.9 us -> 43.9 us (level)
  no operation moved by 1% of the time
where the time goes in v10:
time: 43.9 us; the launch traced here: 43.5 us
  blocking collectives  22.1 us (50%)
  starting transfers between devices  15.8 us (36%)
  Pallas kernels  5.58 us (13%)
    all_to_all x2, blocking collectives, exchange(): return lax.all_to_all(x, axis, 0, 0, axis_index_groups=[list(order)])  22.1 us
    all_to_all x1, starting transfers between devices, exchange(): return lax.all_to_all(x, axis, 0, 0, axis_index_groups=[list(order)])  12.3 us
    ppermute x1, starting transfers between devices, on_device(): other = lax.ppermute(lent, 'ylo', ((0, 1), (1, 0)))  3.47 us
    pallas_call x1, Pallas kernels, on_device(): pl.pallas_call(project, out_shape=(jax.ShapeDtypeStruct((16, 256), f32),...  2.27 us
    pallas_call x1, Pallas kernels, on_device(): pl.pallas_call(pack_factors, out_shape=(jax.ShapeDtypeStruct((8, 16, 384)...  1.58 us
  transfers between devices with their start and end apart: 2, of which 0 were waited for; matrix products, arithmetic and copies ran while one was open for 0% of the time, Pallas kernels for 5%

profile of v10, /device:TPU:6, one launch (start us, length us, event | category | flops | bytes accessed | tf_op | source)
XLA Modules:
  0.0 43.5 jit_solution(918553402107244291)
XLA Ops:
  0.0 0.0 copy-start.3
  0.0 0.0 copy-start.1
  0.0 0.0 copy-start
  0.0 0.0 copy-start.2
  0.0 1.6 %pack_factors.1 = (bf16[8,16,384]{2,1,0:T(8,128)(2,1)}, bf16[4,3072]{1,0:T(4,128)(2,1)S(1)}, bf16[4,3072]{1,0:T(4,128)(2,1)S(1)}) custom-call(bf16[64,320]{1,0:T(8,128)(2,1)} %bitcast.5, bf16[4,256]{1,0:T(4,128)(2,1)} %up_hbm.1, bf16[2,2,5120]{2,1,0:T(2,128)(2,1)} %hidden_hbm.3), custom_call_target="tpu_custom_call" | custom-call | tf_op jit(solution)/shard_map/pack_factors/pallas_call | solution.py:234
  1.6 12.3 %all-to-all-start = ((bf16[8,16,384]{2,1,0:T(8,128)(2,1)}), bf16[8,16,384]{2,1,0:T(8,128)(2,1)S(1)}, u32[]{:S(2)}, u32[]{:S(2)}) async-start(bf16[8,16,384]{2,1,0:T(8,128)(2,1)} %get-tuple-element.18), calls=%async_computation | async-start | bytes 196608 | tf_op jit(solution)/shard_map/all_to_all | solution.py:207
  13.9 3.5 %collective-permute-start = (bf16[4,3072]{1,0:T(4,128)(2,1)S(1)}, bf16[4,3072]{1,0:T(4,128)(2,1)S(1)}, u32[]{:S(2)}, u32[]{:S(2)}) collective-permute-start(bf16[4,3072]{1,0:T(4,128)(2,1)S(1)} %get-tuple-element.14), channel_id=1, source_target_pairs={{0,32},{32,0},{1,33},{33,1},{2,34},{34,2},{3,35},{35,3},{4,36},{36... | collective-permute-start | bytes 73736 | tf_op jit(solution)/shard_map/ppermute | solution.py:256
  17.4 2.3 %project.1 = (f32[16,256]{1,0:T(8,128)S(1)}, bf16[32,128]{1,0:T(8,128)(2,1)S(1)}, bf16[48,256]{1,0:T(8,128)(2,1)S(1)}, bf16[2,1024,128]{2,1,0:T(8,128)(2,1)S(1)}, bf16[2,1024,128]{2,1,0:T(8,128)(2,1)S(1)}) custom-call(bf16[2,2,5120]{2,1,0:T(2,128)(2,1)} %hidden_hbm.3, bf16[5120,256]{1,0:T(8,128)(2,1)} %frozen_hbm.1, bf16[2,1024,128]{2,1,0:T(8,128)(2,1)} %keys_hbm.1, ...), custom_call_target="tpu_custom_call" | custom-call | flops 10485760 | bytes 8388608 | tf_op jit(solution)/shard_map/project/pallas_call | solution.py:257
  19.7 0.0 collective-permute-done.other_ref
  19.7 0.0 all-to-all-done.factors_ref
  19.7 0.3 pack_queries.1
  20.0 12.7 %all_to_all.15.parts_ref = bf16[8,48,256]{2,1,0:T(8,128)(2,1)S(1)} all-to-all(bf16[8,48,256]{2,1,0:T(8,128)(2,1)S(1)} %pack_queries.1), channel_id=1, replica_groups={{34,32,0,1,33,2,3,35},{38,36,4,5,37,6,7,39},{42,40,8,9,41,10,11,43},{46..., dimensions={0} | all-to-all | bytes 393216 | tf_op jit(solution)/shard_map/all_to_all | solution.py:207
  32.7 0.0 copy-done.3
  32.7 0.0 copy-done.1
  32.7 0.0 copy-done
  32.7 0.0 copy-done.2
  32.7 0.8 %attend.1 = f32[4,24,128]{2,1,0:T(8,128)S(1)} custom-call(bf16[8,48,256]{2,1,0:T(8,128)(2,1)S(1)} %all_to_all.15.parts_ref, f32[1,128]{1,0:T(1,128)S(1)} %bitcast.3, bf16[2,1024,128]{2,1,0:T(8,128)(2,1)S(1)} %get-tuple-element.19.keys_ref, bf16[2,1024,128]{2,1,0:T(8,128)(2,1)S(1)} %get-tuple-element.20.values_ref, bf16[2,2,128]{2,1,0:T(2,128)(2,1)S(1)} %copy-done, ...), custom_call_target="tpu_custom_call" | custom-call | tf_op jit(solution)/shard_map/attend/pallas_call | solution.py:287
  33.5 9.4 %all_to_all.16.parts_ref = f32[4,24,128]{2,1,0:T(8,128)S(1)} all-to-all(f32[4,24,128]{2,1,0:T(8,128)S(1)} %attend.1), channel_id=1, replica_groups={{2,3,0,1},{6,7,4,5},{10,11,8,9},{14,15,12,13},{18,19,16,17},{22,23,20,2..., dimensions={0} | all-to-all | bytes 98304 | tf_op jit(solution)/shard_map/all_to_all | solution.py:207
  42.9 0.6 %merge.1 = bf16[2,2,256]{2,1,0:T(2,128)(2,1)} custom-call(f32[4,24,128]{2,1,0:T(8,128)S(1)} %all_to_all.16.parts_ref), custom_call_target="tpu_custom_call" | custom-call | tf_op jit(solution)/shard_map/merge/pallas_call | solution.py:297
Async XLA Ops:
  0.0 32.7 %copy-start.3 = (s32[2]{0:T(128)S(1)}, s32[2]{0:T(128)}, u32[]{:S(2)}) copy-start(s32[2]{0:T(128)} %param.19) | copy-start | bytes 28
  0.0 32.7 %copy-start.1 = (bf16[2,2,128]{2,1,0:T(2,128)(2,1)S(1)}, bf16[2,2,128]{2,1,0:T(2,128)(2,1)}, u32[]{:S(2)}) copy-start(bf16[2,2,128]{2,1,0:T(2,128)(2,1)} %new_values_ref.1) | copy-start | bytes 3076
  0.0 32.7 %copy-start = (bf16[2,2,128]{2,1,0:T(2,128)(2,1)S(1)}, bf16[2,2,128]{2,1,0:T(2,128)(2,1)}, u32[]{:S(2)}) copy-start(bf16[2,2,128]{2,1,0:T(2,128)(2,1)} %new_keys_ref.1) | copy-start | bytes 3076
  0.0 32.7 %copy-start.2 = (f32[128]{0:T(128)S(1)}, f32[128]{0:T(128)}, u32[]{:S(2)}) copy-start(f32[128]{0:T(128)} %param.14) | copy-start | bytes 1540
  1.6 18.1 %all-to-all-start = ((bf16[8,16,384]{2,1,0:T(8,128)(2,1)}), bf16[8,16,384]{2,1,0:T(8,128)(2,1)S(1)}, u32[]{:S(2)}, u32[]{:S(2)}) async-start(bf16[8,16,384]{2,1,0:T(8,128)(2,1)} %get-tuple-element.18), calls=%async_computation | async-start | bytes 196608 | tf_op jit(solution)/shard_map/all_to_all | solution.py:207
  13.9 5.8 %collective-permute-start = (bf16[4,3072]{1,0:T(4,128)(2,1)S(1)}, bf16[4,3072]{1,0:T(4,128)(2,1)S(1)}, u32[]{:S(2)}, u32[]{:S(2)}) collective-permute-start(bf16[4,3072]{1,0:T(4,128)(2,1)S(1)} %get-tuple-element.14), channel_id=1, source_target_pairs={{0,32},{32,0},{1,33},{33,1},{2,34},{34,2},{3,35},{35,3},{4,36},{36... | collective-permute-start | bytes 73736 | tf_op jit(solution)/shard_map/ppermute | solution.py:256

commit v11 on v10

--- a/solution.py
+++ b/solution.py
@@ -9,7 +9,7 @@
 norm_epsilon = 1e-06
 masked_score = -1e30
 
-z_order = (6, 7, 0, 1, 2, 3, 4, 5)
+z_order = (6, 7, 5, 0, 4, 1, 3, 2)
 y_order = (5, 1, 0, 2, 3, 4, 6, 7)
 fsdp_order = (2, 3, 0, 1)
 

time: 43.9 us -> 43.9 us (level)
  no operation moved by 1% of the time
where the time goes in v11:
time: 43.9 us; the launch traced here: 43.6 us
  blocking collectives  22.1 us (50%)
  starting transfers between devices  15.8 us (36%)
  Pallas kernels  5.58 us (13%)
    all_to_all x2, blocking collectives, exchange(): return lax.all_to_all(x, axis, 0, 0, axis_index_groups=[list(order)])  22.1 us
    all_to_all x1, starting transfers between devices, exchange(): return lax.all_to_all(x, axis, 0, 0, axis_index_groups=[list(order)])  12.3 us
    ppermute x1, starting transfers between devices, on_device(): other = lax.ppermute(lent, 'ylo', ((0, 1), (1, 0)))  3.47 us
    pallas_call x1, Pallas kernels, on_device(): pl.pallas_call(project, out_shape=(jax.ShapeDtypeStruct((16, 256), f32),...  2.27 us
    pallas_call x1, Pallas kernels, on_device(): pl.pallas_call(pack_factors, out_shape=(jax.ShapeDtypeStruct((8, 16, 384)...  1.58 us
  transfers between devices with their start and end apart: 2, of which 0 were waited for; matrix products, arithmetic and copies ran while one was open for 0% of the time, Pallas kernels for 5%

profile of v11, /device:TPU:6, one launch (start us, length us, event | category | flops | bytes accessed | tf_op | source)
XLA Modules:
  0.0 43.6 jit_solution(14765655317277492625)
XLA Ops:
  0.0 0.0 copy-start.3
  0.0 0.0 copy-start.1
  0.0 0.0 copy-start
  0.0 0.0 copy-start.2
  0.0 1.6 %pack_factors.1 = (bf16[8,16,384]{2,1,0:T(8,128)(2,1)}, bf16[4,3072]{1,0:T(4,128)(2,1)S(1)}, bf16[4,3072]{1,0:T(4,128)(2,1)S(1)}) custom-call(bf16[64,320]{1,0:T(8,128)(2,1)} %bitcast.5, bf16[4,256]{1,0:T(4,128)(2,1)} %up_hbm.1, bf16[2,2,5120]{2,1,0:T(2,128)(2,1)} %hidden_hbm.3), custom_call_target="tpu_custom_call" | custom-call | tf_op jit(solution)/shard_map/pack_factors/pallas_call | solution.py:234
  1.6 12.3 %all-to-all-start = ((bf16[8,16,384]{2,1,0:T(8,128)(2,1)}), bf16[8,16,384]{2,1,0:T(8,128)(2,1)S(1)}, u32[]{:S(2)}, u32[]{:S(2)}) async-start(bf16[8,16,384]{2,1,0:T(8,128)(2,1)} %get-tuple-element.18), calls=%async_computation | async-start | bytes 196608 | tf_op jit(solution)/shard_map/all_to_all | solution.py:207
  13.9 3.5 %collective-permute-start = (bf16[4,3072]{1,0:T(4,128)(2,1)S(1)}, bf16[4,3072]{1,0:T(4,128)(2,1)S(1)}, u32[]{:S(2)}, u32[]{:S(2)}) collective-permute-start(bf16[4,3072]{1,0:T(4,128)(2,1)S(1)} %get-tuple-element.14), channel_id=1, source_target_pairs={{0,32},{32,0},{1,33},{33,1},{2,34},{34,2},{3,35},{35,3},{4,36},{36... | collective-permute-start | bytes 73736 | tf_op jit(solution)/shard_map/ppermute | solution.py:256
  17.4 2.3 %project.1 = (f32[16,256]{1,0:T(8,128)S(1)}, bf16[32,128]{1,0:T(8,128)(2,1)S(1)}, bf16[48,256]{1,0:T(8,128)(2,1)S(1)}, bf16[2,1024,128]{2,1,0:T(8,128)(2,1)S(1)}, bf16[2,1024,128]{2,1,0:T(8,128)(2,1)S(1)}) custom-call(bf16[2,2,5120]{2,1,0:T(2,128)(2,1)} %hidden_hbm.3, bf16[5120,256]{1,0:T(8,128)(2,1)} %frozen_hbm.1, bf16[2,1024,128]{2,1,0:T(8,128)(2,1)} %keys_hbm.1, ...), custom_call_target="tpu_custom_call" | custom-call | flops 10485760 | bytes 8388608 | tf_op jit(solution)/shard_map/project/pallas_call | solution.py:257
  19.7 0.0 collective-permute-done.other_ref
  19.7 0.0 all-to-all-done.factors_ref
  19.7 0.3 pack_queries.1
  20.0 12.7 %all_to_all.15.parts_ref = bf16[8,48,256]{2,1,0:T(8,128)(2,1)S(1)} all-to-all(bf16[8,48,256]{2,1,0:T(8,128)(2,1)S(1)} %pack_queries.1), channel_id=1, replica_groups={{34,32,0,1,33,2,3,35},{38,36,4,5,37,6,7,39},{42,40,8,9,41,10,11,43},{46..., dimensions={0} | all-to-all | bytes 393216 | tf_op jit(solution)/shard_map/all_to_all | solution.py:207
  32.7 0.0 copy-done.3
  32.7 0.0 copy-done.1
  32.7 0.0 copy-done
  32.7 0.0 copy-done.2
  32.7 0.8 %attend.1 = f32[4,24,128]{2,1,0:T(8,128)S(1)} custom-call(bf16[8,48,256]{2,1,0:T(8,128)(2,1)S(1)} %all_to_all.15.parts_ref, f32[1,128]{1,0:T(1,128)S(1)} %bitcast.3, bf16[2,1024,128]{2,1,0:T(8,128)(2,1)S(1)} %get-tuple-element.19.keys_ref, bf16[2,1024,128]{2,1,0:T(8,128)(2,1)S(1)} %get-tuple-element.20.values_ref, bf16[2,2,128]{2,1,0:T(2,128)(2,1)S(1)} %copy-done, ...), custom_call_target="tpu_custom_call" | custom-call | tf_op jit(solution)/shard_map/attend/pallas_call | solution.py:287
  33.5 9.4 %all_to_all.16.parts_ref = f32[4,24,128]{2,1,0:T(8,128)S(1)} all-to-all(f32[4,24,128]{2,1,0:T(8,128)S(1)} %attend.1), channel_id=1, replica_groups={{2,3,0,1},{6,7,4,5},{10,11,8,9},{14,15,12,13},{18,19,16,17},{22,23,20,2..., dimensions={0} | all-to-all | bytes 98304 | tf_op jit(solution)/shard_map/all_to_all | solution.py:207
  42.9 0.6 %merge.1 = bf16[2,2,256]{2,1,0:T(2,128)(2,1)} custom-call(f32[4,24,128]{2,1,0:T(8,128)S(1)} %all_to_all.16.parts_ref), custom_call_target="tpu_custom_call" | custom-call | tf_op jit(solution)/shard_map/merge/pallas_call | solution.py:297
Async XLA Ops:
  0.0 32.7 %copy-start.3 = (s32[2]{0:T(128)S(1)}, s32[2]{0:T(128)}, u32[]{:S(2)}) copy-start(s32[2]{0:T(128)} %param.19) | copy-start | bytes 28
  0.0 32.7 %copy-start.1 = (bf16[2,2,128]{2,1,0:T(2,128)(2,1)S(1)}, bf16[2,2,128]{2,1,0:T(2,128)(2,1)}, u32[]{:S(2)}) copy-start(bf16[2,2,128]{2,1,0:T(2,128)(2,1)} %new_values_ref.1) | copy-start | bytes 3076
  0.0 32.7 %copy-start = (bf16[2,2,128]{2,1,0:T(2,128)(2,1)S(1)}, bf16[2,2,128]{2,1,0:T(2,128)(2,1)}, u32[]{:S(2)}) copy-start(bf16[2,2,128]{2,1,0:T(2,128)(2,1)} %new_keys_ref.1) | copy-start | bytes 3076
  0.0 32.7 %copy-start.2 = (f32[128]{0:T(128)S(1)}, f32[128]{0:T(128)}, u32[]{:S(2)}) copy-start(f32[128]{0:T(128)} %param.14) | copy-start | bytes 1540
  1.6 18.1 %all-to-all-start = ((bf16[8,16,384]{2,1,0:T(8,128)(2,1)}), bf16[8,16,384]{2,1,0:T(8,128)(2,1)S(1)}, u32[]{:S(2)}, u32[]{:S(2)}) async-start(bf16[8,16,384]{2,1,0:T(8,128)(2,1)} %get-tuple-element.18), calls=%async_computation | async-start | bytes 196608 | tf_op jit(solution)/shard_map/all_to_all | solution.py:207
  13.9 5.8 %collective-permute-start = (bf16[4,3072]{1,0:T(4,128)(2,1)S(1)}, bf16[4,3072]{1,0:T(4,128)(2,1)S(1)}, u32[]{:S(2)}, u32[]{:S(2)}) collective-permute-start(bf16[4,3072]{1,0:T(4,128)(2,1)S(1)} %get-tuple-element.14), channel_id=1, source_target_pairs={{0,32},{32,0},{1,33},{33,1},{2,34},{34,2},{3,35},{35,3},{4,36},{36... | collective-permute-start | bytes 73736 | tf_op jit(solution)/shard_map/ppermute | solution.py:256
